TPU v7x, 256 devices: a whole 4x4x8 slice. The times are simulated.
256 devices in a mesh: tm: 32 (over y, z), head: 8 (over x, core).
Axes of the slice: x: 4, y: 4, z: 8, core: 2. Of those that a mesh axis runs over, the one named last changes fastest.
Arguments:
- query: bfloat16 [6144, 3072], P(('tm', 'head')), may hold values from -6 to 6
- keys: bfloat16 [6144, 3072], P(('tm', 'head')), may hold values from -6 to 6
- values: bfloat16 [6144, 3072], P(('tm', 'head')), may hold values from -6 to 6
- dout: bfloat16 [6144, 3072], P(('tm', 'head')), may hold values from -6 to 6
- slot_group: int32 [32], replicated, may hold values from 0 to 31, each once
- valid: int32 [32], replicated, may hold values from 48 to 192, as said below
Outputs:
- grad_query: bfloat16 [6144, 3072], P(('tm', 'head'))
- grad_keys: bfloat16 [6144, 3072], P(('tm', 'head'))
- grad_values: bfloat16 [6144, 3072], P(('tm', 'head'))
Inputs may be any that keep to these rules, and one draw needn't show every extreme that they name: `slot_group`: each group number appears once. valid tokens are the first of each group; some group is full.
All inputs are finite; a program needn't handle non-finite values.
Results may differ from a plain program's by a relative error of at most 0.015.
Values may be sent and summed in bfloat16 or wider, within the bound.
No kernel may reach another device: no remote copies, remote signals or barrier semaphores. Data moves between devices by JAX's collectives and lax.ppermute only.
A program may use at most 64 MiB of HBM per device.

v0:
```python
import functools
import math

import jax
import jax.numpy as jnp
from jax import lax
from jax.experimental import pallas as pl
from jax.experimental.pallas import tpu as pltpu
from jax.sharding import PartitionSpec as P

HD = 128
HEADS = 3
COLS = HEADS * HD
NY, NZ, NX, NC = 4, 8, 4, 2
PART = 48
SUB = 24
QROWS = 768
NEG = -1e30
LOW = -1e29
FAR = 1000
SCALE = 1.0 / math.sqrt(HD)
LOG2E = 1.4426950408889634
QCHUNK = 256
KROWS = 768
KCHUNK = 512

NT = (((1,), (1,)), ((), ()))
NN = (((1,), (0,)), ((), ()))
TN = (((0,), (0,)), ((), ()))


def pairs(move):
    out = []
    for y in range(NY):
        for z in range(NZ):
            for x in range(NX):
                for c in range(NC):
                    ty, tz, tx, tc = move(y, z, x, c)
                    ty, tz, tx = ty % NY, tz % NZ, tx % NX
                    out.append((((y * NZ + z) * NX + x) * NC + c, ((ty * NZ + tz) * NX + tx) * NC + tc))
    return out


def send(array, move):
    return lax.ppermute(array, ("tm", "head"), pairs(move))


def swap_core(array):
    return send(array, lambda y, z, x, c: (y, z, x, 1 - c))


def dot(a, b, dims):
    return lax.dot_general(a, b, dims, preferred_element_type=jnp.float32)


def position():
    tm = lax.axis_index("tm")
    head = lax.axis_index("head")
    return tm // NZ, tm % NZ, head // NC, head % NC


def pack_kernel(query, grad, keys, values, keep, give):
    _, z, _, c = position()
    for j in range(4):
        mine = pl.ds(pl.multiple_of(((z + c + 2 * j) & 7) * COLS, HD), COLS)
        theirs = pl.ds(pl.multiple_of(((z + 1 - c + 2 * j) & 7) * COLS, HD), COLS)
        for n, array in enumerate((query, grad, keys, values)):
            keep[j, n] = array[:, mine]
            give[j, n] = array[:, theirs]


def unpack_kernel(mine, theirs, *outs):
    _, z, _, c = position()
    for j in range(4):
        own = pl.ds(pl.multiple_of(((z + c + 2 * j) & 7) * COLS, HD), COLS)
        other = pl.ds(pl.multiple_of(((z + 1 - c + 2 * j) & 7) * COLS, HD), COLS)
        for n in range(3):
            outs[n][:, own] = mine[j, n]
            outs[n][:, other] = theirs[j, n]


def flip(s, core):
    return (0, 1 + 2 * core, 3 - 2 * core, 2)[s]


def query_slot(at, s, j):
    return (at[0] ^ flip(s, at[3])) * NZ + ((at[1] - at[3] - 2 * j) & 7)


def key_slot(at, o, j):
    core = 1 - at[3] if o else at[3]
    return at[0] * NZ + ((at[1] - core - 2 * j) & 7)


def key_part(at, o, s):
    return at[2] ^ flip(s, 1 - at[3] if o else at[3])


def first_y(array):
    return send(array, lambda y, z, x, c: (y ^ (1 + 2 * c), z, x, c))


def second_y(array):
    return send(array, lambda y, z, x, c: (y ^ (3 - 2 * c), z, x, c))


def first_x(array):
    return send(array, lambda y, z, x, c: (y, z, x ^ (1 + 2 * c), c))


def second_x(array):
    return send(array, lambda y, z, x, c: (y, z, x ^ (3 - 2 * c), c))


def pieces(own, first, rest):
    return (own, first, rest.at[0], rest.at[1])


def clip_rows(count):
    return jnp.minimum(jnp.maximum(count, 0), PART)


def round_rows(count):
    return ((count + 15) // 16) * 16


def place_queries(at, groups, valid):
    group = [groups[query_slot(at, s, j)] for s in range(4) for j in range(4)]
    live = [clip_rows(valid[g] - PART * at[2]) for g in group]
    padded = [round_rows(n) for n in live]
    first = [sum(jnp.where(other < mine, n, 0) for other, n in zip(group, padded)) for mine in group]
    tops = []
    for n in range(QROWS // QCHUNK):
        inside = [
            jnp.where((f < QCHUNK * (n + 1)) & (count > 0), g, -1) for g, f, count in zip(group, first, live)
        ]
        tops.append(jnp.where(sum(padded) > QCHUNK * n, functools.reduce(jnp.maximum, inside), -1))
    return group, live, first, tops


def place_keys(at, groups, valid, o, tops):
    group = [groups[key_slot(at, o, j)] for j in range(4)]
    rows = [round_rows(valid[g]) for g in group]
    first, live = [], []
    for mine in group:
        here = sum(jnp.where(other < mine, n, 0) for other, n in zip(group, rows))
        firsts, lives = [], []
        for s in range(4):
            count = clip_rows(valid[mine] - PART * key_part(at, o, s))
            firsts.append(here)
            lives.append(count)
            here = here + round_rows(count)
        first.append(firsts)
        live.append(lives)
    half = KCHUNK // 2
    blocks = []
    for top in tops:
        seen = sum(jnp.where(g <= top, n, 0) for g, n in zip(group, rows))
        blocks.append((seen + half - 1) // half)
    return group, live, first, blocks


def pick(values, n):
    out = values[-1]
    for i in range(len(values) - 1):
        out = jnp.where(n == i, values[i], out)
    return out


def visit(blocks, step, state):
    half = KCHUNK // 2
    whole = blocks // 2
    state = lax.fori_loop(0, whole, lambda i, v: step(pl.ds(pl.multiple_of(i * KCHUNK, KCHUNK), KCHUNK), v), state)
    return lax.fori_loop(
        0, blocks - 2 * whole, lambda i, v: step(pl.ds(pl.multiple_of(whole * KCHUNK, KCHUNK), half), v), state
    )


def aligned(first):
    return pl.ds(pl.multiple_of(first, 16), PART)


def load_queries(qd, qbuf, qgrp, q_group, q_live, q_first):
    qbuf[...] = jnp.zeros_like(qbuf)
    row = lax.broadcasted_iota(jnp.int32, (PART, COLS), 0)
    lane = lax.broadcasted_iota(jnp.int32, (8, QROWS), 1)
    lane_group = jnp.full((8, QROWS), -1, jnp.int32)
    for s in range(4):
        for j in range(4):
            n = s * 4 + j
            rows = aligned(q_first[n])
            live = row < q_live[n]
            for a in range(2):
                qbuf[a, rows, :] = jnp.where(live, qd[s][j, a], qbuf[a, rows, :])
            here = (lane >= q_first[n]) & (lane < q_first[n] + q_live[n])
            lane_group = jnp.where(here, q_group[n], lane_group)
    qgrp[...] = lane_group


def load_keys(kv, kbuf, kgrp, k_group, k_live, k_first):
    kbuf[...] = jnp.zeros_like(kbuf)
    kgrp[...] = jnp.full_like(kgrp, FAR)
    row = lax.broadcasted_iota(jnp.int32, (PART, COLS), 0)
    row_lanes = lax.broadcasted_iota(jnp.int32, (PART, HD), 0)
    for j in range(4):
        for s in range(4):
            rows = aligned(k_first[j][s])
            live = row < k_live[j][s]
            for a in range(2):
                kbuf[a, rows, :] = jnp.where(live, kv[s][j, a], kbuf[a, rows, :])
            kgrp[rows, :] = jnp.where(row_lanes < k_live[j][s], k_group[j], kgrp[rows, :])


def stats_kernel(o, groups, valid, *refs):
    at = position()
    q_group, q_live, q_first, tops = place_queries(at, groups, valid)
    k_group, k_live, k_first, blocks = place_keys(at, groups, valid, o, tops)
    if o == 0:
        qbuf, qgrp, kbuf, kgrp, stats = refs[6:11]
        load_queries(pieces(*refs[0:3]), qbuf, qgrp, q_group, q_live, q_first)
    else:
        qbuf, qgrp, before = refs[0:3]
        kbuf, kgrp, stats = refs[6:9]
    load_keys(pieces(*refs[3:6]), kbuf, kgrp, k_group, k_live, k_first)
    stats[...] = jnp.zeros_like(stats)
    def chunk(n, _):
        rows = pl.ds(pl.multiple_of(n * QCHUNK, QCHUNK), QCHUNK)

        def step(keys, carry):
            group = kgrp[keys, :]
            ok = jnp.concatenate([group] * (QCHUNK // HD), axis=1) <= qgrp[0:1, rows]
            out = []
            for h in range(HEADS):
                cols = slice(h * HD, (h + 1) * HD)
                top, total, weighted = carry[h]
                scores = dot(kbuf[0, keys, cols], qbuf[0, rows, cols], NT)
                dprobs = dot(kbuf[1, keys, cols], qbuf[1, rows, cols], NT)
                scores = jnp.where(ok, scores * (SCALE * LOG2E), NEG)
                new_top = jnp.maximum(top, jnp.max(scores, axis=0, keepdims=True))
                weights = jnp.exp2(scores - new_top)
                factor = jnp.exp2(top - new_top)
                total = total * factor + jnp.sum(weights, axis=0, keepdims=True)
                weighted = weighted * factor + jnp.sum(weights * dprobs, axis=0, keepdims=True)
                out.append((new_top, total, weighted))
            return tuple(out)

        if o == 0:
            start = (
                jnp.full((1, QCHUNK), LOW, jnp.float32),
                jnp.zeros((1, QCHUNK), jnp.float32),
                jnp.zeros((1, QCHUNK), jnp.float32),
            )
            start = (start,) * HEADS
        else:
            start = tuple(
                tuple(before[3 * k + h : 3 * k + h + 1, rows] for k in range(3)) for h in range(HEADS)
            )
        final = visit(pick(blocks, n), step, start)
        for h in range(HEADS):
            for k in range(3):
                stats[3 * k + h : 3 * k + h + 1, rows] = final[h][k]
        return 0

    lax.fori_loop(0, QROWS // QCHUNK, chunk, 0)


def combine(st0, st1, st23, levels):
    sts = [st0[...], st1[...], st23[0], st23[1]]
    top = functools.reduce(jnp.maximum, [st[0:3, :] for st in sts])
    factors = [jnp.exp2(st[0:3, :] - top) for st in sts]
    total = sum(f * st[3:6, :] for f, st in zip(factors, sts))
    weighted = sum(f * st[6:9, :] for f, st in zip(factors, sts))
    some = total > 0.0
    safe = jnp.where(some, total, 1.0)
    levels[0:3, :] = jnp.where(some, top + jnp.log2(safe), 0.0)
    levels[3:6, :] = weighted / safe
    levels[6:8, :] = jnp.zeros_like(levels[6:8, :])


def grad_kernel(o, groups, valid, qbuf, qgrp, kbuf, kgrp, *refs):
    at = position()
    q_group, q_live, q_first, tops = place_queries(at, groups, valid)
    k_group, k_live, k_first, blocks = place_keys(at, groups, valid, o, tops)
    if o == 1:
        dkv, dqt, levels, dks, dvs = refs[3:8]
        combine(*refs[0:3], levels)
        dqt[...] = jnp.zeros_like(dqt)
    else:
        before, levels, dkv, dq, dqt, dks, dvs, dqs = refs
        dqt[...] = before[...]
    dks[...] = jnp.zeros_like(dks)
    dvs[...] = jnp.zeros_like(dvs)

    def chunk(n, _):
        rows = pl.ds(pl.multiple_of(n * QCHUNK, QCHUNK), QCHUNK)

        def step(keys, _):
            group = kgrp[keys, :]
            ok = jnp.concatenate([group] * (QCHUNK // HD), axis=1) <= qgrp[0:1, rows]
            for h in range(HEADS):
                cols = slice(h * HD, (h + 1) * HD)
                key = kbuf[0, keys, cols]
                query = qbuf[0, rows, cols]
                grad = qbuf[1, rows, cols]
                scores = dot(key, query, NT)
                dprobs = dot(kbuf[1, keys, cols], grad, NT)
                scores = jnp.where(ok, scores * (SCALE * LOG2E), NEG)
                probs = jnp.exp2(scores - levels[h : h + 1, rows])
                dscores = (probs * (dprobs - levels[3 + h : 4 + h, rows])).astype(jnp.bfloat16)
                dvs[keys, cols] += dot(probs.astype(jnp.bfloat16), grad, NN)
                dks[keys, cols] += dot(dscores, query, NN)
                dqt[h, :, rows] += dot(key, dscores, TN)
            return 0

        visit(pick(blocks, n), step, 0)
        return 0

    lax.fori_loop(0, QROWS // QCHUNK, chunk, 0)
    row = lax.broadcasted_iota(jnp.int32, (PART, COLS), 0)
    for j in range(4):
        for s in range(4):
            rows = aligned(k_first[j][s])
            live = row < k_live[j][s]
            dkv[s, j, 0] = jnp.where(live, dks[rows, :] * SCALE, 0.0).astype(jnp.bfloat16)
            dkv[s, j, 1] = jnp.where(live, dvs[rows, :], 0.0).astype(jnp.bfloat16)
    if o == 0:
        for h in range(HEADS):
            dqs[:, h * HD : (h + 1) * HD] = (dqt[h] * SCALE).T
        for s in range(4):
            for j in range(4):
                n = s * 4 + j
                rows = aligned(q_first[n])
                dq[s, j] = jnp.where(row < q_live[n], dqs[rows, :], 0.0).astype(jnp.bfloat16)


SMEM = pl.BlockSpec(memory_space=pltpu.SMEM)
VMEM = pl.BlockSpec(memory_space=pltpu.VMEM)
PARAMS = pltpu.CompilerParams(vmem_limit_bytes=48 * 1024 * 1024)


def run(kernel, name, out_shape, tables, arrays, scratch=()):
    return pl.pallas_call(
        kernel,
        out_shape=out_shape,
        in_specs=[SMEM] * len(tables) + [VMEM] * len(arrays),
        out_specs=(VMEM,) * len(out_shape),
        scratch_shapes=list(scratch),
        compiler_params=PARAMS,
        cost_estimate=pl.CostEstimate(flops=3 * 10**9, bytes_accessed=6 * 10**6, transcendentals=2 * 10**6),
        name=name,
    )(*tables, *arrays)


def local(query, keys, values, dout, slot_group, valid):
    c = lax.axis_index("head") % NC
    bf16, f32 = jnp.bfloat16, jnp.float32

    keep, give = pl.pallas_call(
        pack_kernel,
        out_shape=(jax.ShapeDtypeStruct((4, 4, SUB, COLS), bf16),) * 2,
        in_specs=[VMEM] * 4,
        out_specs=(VMEM,) * 2,
        name="pack",
    )(query, dout, keys, values)
    take = swap_core(give)
    both = jnp.where(c == 0, jnp.concatenate([keep, take], axis=2), jnp.concatenate([take, keep], axis=2))
    got = {j: send(both[j], lambda y, z, x, c: (y, z + c + 2 * j, x, c)) for j in (2, 1, 3, 0)}
    own_qd = jnp.stack([got[j][0:2] for j in range(4)])
    own_kv = jnp.stack([got[j][2:4] for j in range(4)])

    kv_first, qd_first = lax.optimization_barrier((first_x(own_kv), first_y(own_qd)))
    kv_rest = second_x(jnp.stack([own_kv, kv_first]))
    qd_rest = second_y(jnp.stack([own_qd, qd_first]))

    i32 = jnp.int32
    tables = (slot_group, valid)
    kbuf_type = jax.ShapeDtypeStruct((2, KROWS, COLS), bf16)
    kgrp_type = jax.ShapeDtypeStruct((KROWS, HD), i32)
    stats_type = jax.ShapeDtypeStruct((16, QROWS), f32)
    qbuf, qgrp, kbuf, kgrp, part = run(
        functools.partial(stats_kernel, 0),
        "stats_own",
        (jax.ShapeDtypeStruct((2, QROWS, COLS), bf16), jax.ShapeDtypeStruct((8, QROWS), i32))
        + (kbuf_type, kgrp_type, stats_type),
        tables,
        (own_qd, qd_first, qd_rest, own_kv, kv_first, kv_rest),
    )
    kbuf_other, kgrp_other, stats = run(
        functools.partial(stats_kernel, 1),
        "stats_other",
        (kbuf_type, kgrp_type, stats_type),
        tables,
        (qbuf, qgrp, part, swap_core(own_kv), swap_core(kv_first), swap_core(kv_rest)),
    )

    stats_first = first_y(stats)
    stats_rest = second_y(jnp.stack([stats, stats_first]))

    dkv_type = jax.ShapeDtypeStruct((4, 4, 2, PART, COLS), bf16)
    scratch = [
        pltpu.VMEM((HEADS, HD, QROWS), f32),
        pltpu.VMEM((KROWS, COLS), f32),
        pltpu.VMEM((KROWS, COLS), f32),
    ]
    dkv_other, dqt, levels = run(
        functools.partial(grad_kernel, 1),
        "grads_other",
        (
            dkv_type,
            jax.ShapeDtypeStruct((HEADS, HD, QROWS), f32),
            jax.ShapeDtypeStruct((8, QROWS), f32),
        ),
        tables,
        (qbuf, qgrp, kbuf_other, kgrp_other, stats, stats_first, stats_rest),
        scratch[1:],
    )
    swapped = swap_core(dkv_other)
    dkv_own, dq = run(
        functools.partial(grad_kernel, 0),
        "grads_own",
        (dkv_type, jax.ShapeDtypeStruct((4, 4, PART, COLS), bf16)),
        tables,
        (qbuf, qgrp, kbuf, kgrp, dqt, levels),
        scratch + [pltpu.VMEM((QROWS, COLS), f32)],
    )

    dkv_sum = dkv_own.astype(f32) + swapped.astype(f32)
    dkv_half, dq_half = lax.optimization_barrier((second_x(dkv_sum[2:4].astype(bf16)), second_y(dq[2:4])))
    dkv_sum = dkv_sum[0:2] + dkv_half.astype(f32)
    dq_sum = dq[0:2].astype(f32) + dq_half.astype(f32)
    dkv_last, dq_last = lax.optimization_barrier(
        (first_x(dkv_sum[1].astype(bf16)), first_y(dq_sum[1].astype(bf16)))
    )
    dkv_sum = (dkv_sum[0] + dkv_last.astype(f32)).astype(bf16)
    dq_sum = (dq_sum[0] + dq_last.astype(f32)).astype(bf16)

    back = {}
    for j in (2, 1, 3, 0):
        block = jnp.concatenate([dq_sum[j][None], dkv_sum[j]], axis=0)
        back[j] = send(block, lambda y, z, x, c: (y, z - c - 2 * j, x, c))
    back = [back[j] for j in range(4)]
    first = jnp.stack([b[:, :SUB] for b in back])
    second = jnp.stack([b[:, SUB:] for b in back])
    theirs = swap_core(jnp.where(c == 0, second, first))
    return pl.pallas_call(
        unpack_kernel,
        out_shape=(jax.ShapeDtypeStruct((SUB, NZ * COLS), bf16),) * 3,
        in_specs=[VMEM] * 2,
        out_specs=(VMEM,) * 3,
        name="unpack",
    )(jnp.where(c == 0, first, second), theirs)


def solution(mesh):
    spec = P(("tm", "head"), None)
    return jax.shard_map(
        local,
        mesh=mesh,
        in_specs=(spec, spec, spec, spec, P(), P()),
        out_specs=(spec, spec, spec),
        check_vma=False,
    )
```

profile of v0, /device:TPU:1, one launch (start us, length us, event | category | flops | bytes accessed | tf_op | source)
XLA Modules:
  0.0 118.2 jit_solution(6222201478518479234)
XLA Ops:
  0.6 2.0 %pack.1 = (bf16[4,4,24,384]{3,2,1,0:T(8,128)(2,1)}, bf16[4,4,24,384]{3,2,1,0:T(8,128)(2,1)}) custom-call(bf16[24,3072]{1,0:T(8,128)(2,1)} %query.1, bf16[24,3072]{1,0:T(8,128)(2,1)} %grad.1, bf16[24,3072]{1,0:T(8,128)(2,1)} %keys.1, bf16[24,3072]{1,0:T(8,128)(2,1)} %values.1), custom_call_target="tpu_custom_call" | custom-call | tf_op jit(solution)/shard_map/pack/pallas_call | solution.py:358
  2.6 3.2 %collective-permute-start = (bf16[4,4,24,384]{3,2,1,0:T(8,128)(2,1)}, bf16[4,4,24,384]{3,2,1,0:T(8,128)(2,1)S(1)}, u32[]{:S(2)}, u32[]{:S(2)}) collective-permute-start(bf16[4,4,24,384]{3,2,1,0:T(8,128)(2,1)} %get-tuple-element.25), channel_id=1, source_target_pairs={{0,1},{1,0},{2,3},{3,2},{4,5},{5,4},{6,7},{7,6},{8,9},{9,8},{10,11... | collective-permute-start | bytes 884744 | tf_op jit(solution)/shard_map/ppermute | solution.py:45
  10.5 3.9 %collective-permute-start.4 = (bf16[4,48,384]{2,1,0:T(8,128)(2,1)S(1)}, bf16[4,48,384]{2,1,0:T(8,128)(2,1)S(1)}, u32[]{:S(2)}, u32[]{:S(2)}) collective-permute-start(bf16[4,48,384]{2,1,0:T(8,128)(2,1)S(1)} %get-tuple-element.46), channel_id=1, source_target_pairs={{0,48},{1,57},{2,50},{3,59},{4,52},{5,61},{6,54},{7,63},{8,56},{9,... | collective-permute-start | bytes 442376 | tf_op jit(solution)/shard_map/ppermute | solution.py:45
  14.4 2.3 %collective-permute-start.3 = (bf16[4,48,384]{2,1,0:T(8,128)(2,1)S(1)}, bf16[4,48,384]{2,1,0:T(8,128)(2,1)S(1)}, u32[]{:S(2)}, u32[]{:S(2)}) collective-permute-start(bf16[4,48,384]{2,1,0:T(8,128)(2,1)S(1)} %get-tuple-element.47), channel_id=1, source_target_pairs={{0,32},{1,41},{2,34},{3,43},{4,36},{5,45},{6,38},{7,47},{8,40},{9,... | collective-permute-start | bytes 442376 | tf_op jit(solution)/shard_map/ppermute | solution.py:45
  17.7 5.1 %collective-permute-done.4 = bf16[4,48,384]{2,1,0:T(8,128)(2,1)S(1)} collective-permute-done((bf16[4,48,384]{2,1,0:T(8,128)(2,1)S(1)}, bf16[4,48,384]{2,1,0:T(8,128)(2,1)S(1)}, u32[]{:S(2)}, u32[]{:S(2)}) %collective-permute-start.4) | collective-permute-done | bytes 147488 | tf_op jit(solution)/shard_map/ppermute | solution.py:45
  22.9 4.7 %collective-permute-done.3 = bf16[4,48,384]{2,1,0:T(8,128)(2,1)S(1)} collective-permute-done((bf16[4,48,384]{2,1,0:T(8,128)(2,1)S(1)}, bf16[4,48,384]{2,1,0:T(8,128)(2,1)S(1)}, u32[]{:S(2)}, u32[]{:S(2)}) %collective-permute-start.3) | collective-permute-done | bytes 147488 | tf_op jit(solution)/shard_map/ppermute | solution.py:45
  27.6 2.3 %collective-permute-done.2 = bf16[4,48,384]{2,1,0:T(8,128)(2,1)S(1)} collective-permute-done((bf16[4,48,384]{2,1,0:T(8,128)(2,1)S(1)}, bf16[4,48,384]{2,1,0:T(8,128)(2,1)S(1)}, u32[]{:S(2)}, u32[]{:S(2)}) %collective-permute-start.2) | collective-permute-done | bytes 147488 | tf_op jit(solution)/shard_map/ppermute | solution.py:45
  30.0 2.6 %collective-permute-start.5 = (bf16[4,2,48,384]{3,2,1,0:T(8,128)(2,1)S(1)}, bf16[4,2,48,384]{3,2,1,0:T(8,128)(2,1)S(1)}, u32[]{:S(2)}, u32[]{:S(2)}) collective-permute-start(bf16[4,2,48,384]{3,2,1,0:T(8,128)(2,1)S(1)} %get-tuple-element.56.refs_3_), channel_id=1, source_target_pairs={{0,2},{1,7},{2,0},{3,5},{4,6},{5,3},{6,4},{7,1},{8,10},{9,15},{10,... | collective-permute-start | bytes 884744 | tf_op jit(solution)/shard_map/ppermute | solution.py:45
  32.7 2.8 %collective-permute-start.6 = (bf16[4,2,48,384]{3,2,1,0:T(8,128)(2,1)S(1)}, bf16[4,2,48,384]{3,2,1,0:T(8,128)(2,1)S(1)}, u32[]{:S(2)}, u32[]{:S(2)}) collective-permute-start(bf16[4,2,48,384]{3,2,1,0:T(8,128)(2,1)S(1)} %get-tuple-element.58.refs_0_), channel_id=1, source_target_pairs={{0,64},{1,193},{2,66},{3,195},{4,68},{5,197},{6,70},{7,199},{8,72}... | collective-permute-start | bytes 884744 | tf_op jit(solution)/shard_map/ppermute | solution.py:45
  36.9 2.7 %collective-permute-done.6.refs_1_ = bf16[4,2,48,384]{3,2,1,0:T(8,128)(2,1)S(1)} collective-permute-done((bf16[4,2,48,384]{3,2,1,0:T(8,128)(2,1)S(1)}, bf16[4,2,48,384]{3,2,1,0:T(8,128)(2,1)S(1)}, u32[]{:S(2)}, u32[]{:S(2)}) %collective-permute-start.6) | collective-permute-done | bytes 294944 | tf_op jit(solution)/shard_map/ppermute | solution.py:45
  40.0 8.8 %collective-permute-done.8.refs_5_ = bf16[2,4,2,48,384]{4,3,2,1,0:T(8,128)(2,1)S(1)} collective-permute-done((bf16[2,4,2,48,384]{4,3,2,1,0:T(8,128)(2,1)S(1)}, bf16[2,4,2,48,384]{4,3,2,1,0:T(8,128)(2,1)S(1)}, u32[]{:S(2)}, u32[]{:S(2)}) %collective-permute-start.8) | collective-permute-done | bytes 589856 | tf_op jit(solution)/shard_map/ppermute | solution.py:45
  49.3 4.2 %stats_own.1 = (bf16[2,768,384]{2,1,0:T(8,128)(2,1)S(1)}, s32[8,768]{1,0:T(8,128)S(1)}, bf16[2,768,384]{2,1,0:T(8,128)(2,1)S(1)}, s32[768,128]{1,0:T(8,128)S(1)}, f32[16,768]{1,0:T(8,128)S(1)}) custom-call(s32[32]{0:T(128)S(1)} %copy-done, s32[32]{0:T(128)S(1)} %copy-done.1, bf16[4,2,48,384]{3,2,1,0:T(8,128)(2,1)S(1)} %get-tuple-element.58.refs_0_, ...), custom_call_target="tpu_custom_call" | custom-call | flops 3000000000 | bytes 6000000 | tf_op jit(solution)/shard_map/stats_own/pallas_call | solution.py:342
  53.5 4.4 %stats_other.1 = (bf16[2,768,384]{2,1,0:T(8,128)(2,1)S(1)}, s32[768,128]{1,0:T(8,128)S(1)}, f32[16,768]{1,0:T(8,128)S(1)}) custom-call(s32[32]{0:T(128)S(1)} %copy-done, s32[32]{0:T(128)S(1)} %copy-done.1, bf16[2,768,384]{2,1,0:T(8,128)(2,1)S(1)} %get-tuple-element.28.refs_0_.qbuf, s32[8,768]{1,0:T(8,128)S(1)} %get-tuple-element.29.refs_1_.qgrp, ...), custom_call_target="tpu_custom_call" | custom-call | flops 3000000000 | bytes 6000000 | tf_op jit(solution)/shard_map/stats_other/pallas_call | solution.py:342
  59.4 2.8 %collective-permute-done.12.refs_1_ = f32[16,768]{1,0:T(8,128)S(1)} collective-permute-done((f32[16,768]{1,0:T(8,128)S(1)}, f32[16,768]{1,0:T(8,128)S(1)}, u32[]{:S(2)}, u32[]{:S(2)}) %collective-permute-start.12) | collective-permute-done | bytes 49184 | tf_op jit(solution)/shard_map/ppermute | solution.py:45
  62.3 3.5 %collective-permute-done.13.refs_2_ = f32[2,16,768]{2,1,0:T(8,128)S(1)} collective-permute-done((f32[2,16,768]{2,1,0:T(8,128)S(1)}, f32[2,16,768]{2,1,0:T(8,128)S(1)}, u32[]{:S(2)}, u32[]{:S(2)}) %collective-permute-start.13) | collective-permute-done | bytes 98336 | tf_op jit(solution)/shard_map/ppermute | solution.py:45
  65.7 5.9 %grads_other.1 = (bf16[4,4,2,48,384]{4,3,2,1,0:T(8,128)(2,1)S(1)}, f32[3,128,768]{2,1,0:T(8,128)S(1)}, f32[8,768]{1,0:T(8,128)S(1)}) custom-call(s32[32]{0:T(128)S(1)} %copy-done, s32[32]{0:T(128)S(1)} %copy-done.1, bf16[2,768,384]{2,1,0:T(8,128)(2,1)S(1)} %get-tuple-element.28.refs_0_.qbuf, s32[8,768]{1,0:T(8,128)S(1)} %get-tuple-element.29.refs_1_.qgrp, ...), custom_call_target="tpu_custom_call" | custom-call | flops 3000000000 | bytes 6000000 | tf_op jit(solution)/shard_map/grads_other/pallas_call | solution.py:342
  73.1 5.2 %grads_own.1 = (bf16[4,4,2,48,384]{4,3,2,1,0:T(8,128)(2,1)S(1)}, bf16[4,4,48,384]{3,2,1,0:T(8,128)(2,1)S(1)}) custom-call(s32[32]{0:T(128)S(1)} %copy-done, s32[32]{0:T(128)S(1)} %copy-done.1, bf16[2,768,384]{2,1,0:T(8,128)(2,1)S(1)} %get-tuple-element.28.refs_0_.qbuf, s32[8,768]{1,0:T(8,128)S(1)} %get-tuple-element.29.refs_1_.qgrp, ...), custom_call_target="tpu_custom_call" | custom-call | flops 3000000000 | bytes 6000000 | tf_op jit(solution)/shard_map/grads_own/pallas_call | solution.py:342
  79.7 5.9 %collective-permute-done.16 = bf16[2,4,48,384]{3,2,1,0:T(8,128)(2,1)S(1)} collective-permute-done((bf16[2,4,48,384]{3,2,1,0:T(8,128)(2,1)S(1)}, bf16[2,4,48,384]{3,2,1,0:T(8,128)(2,1)S(1)}, u32[]{:S(2)}, u32[]{:S(2)}) %collective-permute-start.16) | collective-permute-done | bytes 294944 | tf_op jit(solution)/shard_map/ppermute | solution.py:45
  85.5 2.4 %collective-permute-done.15 = bf16[2,4,2,48,384]{4,3,2,1,0:T(8,128)(2,1)S(1)} collective-permute-done((bf16[2,4,2,48,384]{4,3,2,1,0:T(8,128)(2,1)S(1)}, bf16[2,4,2,48,384]{4,3,2,1,0:T(8,128)(2,1)S(1)}, u32[]{:S(2)}, u32[]{:S(2)}) %collective-permute-start.15) | collective-permute-done | bytes 589856 | tf_op jit(solution)/shard_map/ppermute | solution.py:45
  88.7 4.8 %collective-permute-done.18 = bf16[4,48,384]{2,1,0:T(8,128)(2,1)S(1)} collective-permute-done((bf16[4,48,384]{2,1,0:T(8,128)(2,1)S(1)}, bf16[4,48,384]{2,1,0:T(8,128)(2,1)S(1)}, u32[]{:S(2)}, u32[]{:S(2)}) %collective-permute-start.18) | collective-permute-done | bytes 147488 | tf_op jit(solution)/shard_map/ppermute | solution.py:45
  95.2 6.3 %collective-permute-start.20 = (bf16[3,48,384]{2,1,0:T(8,128)(2,1)S(1)}, bf16[3,48,384]{2,1,0:T(8,128)(2,1)S(1)}, u32[]{:S(2)}, u32[]{:S(2)}) collective-permute-start(bf16[3,48,384]{2,1,0:T(8,128)(2,1)S(1)} %pad_maximum_fusion.7), channel_id=1, source_target_pairs={{0,48},{1,41},{2,50},{3,43},{4,52},{5,45},{6,54},{7,47},{8,56},{9,... | collective-permute-start | bytes 331784 | tf_op jit(solution)/shard_map/ppermute | solution.py:45
  101.6 2.7 %collective-permute-start.22 = (bf16[3,48,384]{2,1,0:T(8,128)(2,1)S(1)}, bf16[3,48,384]{2,1,0:T(8,128)(2,1)S(1)}, u32[]{:S(2)}, u32[]{:S(2)}) collective-permute-start(bf16[3,48,384]{2,1,0:T(8,128)(2,1)S(1)} %pad_maximum_fusion.9), channel_id=1, source_target_pairs={{0,16},{1,9},{2,18},{3,11},{4,20},{5,13},{6,22},{7,15},{8,24},{9,1... | collective-permute-start | bytes 331784 | tf_op jit(solution)/shard_map/ppermute | solution.py:45
  104.3 2.0 %collective-permute-start.19 = (bf16[3,48,384]{2,1,0:T(8,128)(2,1)S(1)}, bf16[3,48,384]{2,1,0:T(8,128)(2,1)S(1)}, u32[]{:S(2)}, u32[]{:S(2)}) collective-permute-start(bf16[3,48,384]{2,1,0:T(8,128)(2,1)S(1)} %pad_maximum_fusion.6), channel_id=1, source_target_pairs={{0,0},{1,57},{2,2},{3,59},{4,4},{5,61},{6,6},{7,63},{8,8},{9,1},{1... | collective-permute-start | bytes 331784 | tf_op jit(solution)/shard_map/ppermute | solution.py:45
  109.6 3.8 %collective-permute-done.22 = bf16[3,48,384]{2,1,0:T(8,128)(2,1)S(1)} collective-permute-done((bf16[3,48,384]{2,1,0:T(8,128)(2,1)S(1)}, bf16[3,48,384]{2,1,0:T(8,128)(2,1)S(1)}, u32[]{:S(2)}, u32[]{:S(2)}) %collective-permute-start.22) | collective-permute-done | bytes 110624 | tf_op jit(solution)/shard_map/ppermute | solution.py:45
  (67 shorter events, 22.9 us)
Async XLA Ops:
  2.6 4.7 %collective-permute-start = (bf16[4,4,24,384]{3,2,1,0:T(8,128)(2,1)}, bf16[4,4,24,384]{3,2,1,0:T(8,128)(2,1)S(1)}, u32[]{:S(2)}, u32[]{:S(2)}) collective-permute-start(bf16[4,4,24,384]{3,2,1,0:T(8,128)(2,1)} %get-tuple-element.25), channel_id=1, source_target_pairs={{0,1},{1,0},{2,3},{3,2},{4,5},{5,4},{6,7},{7,6},{8,9},{9,8},{10,11... | collective-permute-start | bytes 884744 | tf_op jit(solution)/shard_map/ppermute | solution.py:45
  8.6 9.1 %collective-permute-start.1 = (bf16[4,48,384]{2,1,0:T(8,128)(2,1)S(1)}, bf16[4,48,384]{2,1,0:T(8,128)(2,1)S(1)}, u32[]{:S(2)}, u32[]{:S(2)}) collective-permute-start(bf16[4,48,384]{2,1,0:T(8,128)(2,1)S(1)} %get-tuple-element.45), channel_id=1, source_target_pairs={{0,0},{1,9},{2,2},{3,11},{4,4},{5,13},{6,6},{7,15},{8,8},{9,17},{1... | collective-permute-start | bytes 442376 | tf_op jit(solution)/shard_map/ppermute | solution.py:45
  10.5 12.3 %collective-permute-start.4 = (bf16[4,48,384]{2,1,0:T(8,128)(2,1)S(1)}, bf16[4,48,384]{2,1,0:T(8,128)(2,1)S(1)}, u32[]{:S(2)}, u32[]{:S(2)}) collective-permute-start(bf16[4,48,384]{2,1,0:T(8,128)(2,1)S(1)} %get-tuple-element.46), channel_id=1, source_target_pairs={{0,48},{1,57},{2,50},{3,59},{4,52},{5,61},{6,54},{7,63},{8,56},{9,... | collective-permute-start | bytes 442376 | tf_op jit(solution)/shard_map/ppermute | solution.py:45
  14.4 13.1 %collective-permute-start.3 = (bf16[4,48,384]{2,1,0:T(8,128)(2,1)S(1)}, bf16[4,48,384]{2,1,0:T(8,128)(2,1)S(1)}, u32[]{:S(2)}, u32[]{:S(2)}) collective-permute-start(bf16[4,48,384]{2,1,0:T(8,128)(2,1)S(1)} %get-tuple-element.47), channel_id=1, source_target_pairs={{0,32},{1,41},{2,34},{3,43},{4,36},{5,45},{6,38},{7,47},{8,40},{9,... | collective-permute-start | bytes 442376 | tf_op jit(solution)/shard_map/ppermute | solution.py:45
  16.8 13.1 %collective-permute-start.2 = (bf16[4,48,384]{2,1,0:T(8,128)(2,1)S(1)}, bf16[4,48,384]{2,1,0:T(8,128)(2,1)S(1)}, u32[]{:S(2)}, u32[]{:S(2)}) collective-permute-start(bf16[4,48,384]{2,1,0:T(8,128)(2,1)S(1)} %get-tuple-element.48), channel_id=1, source_target_pairs={{0,16},{1,25},{2,18},{3,27},{4,20},{5,29},{6,22},{7,31},{8,24},{9,... | collective-permute-start | bytes 442376 | tf_op jit(solution)/shard_map/ppermute | solution.py:45
  30.0 6.9 %collective-permute-start.5 = (bf16[4,2,48,384]{3,2,1,0:T(8,128)(2,1)S(1)}, bf16[4,2,48,384]{3,2,1,0:T(8,128)(2,1)S(1)}, u32[]{:S(2)}, u32[]{:S(2)}) collective-permute-start(bf16[4,2,48,384]{3,2,1,0:T(8,128)(2,1)S(1)} %get-tuple-element.56.refs_3_), channel_id=1, source_target_pairs={{0,2},{1,7},{2,0},{3,5},{4,6},{5,3},{6,4},{7,1},{8,10},{9,15},{10,... | collective-permute-start | bytes 884744 | tf_op jit(solution)/shard_map/ppermute | solution.py:45
  32.7 6.9 %collective-permute-start.6 = (bf16[4,2,48,384]{3,2,1,0:T(8,128)(2,1)S(1)}, bf16[4,2,48,384]{3,2,1,0:T(8,128)(2,1)S(1)}, u32[]{:S(2)}, u32[]{:S(2)}) collective-permute-start(bf16[4,2,48,384]{3,2,1,0:T(8,128)(2,1)S(1)} %get-tuple-element.58.refs_0_), channel_id=1, source_target_pairs={{0,64},{1,193},{2,66},{3,195},{4,68},{5,197},{6,70},{7,199},{8,72}... | collective-permute-start | bytes 884744 | tf_op jit(solution)/shard_map/ppermute | solution.py:45
  39.7 9.1 %collective-permute-start.8 = (bf16[2,4,2,48,384]{4,3,2,1,0:T(8,128)(2,1)S(1)}, bf16[2,4,2,48,384]{4,3,2,1,0:T(8,128)(2,1)S(1)}, u32[]{:S(2)}, u32[]{:S(2)}) collective-permute-start(bf16[2,4,2,48,384]{4,3,2,1,0:T(8,128)(2,1)S(1)} %pad_maximum_fusion.1), channel_id=1, source_target_pairs={{0,6},{1,3},{2,4},{3,1},{4,2},{5,7},{6,0},{7,5},{8,14},{9,11},{10,... | collective-permute-start | bytes 1769480 | tf_op jit(solution)/shard_map/ppermute | solution.py:45
  39.8 9.5 %collective-permute-start.7 = (bf16[2,4,2,48,384]{4,3,2,1,0:T(8,128)(2,1)S(1)}, bf16[2,4,2,48,384]{4,3,2,1,0:T(8,128)(2,1)S(1)}, u32[]{:S(2)}, u32[]{:S(2)}) collective-permute-start(bf16[2,4,2,48,384]{4,3,2,1,0:T(8,128)(2,1)S(1)} %pad_maximum_fusion), channel_id=1, source_target_pairs={{0,192},{1,65},{2,194},{3,67},{4,196},{5,69},{6,198},{7,71},{8,200... | collective-permute-start | bytes 1769480 | tf_op jit(solution)/shard_map/ppermute | solution.py:45
  48.8 4.8 %collective-permute-start.11 = (bf16[2,4,2,48,384]{4,3,2,1,0:T(8,128)(2,1)S(1)}, bf16[2,4,2,48,384]{4,3,2,1,0:T(8,128)(2,1)S(1)}, u32[]{:S(2)}, u32[]{:S(2)}) collective-permute-start(bf16[2,4,2,48,384]{4,3,2,1,0:T(8,128)(2,1)S(1)} %collective-permute-done.8.refs_5_), channel_id=1, source_target_pairs={{0,1},{1,0},{2,3},{3,2},{4,5},{5,4},{6,7},{7,6},{8,9},{9,8},{10,11... | collective-permute-start | bytes 1769480 | tf_op jit(solution)/shard_map/ppermute | solution.py:45
  48.8 4.7 %collective-permute-start.9 = (bf16[4,2,48,384]{3,2,1,0:T(8,128)(2,1)S(1)}, bf16[4,2,48,384]{3,2,1,0:T(8,128)(2,1)S(1)}, u32[]{:S(2)}, u32[]{:S(2)}) collective-permute-start(bf16[4,2,48,384]{3,2,1,0:T(8,128)(2,1)S(1)} %get-tuple-element.56.refs_3_), channel_id=1, source_target_pairs={{0,1},{1,0},{2,3},{3,2},{4,5},{5,4},{6,7},{7,6},{8,9},{9,8},{10,11... | collective-permute-start | bytes 884744 | tf_op jit(solution)/shard_map/ppermute | solution.py:45
  49.3 4.2 %collective-permute-start.10 = (bf16[4,2,48,384]{3,2,1,0:T(8,128)(2,1)S(1)}, bf16[4,2,48,384]{3,2,1,0:T(8,128)(2,1)S(1)}, u32[]{:S(2)}, u32[]{:S(2)}) collective-permute-start(bf16[4,2,48,384]{3,2,1,0:T(8,128)(2,1)S(1)} %collective-permute-done.5.refs_4_), channel_id=1, source_target_pairs={{0,1},{1,0},{2,3},{3,2},{4,5},{5,4},{6,7},{7,6},{8,9},{9,8},{10,11... | collective-permute-start | bytes 884744 | tf_op jit(solution)/shard_map/ppermute | solution.py:45
  57.9 4.2 %collective-permute-start.12 = (f32[16,768]{1,0:T(8,128)S(1)}, f32[16,768]{1,0:T(8,128)S(1)}, u32[]{:S(2)}, u32[]{:S(2)}) collective-permute-start(f32[16,768]{1,0:T(8,128)S(1)} %get-tuple-element.35.refs_0_), channel_id=1, source_target_pairs={{0,64},{1,193},{2,66},{3,195},{4,68},{5,197},{6,70},{7,199},{8,72}... | collective-permute-start | bytes 147464 | tf_op jit(solution)/shard_map/ppermute | solution.py:45
  62.2 3.6 %collective-permute-start.13 = (f32[2,16,768]{2,1,0:T(8,128)S(1)}, f32[2,16,768]{2,1,0:T(8,128)S(1)}, u32[]{:S(2)}, u32[]{:S(2)}) collective-permute-start(f32[2,16,768]{2,1,0:T(8,128)S(1)} %pad_maximum_fusion.10), channel_id=1, source_target_pairs={{0,192},{1,65},{2,194},{3,67},{4,196},{5,69},{6,198},{7,71},{8,200... | collective-permute-start | bytes 294920 | tf_op jit(solution)/shard_map/ppermute | solution.py:45
  71.6 6.7 %collective-permute-start.14 = (bf16[4,4,2,48,384]{4,3,2,1,0:T(8,128)(2,1)S(1)}, bf16[4,4,2,48,384]{4,3,2,1,0:T(8,128)(2,1)S(1)}, u32[]{:S(2)}, u32[]{:S(2)}) collective-permute-start(bf16[4,4,2,48,384]{4,3,2,1,0:T(8,128)(2,1)S(1)} %get-tuple-element.40), channel_id=1, source_target_pairs={{0,1},{1,0},{2,3},{3,2},{4,5},{5,4},{6,7},{7,6},{8,9},{9,8},{10,11... | collective-permute-start | bytes 3538952 | tf_op jit(solution)/shard_map/ppermute | solution.py:45
  78.8 9.1 %collective-permute-start.15 = (bf16[2,4,2,48,384]{4,3,2,1,0:T(8,128)(2,1)S(1)}, bf16[2,4,2,48,384]{4,3,2,1,0:T(8,128)(2,1)S(1)}, u32[]{:S(2)}, u32[]{:S(2)}) collective-permute-start(bf16[2,4,2,48,384]{4,3,2,1,0:T(8,128)(2,1)S(1)} %slice.224), channel_id=1, source_target_pairs={{0,6},{1,3},{2,4},{3,1},{4,2},{5,7},{6,0},{7,5},{8,14},{9,11},{10,... | collective-permute-start | bytes 1769480 | tf_op jit(solution)/shard_map/ppermute | solution.py:45
  79.6 6.0 %collective-permute-start.16 = (bf16[2,4,48,384]{3,2,1,0:T(8,128)(2,1)S(1)}, bf16[2,4,48,384]{3,2,1,0:T(8,128)(2,1)S(1)}, u32[]{:S(2)}, u32[]{:S(2)}) collective-permute-start(bf16[2,4,48,384]{3,2,1,0:T(8,128)(2,1)S(1)} %slice.125), channel_id=1, source_target_pairs={{0,192},{1,65},{2,194},{3,67},{4,196},{5,69},{6,198},{7,71},{8,200... | collective-permute-start | bytes 884744 | tf_op jit(solution)/shard_map/ppermute | solution.py:45
  88.2 6.9 %collective-permute-start.17 = (bf16[4,2,48,384]{3,2,1,0:T(8,128)(2,1)S(1)}, bf16[4,2,48,384]{3,2,1,0:T(8,128)(2,1)S(1)}, u32[]{:S(2)}, u32[]{:S(2)}) collective-permute-start(bf16[4,2,48,384]{3,2,1,0:T(8,128)(2,1)S(1)} %fusion.2), channel_id=1, source_target_pairs={{0,2},{1,7},{2,0},{3,5},{4,6},{5,3},{6,4},{7,1},{8,10},{9,15},{10,... | collective-permute-start | bytes 884744 | tf_op jit(solution)/shard_map/ppermute | solution.py:45
  88.3 5.3 %collective-permute-start.18 = (bf16[4,48,384]{2,1,0:T(8,128)(2,1)S(1)}, bf16[4,48,384]{2,1,0:T(8,128)(2,1)S(1)}, u32[]{:S(2)}, u32[]{:S(2)}) collective-permute-start(bf16[4,48,384]{2,1,0:T(8,128)(2,1)S(1)} %fusion.5), channel_id=1, source_target_pairs={{0,64},{1,193},{2,66},{3,195},{4,68},{5,197},{6,70},{7,199},{8,72}... | collective-permute-start | bytes 442376 | tf_op jit(solution)/shard_map/ppermute | solution.py:45
  95.2 12.9 %collective-permute-start.20 = (bf16[3,48,384]{2,1,0:T(8,128)(2,1)S(1)}, bf16[3,48,384]{2,1,0:T(8,128)(2,1)S(1)}, u32[]{:S(2)}, u32[]{:S(2)}) collective-permute-start(bf16[3,48,384]{2,1,0:T(8,128)(2,1)S(1)} %pad_maximum_fusion.7), channel_id=1, source_target_pairs={{0,48},{1,41},{2,50},{3,43},{4,52},{5,45},{6,54},{7,47},{8,56},{9,... | collective-permute-start | bytes 331784 | tf_op jit(solution)/shard_map/ppermute | solution.py:45
  101.5 8.0 %collective-permute-start.21 = (bf16[3,48,384]{2,1,0:T(8,128)(2,1)S(1)}, bf16[3,48,384]{2,1,0:T(8,128)(2,1)S(1)}, u32[]{:S(2)}, u32[]{:S(2)}) collective-permute-start(bf16[3,48,384]{2,1,0:T(8,128)(2,1)S(1)} %pad_maximum_fusion.8), channel_id=1, source_target_pairs={{0,32},{1,25},{2,34},{3,27},{4,36},{5,29},{6,38},{7,31},{8,40},{9,... | collective-permute-start | bytes 331784 | tf_op jit(solution)/shard_map/ppermute | solution.py:45
  101.6 11.7 %collective-permute-start.22 = (bf16[3,48,384]{2,1,0:T(8,128)(2,1)S(1)}, bf16[3,48,384]{2,1,0:T(8,128)(2,1)S(1)}, u32[]{:S(2)}, u32[]{:S(2)}) collective-permute-start(bf16[3,48,384]{2,1,0:T(8,128)(2,1)S(1)} %pad_maximum_fusion.9), channel_id=1, source_target_pairs={{0,16},{1,9},{2,18},{3,11},{4,20},{5,13},{6,22},{7,15},{8,24},{9,1... | collective-permute-start | bytes 331784 | tf_op jit(solution)/shard_map/ppermute | solution.py:45
  104.3 9.0 %collective-permute-start.19 = (bf16[3,48,384]{2,1,0:T(8,128)(2,1)S(1)}, bf16[3,48,384]{2,1,0:T(8,128)(2,1)S(1)}, u32[]{:S(2)}, u32[]{:S(2)}) collective-permute-start(bf16[3,48,384]{2,1,0:T(8,128)(2,1)S(1)} %pad_maximum_fusion.6), channel_id=1, source_target_pairs={{0,0},{1,57},{2,2},{3,59},{4,4},{5,61},{6,6},{7,63},{8,8},{9,1},{1... | collective-permute-start | bytes 331784 | tf_op jit(solution)/shard_map/ppermute | solution.py:45
  114.2 1.5 %collective-permute-start.23 = (bf16[4,3,24,384]{3,2,1,0:T(8,128)(2,1)S(1)}, bf16[4,3,24,384]{3,2,1,0:T(8,128)(2,1)S(1)}, u32[]{:S(2)}, u32[]{:S(2)}) collective-permute-start(bf16[4,3,24,384]{3,2,1,0:T(8,128)(2,1)S(1)} %get-tuple-element.49), channel_id=1, source_target_pairs={{0,1},{1,0},{2,3},{3,2},{4,5},{5,4},{6,7},{7,6},{8,9},{9,8},{10,11... | collective-permute-start | bytes 663560 | tf_op jit(solution)/shard_map/ppermute | solution.py:45
  (3 other events, 20.1 us)
where the time goes:
time: 120 us; the launch traced here: 118 us
  waiting for transfers between devices  55.7 us (46%)
  starting transfers between devices  33.9 us (28%)
  Pallas kernels  23.5 us (20%)
  other arithmetic  2.99 us (2%)
    ppermute x24, waiting for transfers between devices, send(): return lax.ppermute(array, ('tm', 'head'), pairs(move))  55.7 us
    ppermute x24, starting transfers between devices, send(): return lax.ppermute(array, ('tm', 'head'), pairs(move))  33.9 us
    pallas_call x4, Pallas kernels, run(): pl.pallas_call(kernel, out_shape=out_shape, in_specs=[SMEM] * len(tables)...  19.7 us
  transfers between devices with their start and end apart: 24, of which 17 were waited for; matrix products, arithmetic and copies ran while one was open for 0% of the time, Pallas kernels for 8%

commit v1 on v0

--- a/solution.py
+++ b/solution.py
@@ -59,14 +59,22 @@
     return tm // NZ, tm % NZ, head // NC, head % NC
 
 
-def pack_kernel(query, grad, keys, values, keep, give):
+def pack_kernel(query, grad, keys, values, keep, give, rows, sems):
     _, z, _, c = position()
+    copies = [
+        pltpu.make_async_copy(array, rows.at[n], sems.at[n])
+        for n, array in enumerate((query, grad, keys, values))
+    ]
+    for copy in copies:
+        copy.start()
+    for copy in copies:
+        copy.wait()
     for j in range(4):
         mine = pl.ds(pl.multiple_of(((z + c + 2 * j) & 7) * COLS, HD), COLS)
         theirs = pl.ds(pl.multiple_of(((z + 1 - c + 2 * j) & 7) * COLS, HD), COLS)
-        for n, array in enumerate((query, grad, keys, values)):
-            keep[j, n] = array[:, mine]
-            give[j, n] = array[:, theirs]
+        for n in range(4):
+            keep[j, n] = rows[n, :, mine]
+            give[j, n] = rows[n, :, theirs]
 
 
 def unpack_kernel(mine, theirs, *outs):
@@ -264,8 +272,8 @@
     lax.fori_loop(0, QROWS // QCHUNK, chunk, 0)
 
 
-def combine(st0, st1, st23, levels):
-    sts = [st0[...], st1[...], st23[0], st23[1]]
+def combine(parts, levels):
+    sts = [st[...] for st in parts]
     top = functools.reduce(jnp.maximum, [st[0:3, :] for st in sts])
     factors = [jnp.exp2(st[0:3, :] - top) for st in sts]
     total = sum(f * st[3:6, :] for f, st in zip(factors, sts))
@@ -282,8 +290,8 @@
     q_group, q_live, q_first, tops = place_queries(at, groups, valid)
     k_group, k_live, k_first, blocks = place_keys(at, groups, valid, o, tops)
     if o == 1:
-        dkv, dqt, levels, dks, dvs = refs[3:8]
-        combine(*refs[0:3], levels)
+        dkv, dqt, levels, dks, dvs = refs[4:9]
+        combine(refs[0:4], levels)
         dqt[...] = jnp.zeros_like(dqt)
     else:
         before, levels, dkv, dq, dqt, dks, dvs, dqs = refs
@@ -297,19 +305,24 @@
         def step(keys, _):
             group = kgrp[keys, :]
             ok = jnp.concatenate([group] * (QCHUNK // HD), axis=1) <= qgrp[0:1, rows]
+            products = []
             for h in range(HEADS):
                 cols = slice(h * HD, (h + 1) * HD)
-                key = kbuf[0, keys, cols]
-                query = qbuf[0, rows, cols]
-                grad = qbuf[1, rows, cols]
-                scores = dot(key, query, NT)
-                dprobs = dot(kbuf[1, keys, cols], grad, NT)
+                scores = dot(kbuf[0, keys, cols], qbuf[0, rows, cols], NT)
+                products.append((scores, dot(kbuf[1, keys, cols], qbuf[1, rows, cols], NT)))
+            weights = []
+            for h in range(HEADS):
+                scores, dprobs = products[h]
                 scores = jnp.where(ok, scores * (SCALE * LOG2E), NEG)
                 probs = jnp.exp2(scores - levels[h : h + 1, rows])
-                dscores = (probs * (dprobs - levels[3 + h : 4 + h, rows])).astype(jnp.bfloat16)
-                dvs[keys, cols] += dot(probs.astype(jnp.bfloat16), grad, NN)
-                dks[keys, cols] += dot(dscores, query, NN)
-                dqt[h, :, rows] += dot(key, dscores, TN)
+                dscores = probs * (dprobs - levels[3 + h : 4 + h, rows])
+                weights.append((probs.astype(jnp.bfloat16), dscores.astype(jnp.bfloat16)))
+            for h in range(HEADS):
+                cols = slice(h * HD, (h + 1) * HD)
+                probs, dscores = weights[h]
+                dvs[keys, cols] += dot(probs, qbuf[1, rows, cols], NN)
+                dks[keys, cols] += dot(dscores, qbuf[0, rows, cols], NN)
+                dqt[h, :, rows] += dot(kbuf[0, keys, cols], dscores, TN)
             return 0
 
         visit(pick(blocks, n), step, 0)
@@ -335,7 +348,9 @@
 
 SMEM = pl.BlockSpec(memory_space=pltpu.SMEM)
 VMEM = pl.BlockSpec(memory_space=pltpu.VMEM)
-PARAMS = pltpu.CompilerParams(vmem_limit_bytes=48 * 1024 * 1024)
+PARAMS = pltpu.CompilerParams(vmem_limit_bytes=24 * 1024 * 1024)
+LARGE = pltpu.CompilerParams(vmem_limit_bytes=60 * 1024 * 1024)
+SMALL = pltpu.CompilerParams(vmem_limit_bytes=6 * 1024 * 1024)
 
 
 def run(kernel, name, out_shape, tables, arrays, scratch=()):
@@ -358,8 +373,10 @@
     keep, give = pl.pallas_call(
         pack_kernel,
         out_shape=(jax.ShapeDtypeStruct((4, 4, SUB, COLS), bf16),) * 2,
-        in_specs=[VMEM] * 4,
+        in_specs=[pl.BlockSpec(memory_space=pltpu.HBM)] * 4,
         out_specs=(VMEM,) * 2,
+        scratch_shapes=[pltpu.VMEM((4, SUB, NZ * COLS), bf16), pltpu.SemaphoreType.DMA((4,))],
+        compiler_params=LARGE,
         name="pack",
     )(query, dout, keys, values)
     take = swap_core(give)
@@ -393,8 +410,7 @@
         (qbuf, qgrp, part, swap_core(own_kv), swap_core(kv_first), swap_core(kv_rest)),
     )
 
-    stats_first = first_y(stats)
-    stats_rest = second_y(jnp.stack([stats, stats_first]))
+    all_stats = [stats] + [send(stats, lambda y, z, x, c: (y + n, z, x, c)) for n in (1, 2, 3)]
 
     dkv_type = jax.ShapeDtypeStruct((4, 4, 2, PART, COLS), bf16)
     scratch = [
@@ -411,7 +427,7 @@
             jax.ShapeDtypeStruct((8, QROWS), f32),
         ),
         tables,
-        (qbuf, qgrp, kbuf_other, kgrp_other, stats, stats_first, stats_rest),
+        (qbuf, qgrp, kbuf_other, kgrp_other, *all_stats),
         scratch[1:],
     )
     swapped = swap_core(dkv_other)
@@ -447,6 +463,7 @@
         out_shape=(jax.ShapeDtypeStruct((SUB, NZ * COLS), bf16),) * 3,
         in_specs=[VMEM] * 2,
         out_specs=(VMEM,) * 3,
+        compiler_params=SMALL,
         name="unpack",
     )(jnp.where(c == 0, first, second), theirs)
 

time: 120 us -> 118 us (0.983)
  starting transfers between devices: 33.9 us -> 39.3 us
  waiting for transfers between devices: 55.7 us -> 50.5 us
    ppermute x24 -> x25, starting transfers between devices: 33.9 us -> 39.3 us  [send(): return lax.ppermute(array, ('tm', 'head'), pairs(move))]
    ppermute x24 -> x25, waiting for transfers between devices: 55.7 us -> 50.5 us  [send(): return lax.ppermute(array, ('tm', 'head'), pairs(move))]
  transfers between devices with their start and end apart: 24 -> 25, of which waited for: 17 -> 18; matrix products, arithmetic and copies ran while one was open for 0% -> 0% of each run, Pallas kernels for 8% -> 10%
where the time goes in v1:
time: 118 us; the launch traced here: 117 us
  waiting for transfers between devices  50.5 us (43%)
  starting transfers between devices  39.3 us (33%)
  Pallas kernels  23.6 us (20%)
  other arithmetic  2.29 us (2%)
    ppermute x25, waiting for transfers between devices, send(): return lax.ppermute(array, ('tm', 'head'), pairs(move))  50.5 us
    ppermute x25, starting transfers between devices, send(): return lax.ppermute(array, ('tm', 'head'), pairs(move))  39.3 us
    pallas_call x4, Pallas kernels, run(): pl.pallas_call(kernel, out_shape=out_shape, in_specs=[SMEM] * len(tables)...  20.7 us
  transfers between devices with their start and end apart: 25, of which 18 were waited for; matrix products, arithmetic and copies ran while one was open for 0% of the time, Pallas kernels for 10%

profile of v1, /device:TPU:1, one launch (start us, length us, event | category | flops | bytes accessed | tf_op | source)
XLA Modules:
  0.0 117.1 jit_solution(7965657293273873912)
XLA Ops:
  0.6 2.0 %pack.1 = (bf16[4,4,24,384]{3,2,1,0:T(8,128)(2,1)}, bf16[4,4,24,384]{3,2,1,0:T(8,128)(2,1)}) custom-call(bf16[24,3072]{1,0:T(8,128)(2,1)} %query.1, bf16[24,3072]{1,0:T(8,128)(2,1)} %grad.1, bf16[24,3072]{1,0:T(8,128)(2,1)} %keys.1, bf16[24,3072]{1,0:T(8,128)(2,1)} %values.1), custom_call_target="tpu_custom_call" | custom-call | tf_op jit(solution)/shard_map/pack/pallas_call | solution.py:373
  2.7 3.3 %collective-permute-start = (bf16[4,4,24,384]{3,2,1,0:T(8,128)(2,1)}, bf16[4,4,24,384]{3,2,1,0:T(8,128)(2,1)S(1)}, u32[]{:S(2)}, u32[]{:S(2)}) collective-permute-start(bf16[4,4,24,384]{3,2,1,0:T(8,128)(2,1)} %get-tuple-element.25), channel_id=1, source_target_pairs={{0,1},{1,0},{2,3},{3,2},{4,5},{5,4},{6,7},{7,6},{8,9},{9,8},{10,11... | collective-permute-start | bytes 884744 | tf_op jit(solution)/shard_map/ppermute | solution.py:45
  10.6 3.9 %collective-permute-start.4 = (bf16[4,48,384]{2,1,0:T(8,128)(2,1)S(1)}, bf16[4,48,384]{2,1,0:T(8,128)(2,1)S(1)}, u32[]{:S(2)}, u32[]{:S(2)}) collective-permute-start(bf16[4,48,384]{2,1,0:T(8,128)(2,1)S(1)} %get-tuple-element.46), channel_id=1, source_target_pairs={{0,48},{1,57},{2,50},{3,59},{4,52},{5,61},{6,54},{7,63},{8,56},{9,... | collective-permute-start | bytes 442376 | tf_op jit(solution)/shard_map/ppermute | solution.py:45
  14.6 2.3 %collective-permute-start.3 = (bf16[4,48,384]{2,1,0:T(8,128)(2,1)S(1)}, bf16[4,48,384]{2,1,0:T(8,128)(2,1)S(1)}, u32[]{:S(2)}, u32[]{:S(2)}) collective-permute-start(bf16[4,48,384]{2,1,0:T(8,128)(2,1)S(1)} %get-tuple-element.47), channel_id=1, source_target_pairs={{0,32},{1,41},{2,34},{3,43},{4,36},{5,45},{6,38},{7,47},{8,40},{9,... | collective-permute-start | bytes 442376 | tf_op jit(solution)/shard_map/ppermute | solution.py:45
  17.9 5.1 %collective-permute-done.4 = bf16[4,48,384]{2,1,0:T(8,128)(2,1)S(1)} collective-permute-done((bf16[4,48,384]{2,1,0:T(8,128)(2,1)S(1)}, bf16[4,48,384]{2,1,0:T(8,128)(2,1)S(1)}, u32[]{:S(2)}, u32[]{:S(2)}) %collective-permute-start.4) | collective-permute-done | bytes 147488 | tf_op jit(solution)/shard_map/ppermute | solution.py:45
  23.0 4.7 %collective-permute-done.3 = bf16[4,48,384]{2,1,0:T(8,128)(2,1)S(1)} collective-permute-done((bf16[4,48,384]{2,1,0:T(8,128)(2,1)S(1)}, bf16[4,48,384]{2,1,0:T(8,128)(2,1)S(1)}, u32[]{:S(2)}, u32[]{:S(2)}) %collective-permute-start.3) | collective-permute-done | bytes 147488 | tf_op jit(solution)/shard_map/ppermute | solution.py:45
  27.7 2.3 %collective-permute-done.2 = bf16[4,48,384]{2,1,0:T(8,128)(2,1)S(1)} collective-permute-done((bf16[4,48,384]{2,1,0:T(8,128)(2,1)S(1)}, bf16[4,48,384]{2,1,0:T(8,128)(2,1)S(1)}, u32[]{:S(2)}, u32[]{:S(2)}) %collective-permute-start.2) | collective-permute-done | bytes 147488 | tf_op jit(solution)/shard_map/ppermute | solution.py:45
  30.1 2.6 %collective-permute-start.5 = (bf16[4,2,48,384]{3,2,1,0:T(8,128)(2,1)S(1)}, bf16[4,2,48,384]{3,2,1,0:T(8,128)(2,1)S(1)}, u32[]{:S(2)}, u32[]{:S(2)}) collective-permute-start(bf16[4,2,48,384]{3,2,1,0:T(8,128)(2,1)S(1)} %get-tuple-element.56.refs_3_), channel_id=1, source_target_pairs={{0,2},{1,7},{2,0},{3,5},{4,6},{5,3},{6,4},{7,1},{8,10},{9,15},{10,... | collective-permute-start | bytes 884744 | tf_op jit(solution)/shard_map/ppermute | solution.py:45
  32.8 2.8 %collective-permute-start.6 = (bf16[4,2,48,384]{3,2,1,0:T(8,128)(2,1)S(1)}, bf16[4,2,48,384]{3,2,1,0:T(8,128)(2,1)S(1)}, u32[]{:S(2)}, u32[]{:S(2)}) collective-permute-start(bf16[4,2,48,384]{3,2,1,0:T(8,128)(2,1)S(1)} %get-tuple-element.58.refs_0_), channel_id=1, source_target_pairs={{0,64},{1,193},{2,66},{3,195},{4,68},{5,197},{6,70},{7,199},{8,72}... | collective-permute-start | bytes 884744 | tf_op jit(solution)/shard_map/ppermute | solution.py:45
  37.0 2.7 %collective-permute-done.6.refs_1_ = bf16[4,2,48,384]{3,2,1,0:T(8,128)(2,1)S(1)} collective-permute-done((bf16[4,2,48,384]{3,2,1,0:T(8,128)(2,1)S(1)}, bf16[4,2,48,384]{3,2,1,0:T(8,128)(2,1)S(1)}, u32[]{:S(2)}, u32[]{:S(2)}) %collective-permute-start.6) | collective-permute-done | bytes 294944 | tf_op jit(solution)/shard_map/ppermute | solution.py:45
  40.1 8.8 %collective-permute-done.8.refs_5_ = bf16[2,4,2,48,384]{4,3,2,1,0:T(8,128)(2,1)S(1)} collective-permute-done((bf16[2,4,2,48,384]{4,3,2,1,0:T(8,128)(2,1)S(1)}, bf16[2,4,2,48,384]{4,3,2,1,0:T(8,128)(2,1)S(1)}, u32[]{:S(2)}, u32[]{:S(2)}) %collective-permute-start.8) | collective-permute-done | bytes 589856 | tf_op jit(solution)/shard_map/ppermute | solution.py:45
  49.5 5.1 %stats_own.1 = (bf16[2,768,384]{2,1,0:T(8,128)(2,1)S(1)}, s32[8,768]{1,0:T(8,128)S(1)}, bf16[2,768,384]{2,1,0:T(8,128)(2,1)S(1)}, s32[768,128]{1,0:T(8,128)S(1)}, f32[16,768]{1,0:T(8,128)S(1)}) custom-call(s32[32]{0:T(128)S(1)} %copy-done, s32[32]{0:T(128)S(1)} %copy-done.1, bf16[4,2,48,384]{3,2,1,0:T(8,128)(2,1)S(1)} %get-tuple-element.58.refs_0_, ...), custom_call_target="tpu_custom_call" | custom-call | flops 3000000000 | bytes 6000000 | tf_op jit(solution)/shard_map/stats_own/pallas_call | solution.py:357
  54.6 4.2 %stats_other.1 = (bf16[2,768,384]{2,1,0:T(8,128)(2,1)S(1)}, s32[768,128]{1,0:T(8,128)S(1)}, f32[16,768]{1,0:T(8,128)S(1)}) custom-call(s32[32]{0:T(128)S(1)} %copy-done, s32[32]{0:T(128)S(1)} %copy-done.1, bf16[2,768,384]{2,1,0:T(8,128)(2,1)S(1)} %get-tuple-element.28.refs_0_.qbuf, s32[8,768]{1,0:T(8,128)S(1)} %get-tuple-element.29.refs_1_.qgrp, ...), custom_call_target="tpu_custom_call" | custom-call | flops 3000000000 | bytes 6000000 | tf_op jit(solution)/shard_map/stats_other/pallas_call | solution.py:357
  61.8 3.2 %collective-permute-done.13.refs_2_ = f32[16,768]{1,0:T(8,128)S(1)} collective-permute-done((f32[16,768]{1,0:T(8,128)S(1)}, f32[16,768]{1,0:T(8,128)S(1)}, u32[]{:S(2)}, u32[]{:S(2)}) %collective-permute-start.13) | collective-permute-done | bytes 49184 | tf_op jit(solution)/shard_map/ppermute | solution.py:45
  65.3 5.2 %grads_other.1 = (bf16[4,4,2,48,384]{4,3,2,1,0:T(8,128)(2,1)S(1)}, f32[3,128,768]{2,1,0:T(8,128)S(1)}, f32[8,768]{1,0:T(8,128)S(1)}) custom-call(s32[32]{0:T(128)S(1)} %copy-done, s32[32]{0:T(128)S(1)} %copy-done.1, bf16[2,768,384]{2,1,0:T(8,128)(2,1)S(1)} %get-tuple-element.28.refs_0_.qbuf, s32[8,768]{1,0:T(8,128)S(1)} %get-tuple-element.29.refs_1_.qgrp, ...), custom_call_target="tpu_custom_call" | custom-call | flops 3000000000 | bytes 6000000 | tf_op jit(solution)/shard_map/grads_other/pallas_call | solution.py:357
  70.5 2.7 %collective-permute-start.15 = (bf16[4,4,2,48,384]{4,3,2,1,0:T(8,128)(2,1)S(1)}, bf16[4,4,2,48,384]{4,3,2,1,0:T(8,128)(2,1)S(1)}, u32[]{:S(2)}, u32[]{:S(2)}) collective-permute-start(bf16[4,4,2,48,384]{4,3,2,1,0:T(8,128)(2,1)S(1)} %get-tuple-element.40), channel_id=1, source_target_pairs={{0,1},{1,0},{2,3},{3,2},{4,5},{5,4},{6,7},{7,6},{8,9},{9,8},{10,11... | collective-permute-start | bytes 3538952 | tf_op jit(solution)/shard_map/ppermute | solution.py:45
  73.2 6.3 %grads_own.1 = (bf16[4,4,2,48,384]{4,3,2,1,0:T(8,128)(2,1)S(1)}, bf16[4,4,48,384]{3,2,1,0:T(8,128)(2,1)S(1)}) custom-call(s32[32]{0:T(128)S(1)} %copy-done, s32[32]{0:T(128)S(1)} %copy-done.1, bf16[2,768,384]{2,1,0:T(8,128)(2,1)S(1)} %get-tuple-element.28.refs_0_.qbuf, s32[8,768]{1,0:T(8,128)S(1)} %get-tuple-element.29.refs_1_.qgrp, ...), custom_call_target="tpu_custom_call" | custom-call | flops 3000000000 | bytes 6000000 | tf_op jit(solution)/shard_map/grads_own/pallas_call | solution.py:357
  81.2 5.9 %collective-permute-done.17 = bf16[2,4,48,384]{3,2,1,0:T(8,128)(2,1)S(1)} collective-permute-done((bf16[2,4,48,384]{3,2,1,0:T(8,128)(2,1)S(1)}, bf16[2,4,48,384]{3,2,1,0:T(8,128)(2,1)S(1)}, u32[]{:S(2)}, u32[]{:S(2)}) %collective-permute-start.17) | collective-permute-done | bytes 294944 | tf_op jit(solution)/shard_map/ppermute | solution.py:45
  89.5 5.2 %collective-permute-done.19 = bf16[4,48,384]{2,1,0:T(8,128)(2,1)S(1)} collective-permute-done((bf16[4,48,384]{2,1,0:T(8,128)(2,1)S(1)}, bf16[4,48,384]{2,1,0:T(8,128)(2,1)S(1)}, u32[]{:S(2)}, u32[]{:S(2)}) %collective-permute-start.19) | collective-permute-done | bytes 147488 | tf_op jit(solution)/shard_map/ppermute | solution.py:45
  96.3 3.8 %collective-permute-start.21 = (bf16[3,48,384]{2,1,0:T(8,128)(2,1)S(1)}, bf16[3,48,384]{2,1,0:T(8,128)(2,1)S(1)}, u32[]{:S(2)}, u32[]{:S(2)}) collective-permute-start(bf16[3,48,384]{2,1,0:T(8,128)(2,1)S(1)} %pad_maximum_fusion.7), channel_id=1, source_target_pairs={{0,48},{1,41},{2,50},{3,43},{4,52},{5,45},{6,54},{7,47},{8,56},{9,... | collective-permute-start | bytes 331784 | tf_op jit(solution)/shard_map/ppermute | solution.py:45
  100.2 2.7 %collective-permute-start.23 = (bf16[3,48,384]{2,1,0:T(8,128)(2,1)S(1)}, bf16[3,48,384]{2,1,0:T(8,128)(2,1)S(1)}, u32[]{:S(2)}, u32[]{:S(2)}) collective-permute-start(bf16[3,48,384]{2,1,0:T(8,128)(2,1)S(1)} %pad_maximum_fusion.9), channel_id=1, source_target_pairs={{0,16},{1,9},{2,18},{3,11},{4,20},{5,13},{6,22},{7,15},{8,24},{9,1... | collective-permute-start | bytes 331784 | tf_op jit(solution)/shard_map/ppermute | solution.py:45
  103.0 1.9 %collective-permute-start.20 = (bf16[3,48,384]{2,1,0:T(8,128)(2,1)S(1)}, bf16[3,48,384]{2,1,0:T(8,128)(2,1)S(1)}, u32[]{:S(2)}, u32[]{:S(2)}) collective-permute-start(bf16[3,48,384]{2,1,0:T(8,128)(2,1)S(1)} %pad_maximum_fusion.6), channel_id=1, source_target_pairs={{0,0},{1,57},{2,2},{3,59},{4,4},{5,61},{6,6},{7,63},{8,8},{9,1},{1... | collective-permute-start | bytes 331784 | tf_op jit(solution)/shard_map/ppermute | solution.py:45
  104.9 3.1 %collective-permute-done.22 = bf16[3,48,384]{2,1,0:T(8,128)(2,1)S(1)} collective-permute-done((bf16[3,48,384]{2,1,0:T(8,128)(2,1)S(1)}, bf16[3,48,384]{2,1,0:T(8,128)(2,1)S(1)}, u32[]{:S(2)}, u32[]{:S(2)}) %collective-permute-start.22) | collective-permute-done | bytes 110624 | tf_op jit(solution)/shard_map/ppermute | solution.py:45
  109.4 5.7 %collective-permute-start.24 = (bf16[4,3,24,384]{3,2,1,0:T(8,128)(2,1)S(1)}, bf16[4,3,24,384]{3,2,1,0:T(8,128)(2,1)S(1)}, u32[]{:S(2)}, u32[]{:S(2)}) collective-permute-start(bf16[4,3,24,384]{3,2,1,0:T(8,128)(2,1)S(1)} %get-tuple-element.49), channel_id=1, source_target_pairs={{0,1},{1,0},{2,3},{3,2},{4,5},{5,4},{6,7},{7,6},{8,9},{9,8},{10,11... | collective-permute-start | bytes 663560 | tf_op jit(solution)/shard_map/ppermute | solution.py:45
  (66 shorter events, 20.4 us)
Async XLA Ops:
  2.7 4.7 %collective-permute-start = (bf16[4,4,24,384]{3,2,1,0:T(8,128)(2,1)}, bf16[4,4,24,384]{3,2,1,0:T(8,128)(2,1)S(1)}, u32[]{:S(2)}, u32[]{:S(2)}) collective-permute-start(bf16[4,4,24,384]{3,2,1,0:T(8,128)(2,1)} %get-tuple-element.25), channel_id=1, source_target_pairs={{0,1},{1,0},{2,3},{3,2},{4,5},{5,4},{6,7},{7,6},{8,9},{9,8},{10,11... | collective-permute-start | bytes 884744 | tf_op jit(solution)/shard_map/ppermute | solution.py:45
  8.7 9.1 %collective-permute-start.1 = (bf16[4,48,384]{2,1,0:T(8,128)(2,1)S(1)}, bf16[4,48,384]{2,1,0:T(8,128)(2,1)S(1)}, u32[]{:S(2)}, u32[]{:S(2)}) collective-permute-start(bf16[4,48,384]{2,1,0:T(8,128)(2,1)S(1)} %get-tuple-element.45), channel_id=1, source_target_pairs={{0,0},{1,9},{2,2},{3,11},{4,4},{5,13},{6,6},{7,15},{8,8},{9,17},{1... | collective-permute-start | bytes 442376 | tf_op jit(solution)/shard_map/ppermute | solution.py:45
  10.6 12.3 %collective-permute-start.4 = (bf16[4,48,384]{2,1,0:T(8,128)(2,1)S(1)}, bf16[4,48,384]{2,1,0:T(8,128)(2,1)S(1)}, u32[]{:S(2)}, u32[]{:S(2)}) collective-permute-start(bf16[4,48,384]{2,1,0:T(8,128)(2,1)S(1)} %get-tuple-element.46), channel_id=1, source_target_pairs={{0,48},{1,57},{2,50},{3,59},{4,52},{5,61},{6,54},{7,63},{8,56},{9,... | collective-permute-start | bytes 442376 | tf_op jit(solution)/shard_map/ppermute | solution.py:45
  14.6 13.1 %collective-permute-start.3 = (bf16[4,48,384]{2,1,0:T(8,128)(2,1)S(1)}, bf16[4,48,384]{2,1,0:T(8,128)(2,1)S(1)}, u32[]{:S(2)}, u32[]{:S(2)}) collective-permute-start(bf16[4,48,384]{2,1,0:T(8,128)(2,1)S(1)} %get-tuple-element.47), channel_id=1, source_target_pairs={{0,32},{1,41},{2,34},{3,43},{4,36},{5,45},{6,38},{7,47},{8,40},{9,... | collective-permute-start | bytes 442376 | tf_op jit(solution)/shard_map/ppermute | solution.py:45
  16.9 13.1 %collective-permute-start.2 = (bf16[4,48,384]{2,1,0:T(8,128)(2,1)S(1)}, bf16[4,48,384]{2,1,0:T(8,128)(2,1)S(1)}, u32[]{:S(2)}, u32[]{:S(2)}) collective-permute-start(bf16[4,48,384]{2,1,0:T(8,128)(2,1)S(1)} %get-tuple-element.48), channel_id=1, source_target_pairs={{0,16},{1,25},{2,18},{3,27},{4,20},{5,29},{6,22},{7,31},{8,24},{9,... | collective-permute-start | bytes 442376 | tf_op jit(solution)/shard_map/ppermute | solution.py:45
  30.1 6.9 %collective-permute-start.5 = (bf16[4,2,48,384]{3,2,1,0:T(8,128)(2,1)S(1)}, bf16[4,2,48,384]{3,2,1,0:T(8,128)(2,1)S(1)}, u32[]{:S(2)}, u32[]{:S(2)}) collective-permute-start(bf16[4,2,48,384]{3,2,1,0:T(8,128)(2,1)S(1)} %get-tuple-element.56.refs_3_), channel_id=1, source_target_pairs={{0,2},{1,7},{2,0},{3,5},{4,6},{5,3},{6,4},{7,1},{8,10},{9,15},{10,... | collective-permute-start | bytes 884744 | tf_op jit(solution)/shard_map/ppermute | solution.py:45
  32.8 6.9 %collective-permute-start.6 = (bf16[4,2,48,384]{3,2,1,0:T(8,128)(2,1)S(1)}, bf16[4,2,48,384]{3,2,1,0:T(8,128)(2,1)S(1)}, u32[]{:S(2)}, u32[]{:S(2)}) collective-permute-start(bf16[4,2,48,384]{3,2,1,0:T(8,128)(2,1)S(1)} %get-tuple-element.58.refs_0_), channel_id=1, source_target_pairs={{0,64},{1,193},{2,66},{3,195},{4,68},{5,197},{6,70},{7,199},{8,72}... | collective-permute-start | bytes 884744 | tf_op jit(solution)/shard_map/ppermute | solution.py:45
  39.8 9.1 %collective-permute-start.8 = (bf16[2,4,2,48,384]{4,3,2,1,0:T(8,128)(2,1)S(1)}, bf16[2,4,2,48,384]{4,3,2,1,0:T(8,128)(2,1)S(1)}, u32[]{:S(2)}, u32[]{:S(2)}) collective-permute-start(bf16[2,4,2,48,384]{4,3,2,1,0:T(8,128)(2,1)S(1)} %pad_maximum_fusion.1), channel_id=1, source_target_pairs={{0,6},{1,3},{2,4},{3,1},{4,2},{5,7},{6,0},{7,5},{8,14},{9,11},{10,... | collective-permute-start | bytes 1769480 | tf_op jit(solution)/shard_map/ppermute | solution.py:45
  40.0 9.5 %collective-permute-start.7 = (bf16[2,4,2,48,384]{4,3,2,1,0:T(8,128)(2,1)S(1)}, bf16[2,4,2,48,384]{4,3,2,1,0:T(8,128)(2,1)S(1)}, u32[]{:S(2)}, u32[]{:S(2)}) collective-permute-start(bf16[2,4,2,48,384]{4,3,2,1,0:T(8,128)(2,1)S(1)} %pad_maximum_fusion), channel_id=1, source_target_pairs={{0,192},{1,65},{2,194},{3,67},{4,196},{5,69},{6,198},{7,71},{8,200... | collective-permute-start | bytes 1769480 | tf_op jit(solution)/shard_map/ppermute | solution.py:45
  48.9 5.7 %collective-permute-start.11 = (bf16[2,4,2,48,384]{4,3,2,1,0:T(8,128)(2,1)S(1)}, bf16[2,4,2,48,384]{4,3,2,1,0:T(8,128)(2,1)S(1)}, u32[]{:S(2)}, u32[]{:S(2)}) collective-permute-start(bf16[2,4,2,48,384]{4,3,2,1,0:T(8,128)(2,1)S(1)} %collective-permute-done.8.refs_5_), channel_id=1, source_target_pairs={{0,1},{1,0},{2,3},{3,2},{4,5},{5,4},{6,7},{7,6},{8,9},{9,8},{10,11... | collective-permute-start | bytes 1769480 | tf_op jit(solution)/shard_map/ppermute | solution.py:45
  48.9 5.7 %collective-permute-start.9 = (bf16[4,2,48,384]{3,2,1,0:T(8,128)(2,1)S(1)}, bf16[4,2,48,384]{3,2,1,0:T(8,128)(2,1)S(1)}, u32[]{:S(2)}, u32[]{:S(2)}) collective-permute-start(bf16[4,2,48,384]{3,2,1,0:T(8,128)(2,1)S(1)} %get-tuple-element.56.refs_3_), channel_id=1, source_target_pairs={{0,1},{1,0},{2,3},{3,2},{4,5},{5,4},{6,7},{7,6},{8,9},{9,8},{10,11... | collective-permute-start | bytes 884744 | tf_op jit(solution)/shard_map/ppermute | solution.py:45
  49.4 5.2 %collective-permute-start.10 = (bf16[4,2,48,384]{3,2,1,0:T(8,128)(2,1)S(1)}, bf16[4,2,48,384]{3,2,1,0:T(8,128)(2,1)S(1)}, u32[]{:S(2)}, u32[]{:S(2)}) collective-permute-start(bf16[4,2,48,384]{3,2,1,0:T(8,128)(2,1)S(1)} %collective-permute-done.5.refs_4_), channel_id=1, source_target_pairs={{0,1},{1,0},{2,3},{3,2},{4,5},{5,4},{6,7},{7,6},{8,9},{9,8},{10,11... | collective-permute-start | bytes 884744 | tf_op jit(solution)/shard_map/ppermute | solution.py:45
  60.4 4.6 %collective-permute-start.13 = (f32[16,768]{1,0:T(8,128)S(1)}, f32[16,768]{1,0:T(8,128)S(1)}, u32[]{:S(2)}, u32[]{:S(2)}) collective-permute-start(f32[16,768]{1,0:T(8,128)S(1)} %get-tuple-element.35.refs_0_), channel_id=1, source_target_pairs={{0,128},{1,129},{2,130},{3,131},{4,132},{5,133},{6,134},{7,135},{8... | collective-permute-start | bytes 147464 | tf_op jit(solution)/shard_map/ppermute | solution.py:45
  60.6 4.7 %collective-permute-start.12 = (f32[16,768]{1,0:T(8,128)S(1)}, f32[16,768]{1,0:T(8,128)S(1)}, u32[]{:S(2)}, u32[]{:S(2)}) collective-permute-start(f32[16,768]{1,0:T(8,128)S(1)} %get-tuple-element.35.refs_0_), channel_id=1, source_target_pairs={{0,64},{1,65},{2,66},{3,67},{4,68},{5,69},{6,70},{7,71},{8,72},{9,... | collective-permute-start | bytes 147464 | tf_op jit(solution)/shard_map/ppermute | solution.py:45
  70.5 9.0 %collective-permute-start.15 = (bf16[4,4,2,48,384]{4,3,2,1,0:T(8,128)(2,1)S(1)}, bf16[4,4,2,48,384]{4,3,2,1,0:T(8,128)(2,1)S(1)}, u32[]{:S(2)}, u32[]{:S(2)}) collective-permute-start(bf16[4,4,2,48,384]{4,3,2,1,0:T(8,128)(2,1)S(1)} %get-tuple-element.40), channel_id=1, source_target_pairs={{0,1},{1,0},{2,3},{3,2},{4,5},{5,4},{6,7},{7,6},{8,9},{9,8},{10,11... | collective-permute-start | bytes 3538952 | tf_op jit(solution)/shard_map/ppermute | solution.py:45
  79.9 9.1 %collective-permute-start.16 = (bf16[2,4,2,48,384]{4,3,2,1,0:T(8,128)(2,1)S(1)}, bf16[2,4,2,48,384]{4,3,2,1,0:T(8,128)(2,1)S(1)}, u32[]{:S(2)}, u32[]{:S(2)}) collective-permute-start(bf16[2,4,2,48,384]{4,3,2,1,0:T(8,128)(2,1)S(1)} %slice.224), channel_id=1, source_target_pairs={{0,6},{1,3},{2,4},{3,1},{4,2},{5,7},{6,0},{7,5},{8,14},{9,11},{10,... | collective-permute-start | bytes 1769480 | tf_op jit(solution)/shard_map/ppermute | solution.py:45
  81.1 6.0 %collective-permute-start.17 = (bf16[2,4,48,384]{3,2,1,0:T(8,128)(2,1)S(1)}, bf16[2,4,48,384]{3,2,1,0:T(8,128)(2,1)S(1)}, u32[]{:S(2)}, u32[]{:S(2)}) collective-permute-start(bf16[2,4,48,384]{3,2,1,0:T(8,128)(2,1)S(1)} %slice.125), channel_id=1, source_target_pairs={{0,192},{1,65},{2,194},{3,67},{4,196},{5,69},{6,198},{7,71},{8,200... | collective-permute-start | bytes 884744 | tf_op jit(solution)/shard_map/ppermute | solution.py:45
  89.2 6.9 %collective-permute-start.18 = (bf16[4,2,48,384]{3,2,1,0:T(8,128)(2,1)S(1)}, bf16[4,2,48,384]{3,2,1,0:T(8,128)(2,1)S(1)}, u32[]{:S(2)}, u32[]{:S(2)}) collective-permute-start(bf16[4,2,48,384]{3,2,1,0:T(8,128)(2,1)S(1)} %fusion.2), channel_id=1, source_target_pairs={{0,2},{1,7},{2,0},{3,5},{4,6},{5,3},{6,4},{7,1},{8,10},{9,15},{10,... | collective-permute-start | bytes 884744 | tf_op jit(solution)/shard_map/ppermute | solution.py:45
  89.4 5.3 %collective-permute-start.19 = (bf16[4,48,384]{2,1,0:T(8,128)(2,1)S(1)}, bf16[4,48,384]{2,1,0:T(8,128)(2,1)S(1)}, u32[]{:S(2)}, u32[]{:S(2)}) collective-permute-start(bf16[4,48,384]{2,1,0:T(8,128)(2,1)S(1)} %fusion.5), channel_id=1, source_target_pairs={{0,64},{1,193},{2,66},{3,195},{4,68},{5,197},{6,70},{7,199},{8,72}... | collective-permute-start | bytes 442376 | tf_op jit(solution)/shard_map/ppermute | solution.py:45
  96.3 8.6 %collective-permute-start.21 = (bf16[3,48,384]{2,1,0:T(8,128)(2,1)S(1)}, bf16[3,48,384]{2,1,0:T(8,128)(2,1)S(1)}, u32[]{:S(2)}, u32[]{:S(2)}) collective-permute-start(bf16[3,48,384]{2,1,0:T(8,128)(2,1)S(1)} %pad_maximum_fusion.7), channel_id=1, source_target_pairs={{0,48},{1,41},{2,50},{3,43},{4,52},{5,45},{6,54},{7,47},{8,56},{9,... | collective-permute-start | bytes 331784 | tf_op jit(solution)/shard_map/ppermute | solution.py:45
  100.1 8.0 %collective-permute-start.22 = (bf16[3,48,384]{2,1,0:T(8,128)(2,1)S(1)}, bf16[3,48,384]{2,1,0:T(8,128)(2,1)S(1)}, u32[]{:S(2)}, u32[]{:S(2)}) collective-permute-start(bf16[3,48,384]{2,1,0:T(8,128)(2,1)S(1)} %pad_maximum_fusion.8), channel_id=1, source_target_pairs={{0,32},{1,25},{2,34},{3,27},{4,36},{5,29},{6,38},{7,31},{8,40},{9,... | collective-permute-start | bytes 331784 | tf_op jit(solution)/shard_map/ppermute | solution.py:45
  100.2 8.1 %collective-permute-start.23 = (bf16[3,48,384]{2,1,0:T(8,128)(2,1)S(1)}, bf16[3,48,384]{2,1,0:T(8,128)(2,1)S(1)}, u32[]{:S(2)}, u32[]{:S(2)}) collective-permute-start(bf16[3,48,384]{2,1,0:T(8,128)(2,1)S(1)} %pad_maximum_fusion.9), channel_id=1, source_target_pairs={{0,16},{1,9},{2,18},{3,11},{4,20},{5,13},{6,22},{7,15},{8,24},{9,1... | collective-permute-start | bytes 331784 | tf_op jit(solution)/shard_map/ppermute | solution.py:45
  103.0 6.3 %collective-permute-start.20 = (bf16[3,48,384]{2,1,0:T(8,128)(2,1)S(1)}, bf16[3,48,384]{2,1,0:T(8,128)(2,1)S(1)}, u32[]{:S(2)}, u32[]{:S(2)}) collective-permute-start(bf16[3,48,384]{2,1,0:T(8,128)(2,1)S(1)} %pad_maximum_fusion.6), channel_id=1, source_target_pairs={{0,0},{1,57},{2,2},{3,59},{4,4},{5,61},{6,6},{7,63},{8,8},{9,1},{1... | collective-permute-start | bytes 331784 | tf_op jit(solution)/shard_map/ppermute | solution.py:45
  109.4 6.8 %collective-permute-start.24 = (bf16[4,3,24,384]{3,2,1,0:T(8,128)(2,1)S(1)}, bf16[4,3,24,384]{3,2,1,0:T(8,128)(2,1)S(1)}, u32[]{:S(2)}, u32[]{:S(2)}) collective-permute-start(bf16[4,3,24,384]{3,2,1,0:T(8,128)(2,1)S(1)} %get-tuple-element.49), channel_id=1, source_target_pairs={{0,1},{1,0},{2,3},{3,2},{4,5},{5,4},{6,7},{7,6},{8,9},{9,8},{10,11... | collective-permute-start | bytes 663560 | tf_op jit(solution)/shard_map/ppermute | solution.py:45
  (3 other events, 22.4 us)

commit v2 on v1

--- a/solution.py
+++ b/solution.py
@@ -168,6 +168,37 @@
     return group, live, first, blocks
 
 
+def table_kernel(groups, valid, table):
+    at = position()
+    q_group, q_live, q_first, tops = place_queries(at, groups, valid)
+    for n in range(16):
+        table[n] = q_group[n]
+        table[16 + n] = q_live[n]
+        table[32 + n] = q_first[n]
+    for o in range(2):
+        k_group, k_live, k_first, blocks = place_keys(at, groups, valid, o, tops)
+        for j in range(4):
+            table[48 + 4 * o + j] = k_group[j]
+            for s in range(4):
+                table[56 + 16 * o + 4 * j + s] = k_live[j][s]
+                table[88 + 16 * o + 4 * j + s] = k_first[j][s]
+        for n in range(QROWS // QCHUNK):
+            table[120 + 3 * o + n] = blocks[n]
+    table[126] = 0
+    table[127] = 0
+
+
+def read_queries(table):
+    return tuple([table[first + n] for n in range(16)] for first in (0, 16, 32))
+
+
+def read_keys(table, o):
+    group = [table[48 + 4 * o + j] for j in range(4)]
+    live = [[table[56 + 16 * o + 4 * j + s] for s in range(4)] for j in range(4)]
+    first = [[table[88 + 16 * o + 4 * j + s] for s in range(4)] for j in range(4)]
+    return group, live, first, [table[120 + 3 * o + n] for n in range(QROWS // QCHUNK)]
+
+
 def pick(values, n):
     out = values[-1]
     for i in range(len(values) - 1):
@@ -219,10 +250,9 @@
             kgrp[rows, :] = jnp.where(row_lanes < k_live[j][s], k_group[j], kgrp[rows, :])
 
 
-def stats_kernel(o, groups, valid, *refs):
-    at = position()
-    q_group, q_live, q_first, tops = place_queries(at, groups, valid)
-    k_group, k_live, k_first, blocks = place_keys(at, groups, valid, o, tops)
+def stats_kernel(o, table, *refs):
+    q_group, q_live, q_first = read_queries(table)
+    k_group, k_live, k_first, blocks = read_keys(table, o)
     if o == 0:
         qbuf, qgrp, kbuf, kgrp, stats = refs[6:11]
         load_queries(pieces(*refs[0:3]), qbuf, qgrp, q_group, q_live, q_first)
@@ -285,10 +315,9 @@
     levels[6:8, :] = jnp.zeros_like(levels[6:8, :])
 
 
-def grad_kernel(o, groups, valid, qbuf, qgrp, kbuf, kgrp, *refs):
-    at = position()
-    q_group, q_live, q_first, tops = place_queries(at, groups, valid)
-    k_group, k_live, k_first, blocks = place_keys(at, groups, valid, o, tops)
+def grad_kernel(o, table, qbuf, qgrp, kbuf, kgrp, *refs):
+    q_group, q_live, q_first = read_queries(table)
+    k_group, k_live, k_first, blocks = read_keys(table, o)
     if o == 1:
         dkv, dqt, levels, dks, dvs = refs[4:9]
         combine(refs[0:4], levels)
@@ -381,16 +410,26 @@
     )(query, dout, keys, values)
     take = swap_core(give)
     both = jnp.where(c == 0, jnp.concatenate([keep, take], axis=2), jnp.concatenate([take, keep], axis=2))
+    i32 = jnp.int32
+    slot_group, valid, both = lax.optimization_barrier((slot_group, valid, both))
+    table = pl.pallas_call(
+        table_kernel,
+        out_shape=jax.ShapeDtypeStruct((128,), i32),
+        in_specs=[SMEM] * 2,
+        out_specs=SMEM,
+        compiler_params=SMALL,
+        cost_estimate=pl.CostEstimate(flops=2 * 10**9, bytes_accessed=10**6, transcendentals=0),
+        name="table",
+    )(slot_group, valid)
     got = {j: send(both[j], lambda y, z, x, c: (y, z + c + 2 * j, x, c)) for j in (2, 1, 3, 0)}
     own_qd = jnp.stack([got[j][0:2] for j in range(4)])
     own_kv = jnp.stack([got[j][2:4] for j in range(4)])
 
-    kv_first, qd_first = lax.optimization_barrier((first_x(own_kv), first_y(own_qd)))
+    kv_first, qd_first, table = lax.optimization_barrier((first_x(own_kv), first_y(own_qd), table))
+    tables = (table,)
     kv_rest = second_x(jnp.stack([own_kv, kv_first]))
     qd_rest = second_y(jnp.stack([own_qd, qd_first]))
 
-    i32 = jnp.int32
-    tables = (slot_group, valid)
     kbuf_type = jax.ShapeDtypeStruct((2, KROWS, COLS), bf16)
     kgrp_type = jax.ShapeDtypeStruct((KROWS, HD), i32)
     stats_type = jax.ShapeDtypeStruct((16, QROWS), f32)

time: 118 us -> 117 us (level)
  Pallas kernels: 23.6 us -> 20.9 us
  starting transfers between devices: 39.3 us -> 41.5 us
  waiting for transfers between devices: 50.5 us -> 49 us
    pallas_call x4, Pallas kernels: 20.7 us -> 16 us  [run(): pl.pallas_call(kernel, out_shape=out_shape, in_specs=[SMEM] * len(tables)...]
    ppermute x25, starting transfers between devices: 39.3 us -> 41.5 us  [send(): return lax.ppermute(array, ('tm', 'head'), pairs(move))]
    pallas_call x0 -> x1, Pallas kernels: none -> 2.15 us  [local(): pl.pallas_call(table_kernel, out_shape=jax.ShapeDtypeStruct((128,), i32),...]
    ppermute x25, waiting for transfers between devices: 50.5 us -> 49 us  [send(): return lax.ppermute(array, ('tm', 'head'), pairs(move))]
  transfers between devices with their start and end apart: 25 -> 25, of which waited for: 18 -> 15; matrix products, arithmetic and copies ran while one was open for 0% -> 0% of each run, Pallas kernels for 10% -> 11%
where the time goes in v2:
time: 117 us; the launch traced here: 115 us
  waiting for transfers between devices  49 us (42%)
  starting transfers between devices  41.5 us (35%)
  Pallas kernels  20.9 us (18%)
  other arithmetic  2.28 us (2%)
    ppermute x25, waiting for transfers between devices, send(): return lax.ppermute(array, ('tm', 'head'), pairs(move))  49 us
    ppermute x25, starting transfers between devices, send(): return lax.ppermute(array, ('tm', 'head'), pairs(move))  41.5 us
    pallas_call x4, Pallas kernels, run(): pl.pallas_call(kernel, out_shape=out_shape, in_specs=[SMEM] * len(tables)...  16 us
  transfers between devices with their start and end apart: 25, of which 15 were waited for; matrix products, arithmetic and copies ran while one was open for 0% of the time, Pallas kernels for 11%

profile of v2, /device:TPU:1, one launch (start us, length us, event | category | flops | bytes accessed | tf_op | source)
XLA Modules:
  0.0 115.1 jit_solution(3802718302620977838)
XLA Ops:
  0.6 2.0 %pack.1 = (bf16[4,4,24,384]{3,2,1,0:T(8,128)(2,1)}, bf16[4,4,24,384]{3,2,1,0:T(8,128)(2,1)}) custom-call(bf16[24,3072]{1,0:T(8,128)(2,1)} %query.1, bf16[24,3072]{1,0:T(8,128)(2,1)} %grad.1, bf16[24,3072]{1,0:T(8,128)(2,1)} %keys.1, bf16[24,3072]{1,0:T(8,128)(2,1)} %values.1), custom_call_target="tpu_custom_call" | custom-call | tf_op jit(solution)/shard_map/pack/pallas_call | solution.py:402
  2.7 3.3 %collective-permute-start = (bf16[4,4,24,384]{3,2,1,0:T(8,128)(2,1)}, bf16[4,4,24,384]{3,2,1,0:T(8,128)(2,1)S(1)}, u32[]{:S(2)}, u32[]{:S(2)}) collective-permute-start(bf16[4,4,24,384]{3,2,1,0:T(8,128)(2,1)} %get-tuple-element.29), channel_id=1, source_target_pairs={{0,1},{1,0},{2,3},{3,2},{4,5},{5,4},{6,7},{7,6},{8,9},{9,8},{10,11... | collective-permute-start | bytes 884744 | tf_op jit(solution)/shard_map/ppermute | solution.py:45
  10.6 3.9 %collective-permute-start.4 = (bf16[4,48,384]{2,1,0:T(8,128)(2,1)S(1)}, bf16[4,48,384]{2,1,0:T(8,128)(2,1)S(1)}, u32[]{:S(2)}, u32[]{:S(2)}) collective-permute-start(bf16[4,48,384]{2,1,0:T(8,128)(2,1)S(1)} %get-tuple-element.54), channel_id=1, source_target_pairs={{0,48},{1,57},{2,50},{3,59},{4,52},{5,61},{6,54},{7,63},{8,56},{9,... | collective-permute-start | bytes 442376 | tf_op jit(solution)/shard_map/ppermute | solution.py:45
  14.6 2.3 %collective-permute-start.3 = (bf16[4,48,384]{2,1,0:T(8,128)(2,1)S(1)}, bf16[4,48,384]{2,1,0:T(8,128)(2,1)S(1)}, u32[]{:S(2)}, u32[]{:S(2)}) collective-permute-start(bf16[4,48,384]{2,1,0:T(8,128)(2,1)S(1)} %get-tuple-element.55), channel_id=1, source_target_pairs={{0,32},{1,41},{2,34},{3,43},{4,36},{5,45},{6,38},{7,47},{8,40},{9,... | collective-permute-start | bytes 442376 | tf_op jit(solution)/shard_map/ppermute | solution.py:45
  17.9 5.1 %collective-permute-done.4 = bf16[4,48,384]{2,1,0:T(8,128)(2,1)S(1)} collective-permute-done((bf16[4,48,384]{2,1,0:T(8,128)(2,1)S(1)}, bf16[4,48,384]{2,1,0:T(8,128)(2,1)S(1)}, u32[]{:S(2)}, u32[]{:S(2)}) %collective-permute-start.4) | collective-permute-done | bytes 147488 | tf_op jit(solution)/shard_map/ppermute | solution.py:45
  23.0 4.7 %collective-permute-done.3 = bf16[4,48,384]{2,1,0:T(8,128)(2,1)S(1)} collective-permute-done((bf16[4,48,384]{2,1,0:T(8,128)(2,1)S(1)}, bf16[4,48,384]{2,1,0:T(8,128)(2,1)S(1)}, u32[]{:S(2)}, u32[]{:S(2)}) %collective-permute-start.3) | collective-permute-done | bytes 147488 | tf_op jit(solution)/shard_map/ppermute | solution.py:45
  27.7 2.3 %collective-permute-done.2 = bf16[4,48,384]{2,1,0:T(8,128)(2,1)S(1)} collective-permute-done((bf16[4,48,384]{2,1,0:T(8,128)(2,1)S(1)}, bf16[4,48,384]{2,1,0:T(8,128)(2,1)S(1)}, u32[]{:S(2)}, u32[]{:S(2)}) %collective-permute-start.2) | collective-permute-done | bytes 147488 | tf_op jit(solution)/shard_map/ppermute | solution.py:45
  30.1 2.9 %collective-permute-start.6 = (bf16[4,2,48,384]{3,2,1,0:T(8,128)(2,1)S(1)}, bf16[4,2,48,384]{3,2,1,0:T(8,128)(2,1)S(1)}, u32[]{:S(2)}, u32[]{:S(2)}) collective-permute-start(bf16[4,2,48,384]{3,2,1,0:T(8,128)(2,1)S(1)} %get-tuple-element.66.refs_0_), channel_id=1, source_target_pairs={{0,64},{1,193},{2,66},{3,195},{4,68},{5,197},{6,70},{7,199},{8,72}... | collective-permute-start | bytes 884744 | tf_op jit(solution)/shard_map/ppermute | solution.py:45
  33.0 2.6 %collective-permute-start.5 = (bf16[4,2,48,384]{3,2,1,0:T(8,128)(2,1)S(1)}, bf16[4,2,48,384]{3,2,1,0:T(8,128)(2,1)S(1)}, u32[]{:S(2)}, u32[]{:S(2)}) collective-permute-start(bf16[4,2,48,384]{3,2,1,0:T(8,128)(2,1)S(1)} %get-tuple-element.64.refs_3_), channel_id=1, source_target_pairs={{0,2},{1,7},{2,0},{3,5},{4,6},{5,3},{6,4},{7,1},{8,10},{9,15},{10,... | collective-permute-start | bytes 884744 | tf_op jit(solution)/shard_map/ppermute | solution.py:45
  35.6 2.1 %table.1 = s32[128]{0:T(128)S(1)} custom-call(s32[32]{0:T(128)S(1)} %copy-done, s32[32]{0:T(128)S(1)} %copy-done.1), custom_call_target="tpu_custom_call" | custom-call | flops 2000000000 | bytes 1000000 | tf_op jit(solution)/shard_map/table/pallas_call | solution.py:415
  37.8 2.1 %collective-permute-done.5.refs_4_ = bf16[4,2,48,384]{3,2,1,0:T(8,128)(2,1)S(1)} collective-permute-done((bf16[4,2,48,384]{3,2,1,0:T(8,128)(2,1)S(1)}, bf16[4,2,48,384]{3,2,1,0:T(8,128)(2,1)S(1)}, u32[]{:S(2)}, u32[]{:S(2)}) %collective-permute-start.5) | collective-permute-done | bytes 294944 | tf_op jit(solution)/shard_map/ppermute | solution.py:45
  40.3 8.8 %collective-permute-done.8.refs_5_ = bf16[2,4,2,48,384]{4,3,2,1,0:T(8,128)(2,1)S(1)} collective-permute-done((bf16[2,4,2,48,384]{4,3,2,1,0:T(8,128)(2,1)S(1)}, bf16[2,4,2,48,384]{4,3,2,1,0:T(8,128)(2,1)S(1)}, u32[]{:S(2)}, u32[]{:S(2)}) %collective-permute-start.8) | collective-permute-done | bytes 589856 | tf_op jit(solution)/shard_map/ppermute | solution.py:45
  49.6 4.6 %stats_own.1 = (bf16[2,768,384]{2,1,0:T(8,128)(2,1)S(1)}, s32[8,768]{1,0:T(8,128)S(1)}, bf16[2,768,384]{2,1,0:T(8,128)(2,1)S(1)}, s32[768,128]{1,0:T(8,128)S(1)}, f32[16,768]{1,0:T(8,128)S(1)}) custom-call(s32[128]{0:T(128)S(1)} %table.1, bf16[4,2,48,384]{3,2,1,0:T(8,128)(2,1)S(1)} %get-tuple-element.66.refs_0_, ...), custom_call_target="tpu_custom_call" | custom-call | flops 3000000000 | bytes 6000000 | tf_op jit(solution)/shard_map/stats_own/pallas_call | solution.py:386
  54.3 2.2 %stats_other.1 = (bf16[2,768,384]{2,1,0:T(8,128)(2,1)S(1)}, s32[768,128]{1,0:T(8,128)S(1)}, f32[16,768]{1,0:T(8,128)S(1)}) custom-call(s32[128]{0:T(128)S(1)} %table.1, bf16[2,768,384]{2,1,0:T(8,128)(2,1)S(1)} %get-tuple-element.36.refs_0_.qbuf, s32[8,768]{1,0:T(8,128)S(1)} %get-tuple-element.37.refs_1_.qgrp, f32[16,768]{1,0:T(8,128)S(1)} %get-tuple-element.40.refs_2_, ...), custom_call_target="tpu_custom_call" | custom-call | flops 3000000000 | bytes 6000000 | tf_op jit(solution)/shard_map/stats_other/pallas_call | solution.py:386
  59.6 2.1 %collective-permute-done.13.refs_2_ = f32[16,768]{1,0:T(8,128)S(1)} collective-permute-done((f32[16,768]{1,0:T(8,128)S(1)}, f32[16,768]{1,0:T(8,128)S(1)}, u32[]{:S(2)}, u32[]{:S(2)}) %collective-permute-start.13) | collective-permute-done | bytes 49184 | tf_op jit(solution)/shard_map/ppermute | solution.py:45
  62.2 2.9 %grads_other.1 = (bf16[4,4,2,48,384]{4,3,2,1,0:T(8,128)(2,1)S(1)}, f32[3,128,768]{2,1,0:T(8,128)S(1)}, f32[8,768]{1,0:T(8,128)S(1)}) custom-call(s32[128]{0:T(128)S(1)} %table.1, bf16[2,768,384]{2,1,0:T(8,128)(2,1)S(1)} %get-tuple-element.36.refs_0_.qbuf, s32[8,768]{1,0:T(8,128)S(1)} %get-tuple-element.37.refs_1_.qgrp, ...), custom_call_target="tpu_custom_call" | custom-call | flops 3000000000 | bytes 6000000 | tf_op jit(solution)/shard_map/grads_other/pallas_call | solution.py:386
  65.1 5.9 %collective-permute-start.15 = (bf16[4,4,2,48,384]{4,3,2,1,0:T(8,128)(2,1)S(1)}, bf16[4,4,2,48,384]{4,3,2,1,0:T(8,128)(2,1)S(1)}, u32[]{:S(2)}, u32[]{:S(2)}) collective-permute-start(bf16[4,4,2,48,384]{4,3,2,1,0:T(8,128)(2,1)S(1)} %get-tuple-element.48), channel_id=1, source_target_pairs={{0,1},{1,0},{2,3},{3,2},{4,5},{5,4},{6,7},{7,6},{8,9},{9,8},{10,11... | collective-permute-start | bytes 3538952 | tf_op jit(solution)/shard_map/ppermute | solution.py:45
  71.0 6.2 %grads_own.1 = (bf16[4,4,2,48,384]{4,3,2,1,0:T(8,128)(2,1)S(1)}, bf16[4,4,48,384]{3,2,1,0:T(8,128)(2,1)S(1)}) custom-call(s32[128]{0:T(128)S(1)} %table.1, bf16[2,768,384]{2,1,0:T(8,128)(2,1)S(1)} %get-tuple-element.36.refs_0_.qbuf, s32[8,768]{1,0:T(8,128)S(1)} %get-tuple-element.37.refs_1_.qgrp, bf16[2,768,384]{2,1,0:T(8,128)(2,1)S(1)} %get-tuple-element.38.kbuf, ...), custom_call_target="tpu_custom_call" | custom-call | flops 3000000000 | bytes 6000000 | tf_op jit(solution)/shard_map/grads_own/pallas_call | solution.py:386
  78.9 5.9 %collective-permute-done.17 = bf16[2,4,48,384]{3,2,1,0:T(8,128)(2,1)S(1)} collective-permute-done((bf16[2,4,48,384]{3,2,1,0:T(8,128)(2,1)S(1)}, bf16[2,4,48,384]{3,2,1,0:T(8,128)(2,1)S(1)}, u32[]{:S(2)}, u32[]{:S(2)}) %collective-permute-start.17) | collective-permute-done | bytes 294944 | tf_op jit(solution)/shard_map/ppermute | solution.py:45
  86.9 5.2 %collective-permute-done.19 = bf16[4,48,384]{2,1,0:T(8,128)(2,1)S(1)} collective-permute-done((bf16[4,48,384]{2,1,0:T(8,128)(2,1)S(1)}, bf16[4,48,384]{2,1,0:T(8,128)(2,1)S(1)}, u32[]{:S(2)}, u32[]{:S(2)}) %collective-permute-start.19) | collective-permute-done | bytes 147488 | tf_op jit(solution)/shard_map/ppermute | solution.py:45
  94.2 2.9 %collective-permute-start.22 = (bf16[3,48,384]{2,1,0:T(8,128)(2,1)S(1)}, bf16[3,48,384]{2,1,0:T(8,128)(2,1)S(1)}, u32[]{:S(2)}, u32[]{:S(2)}) collective-permute-start(bf16[3,48,384]{2,1,0:T(8,128)(2,1)S(1)} %pad_maximum_fusion.8), channel_id=1, source_target_pairs={{0,32},{1,25},{2,34},{3,27},{4,36},{5,29},{6,38},{7,31},{8,40},{9,... | collective-permute-start | bytes 331784 | tf_op jit(solution)/shard_map/ppermute | solution.py:45
  97.2 3.2 %collective-permute-start.23 = (bf16[3,48,384]{2,1,0:T(8,128)(2,1)S(1)}, bf16[3,48,384]{2,1,0:T(8,128)(2,1)S(1)}, u32[]{:S(2)}, u32[]{:S(2)}) collective-permute-start(bf16[3,48,384]{2,1,0:T(8,128)(2,1)S(1)} %pad_maximum_fusion.9), channel_id=1, source_target_pairs={{0,16},{1,9},{2,18},{3,11},{4,20},{5,13},{6,22},{7,15},{8,24},{9,1... | collective-permute-start | bytes 331784 | tf_op jit(solution)/shard_map/ppermute | solution.py:45
  102.4 5.2 %collective-permute-done.23 = bf16[3,48,384]{2,1,0:T(8,128)(2,1)S(1)} collective-permute-done((bf16[3,48,384]{2,1,0:T(8,128)(2,1)S(1)}, bf16[3,48,384]{2,1,0:T(8,128)(2,1)S(1)}, u32[]{:S(2)}, u32[]{:S(2)}) %collective-permute-start.23) | collective-permute-done | bytes 110624 | tf_op jit(solution)/shard_map/ppermute | solution.py:45
  107.7 5.5 %collective-permute-start.24 = (bf16[4,3,24,384]{3,2,1,0:T(8,128)(2,1)S(1)}, bf16[4,3,24,384]{3,2,1,0:T(8,128)(2,1)S(1)}, u32[]{:S(2)}, u32[]{:S(2)}) collective-permute-start(bf16[4,3,24,384]{3,2,1,0:T(8,128)(2,1)S(1)} %get-tuple-element.57), channel_id=1, source_target_pairs={{0,1},{1,0},{2,3},{3,2},{4,5},{5,4},{6,7},{7,6},{8,9},{9,8},{10,11... | collective-permute-start | bytes 663560 | tf_op jit(solution)/shard_map/ppermute | solution.py:45
  (67 shorter events, 20.1 us)
Async XLA Ops:
  2.7 4.7 %collective-permute-start = (bf16[4,4,24,384]{3,2,1,0:T(8,128)(2,1)}, bf16[4,4,24,384]{3,2,1,0:T(8,128)(2,1)S(1)}, u32[]{:S(2)}, u32[]{:S(2)}) collective-permute-start(bf16[4,4,24,384]{3,2,1,0:T(8,128)(2,1)} %get-tuple-element.29), channel_id=1, source_target_pairs={{0,1},{1,0},{2,3},{3,2},{4,5},{5,4},{6,7},{7,6},{8,9},{9,8},{10,11... | collective-permute-start | bytes 884744 | tf_op jit(solution)/shard_map/ppermute | solution.py:45
  8.7 9.1 %collective-permute-start.1 = (bf16[4,48,384]{2,1,0:T(8,128)(2,1)S(1)}, bf16[4,48,384]{2,1,0:T(8,128)(2,1)S(1)}, u32[]{:S(2)}, u32[]{:S(2)}) collective-permute-start(bf16[4,48,384]{2,1,0:T(8,128)(2,1)S(1)} %get-tuple-element.53), channel_id=1, source_target_pairs={{0,0},{1,9},{2,2},{3,11},{4,4},{5,13},{6,6},{7,15},{8,8},{9,17},{1... | collective-permute-start | bytes 442376 | tf_op jit(solution)/shard_map/ppermute | solution.py:45
  10.6 12.3 %collective-permute-start.4 = (bf16[4,48,384]{2,1,0:T(8,128)(2,1)S(1)}, bf16[4,48,384]{2,1,0:T(8,128)(2,1)S(1)}, u32[]{:S(2)}, u32[]{:S(2)}) collective-permute-start(bf16[4,48,384]{2,1,0:T(8,128)(2,1)S(1)} %get-tuple-element.54), channel_id=1, source_target_pairs={{0,48},{1,57},{2,50},{3,59},{4,52},{5,61},{6,54},{7,63},{8,56},{9,... | collective-permute-start | bytes 442376 | tf_op jit(solution)/shard_map/ppermute | solution.py:45
  14.6 13.1 %collective-permute-start.3 = (bf16[4,48,384]{2,1,0:T(8,128)(2,1)S(1)}, bf16[4,48,384]{2,1,0:T(8,128)(2,1)S(1)}, u32[]{:S(2)}, u32[]{:S(2)}) collective-permute-start(bf16[4,48,384]{2,1,0:T(8,128)(2,1)S(1)} %get-tuple-element.55), channel_id=1, source_target_pairs={{0,32},{1,41},{2,34},{3,43},{4,36},{5,45},{6,38},{7,47},{8,40},{9,... | collective-permute-start | bytes 442376 | tf_op jit(solution)/shard_map/ppermute | solution.py:45
  16.9 13.1 %collective-permute-start.2 = (bf16[4,48,384]{2,1,0:T(8,128)(2,1)S(1)}, bf16[4,48,384]{2,1,0:T(8,128)(2,1)S(1)}, u32[]{:S(2)}, u32[]{:S(2)}) collective-permute-start(bf16[4,48,384]{2,1,0:T(8,128)(2,1)S(1)} %get-tuple-element.56), channel_id=1, source_target_pairs={{0,16},{1,25},{2,18},{3,27},{4,20},{5,29},{6,22},{7,31},{8,24},{9,... | collective-permute-start | bytes 442376 | tf_op jit(solution)/shard_map/ppermute | solution.py:45
  30.1 7.7 %collective-permute-start.6 = (bf16[4,2,48,384]{3,2,1,0:T(8,128)(2,1)S(1)}, bf16[4,2,48,384]{3,2,1,0:T(8,128)(2,1)S(1)}, u32[]{:S(2)}, u32[]{:S(2)}) collective-permute-start(bf16[4,2,48,384]{3,2,1,0:T(8,128)(2,1)S(1)} %get-tuple-element.66.refs_0_), channel_id=1, source_target_pairs={{0,64},{1,193},{2,66},{3,195},{4,68},{5,197},{6,70},{7,199},{8,72}... | collective-permute-start | bytes 884744 | tf_op jit(solution)/shard_map/ppermute | solution.py:45
  33.0 6.9 %collective-permute-start.5 = (bf16[4,2,48,384]{3,2,1,0:T(8,128)(2,1)S(1)}, bf16[4,2,48,384]{3,2,1,0:T(8,128)(2,1)S(1)}, u32[]{:S(2)}, u32[]{:S(2)}) collective-permute-start(bf16[4,2,48,384]{3,2,1,0:T(8,128)(2,1)S(1)} %get-tuple-element.64.refs_3_), channel_id=1, source_target_pairs={{0,2},{1,7},{2,0},{3,5},{4,6},{5,3},{6,4},{7,1},{8,10},{9,15},{10,... | collective-permute-start | bytes 884744 | tf_op jit(solution)/shard_map/ppermute | solution.py:45
  40.0 9.1 %collective-permute-start.8 = (bf16[2,4,2,48,384]{4,3,2,1,0:T(8,128)(2,1)S(1)}, bf16[2,4,2,48,384]{4,3,2,1,0:T(8,128)(2,1)S(1)}, u32[]{:S(2)}, u32[]{:S(2)}) collective-permute-start(bf16[2,4,2,48,384]{4,3,2,1,0:T(8,128)(2,1)S(1)} %pad_maximum_fusion.1), channel_id=1, source_target_pairs={{0,6},{1,3},{2,4},{3,1},{4,2},{5,7},{6,0},{7,5},{8,14},{9,11},{10,... | collective-permute-start | bytes 1769480 | tf_op jit(solution)/shard_map/ppermute | solution.py:45
  40.2 9.5 %collective-permute-start.7 = (bf16[2,4,2,48,384]{4,3,2,1,0:T(8,128)(2,1)S(1)}, bf16[2,4,2,48,384]{4,3,2,1,0:T(8,128)(2,1)S(1)}, u32[]{:S(2)}, u32[]{:S(2)}) collective-permute-start(bf16[2,4,2,48,384]{4,3,2,1,0:T(8,128)(2,1)S(1)} %pad_maximum_fusion), channel_id=1, source_target_pairs={{0,192},{1,65},{2,194},{3,67},{4,196},{5,69},{6,198},{7,71},{8,200... | collective-permute-start | bytes 1769480 | tf_op jit(solution)/shard_map/ppermute | solution.py:45
  49.1 5.2 %collective-permute-start.11 = (bf16[2,4,2,48,384]{4,3,2,1,0:T(8,128)(2,1)S(1)}, bf16[2,4,2,48,384]{4,3,2,1,0:T(8,128)(2,1)S(1)}, u32[]{:S(2)}, u32[]{:S(2)}) collective-permute-start(bf16[2,4,2,48,384]{4,3,2,1,0:T(8,128)(2,1)S(1)} %collective-permute-done.8.refs_5_), channel_id=1, source_target_pairs={{0,1},{1,0},{2,3},{3,2},{4,5},{5,4},{6,7},{7,6},{8,9},{9,8},{10,11... | collective-permute-start | bytes 1769480 | tf_op jit(solution)/shard_map/ppermute | solution.py:45
  49.1 5.2 %collective-permute-start.9 = (bf16[4,2,48,384]{3,2,1,0:T(8,128)(2,1)S(1)}, bf16[4,2,48,384]{3,2,1,0:T(8,128)(2,1)S(1)}, u32[]{:S(2)}, u32[]{:S(2)}) collective-permute-start(bf16[4,2,48,384]{3,2,1,0:T(8,128)(2,1)S(1)} %get-tuple-element.64.refs_3_), channel_id=1, source_target_pairs={{0,1},{1,0},{2,3},{3,2},{4,5},{5,4},{6,7},{7,6},{8,9},{9,8},{10,11... | collective-permute-start | bytes 884744 | tf_op jit(solution)/shard_map/ppermute | solution.py:45
  49.6 4.7 %collective-permute-start.10 = (bf16[4,2,48,384]{3,2,1,0:T(8,128)(2,1)S(1)}, bf16[4,2,48,384]{3,2,1,0:T(8,128)(2,1)S(1)}, u32[]{:S(2)}, u32[]{:S(2)}) collective-permute-start(bf16[4,2,48,384]{3,2,1,0:T(8,128)(2,1)S(1)} %collective-permute-done.5.refs_4_), channel_id=1, source_target_pairs={{0,1},{1,0},{2,3},{3,2},{4,5},{5,4},{6,7},{7,6},{8,9},{9,8},{10,11... | collective-permute-start | bytes 884744 | tf_op jit(solution)/shard_map/ppermute | solution.py:45
  57.2 4.5 %collective-permute-start.13 = (f32[16,768]{1,0:T(8,128)S(1)}, f32[16,768]{1,0:T(8,128)S(1)}, u32[]{:S(2)}, u32[]{:S(2)}) collective-permute-start(f32[16,768]{1,0:T(8,128)S(1)} %get-tuple-element.43.refs_0_), channel_id=1, source_target_pairs={{0,128},{1,129},{2,130},{3,131},{4,132},{5,133},{6,134},{7,135},{8... | collective-permute-start | bytes 147464 | tf_op jit(solution)/shard_map/ppermute | solution.py:45
  57.4 4.8 %collective-permute-start.12 = (f32[16,768]{1,0:T(8,128)S(1)}, f32[16,768]{1,0:T(8,128)S(1)}, u32[]{:S(2)}, u32[]{:S(2)}) collective-permute-start(f32[16,768]{1,0:T(8,128)S(1)} %get-tuple-element.43.refs_0_), channel_id=1, source_target_pairs={{0,64},{1,65},{2,66},{3,67},{4,68},{5,69},{6,70},{7,71},{8,72},{9,... | collective-permute-start | bytes 147464 | tf_op jit(solution)/shard_map/ppermute | solution.py:45
  65.1 12.1 %collective-permute-start.15 = (bf16[4,4,2,48,384]{4,3,2,1,0:T(8,128)(2,1)S(1)}, bf16[4,4,2,48,384]{4,3,2,1,0:T(8,128)(2,1)S(1)}, u32[]{:S(2)}, u32[]{:S(2)}) collective-permute-start(bf16[4,4,2,48,384]{4,3,2,1,0:T(8,128)(2,1)S(1)} %get-tuple-element.48), channel_id=1, source_target_pairs={{0,1},{1,0},{2,3},{3,2},{4,5},{5,4},{6,7},{7,6},{8,9},{9,8},{10,11... | collective-permute-start | bytes 3538952 | tf_op jit(solution)/shard_map/ppermute | solution.py:45
  77.6 8.8 %collective-permute-start.16 = (bf16[2,4,2,48,384]{4,3,2,1,0:T(8,128)(2,1)S(1)}, bf16[2,4,2,48,384]{4,3,2,1,0:T(8,128)(2,1)S(1)}, u32[]{:S(2)}, u32[]{:S(2)}) collective-permute-start(bf16[2,4,2,48,384]{4,3,2,1,0:T(8,128)(2,1)S(1)} %slice.220), channel_id=1, source_target_pairs={{0,6},{1,3},{2,4},{3,1},{4,2},{5,7},{6,0},{7,5},{8,14},{9,11},{10,... | collective-permute-start | bytes 1769480 | tf_op jit(solution)/shard_map/ppermute | solution.py:45
  78.5 6.2 %collective-permute-start.17 = (bf16[2,4,48,384]{3,2,1,0:T(8,128)(2,1)S(1)}, bf16[2,4,48,384]{3,2,1,0:T(8,128)(2,1)S(1)}, u32[]{:S(2)}, u32[]{:S(2)}) collective-permute-start(bf16[2,4,48,384]{3,2,1,0:T(8,128)(2,1)S(1)} %slice.125), channel_id=1, source_target_pairs={{0,192},{1,65},{2,194},{3,67},{4,196},{5,69},{6,198},{7,71},{8,200... | collective-permute-start | bytes 884744 | tf_op jit(solution)/shard_map/ppermute | solution.py:45
  86.7 6.9 %collective-permute-start.18 = (bf16[4,2,48,384]{3,2,1,0:T(8,128)(2,1)S(1)}, bf16[4,2,48,384]{3,2,1,0:T(8,128)(2,1)S(1)}, u32[]{:S(2)}, u32[]{:S(2)}) collective-permute-start(bf16[4,2,48,384]{3,2,1,0:T(8,128)(2,1)S(1)} %fusion.2), channel_id=1, source_target_pairs={{0,2},{1,7},{2,0},{3,5},{4,6},{5,3},{6,4},{7,1},{8,10},{9,15},{10,... | collective-permute-start | bytes 884744 | tf_op jit(solution)/shard_map/ppermute | solution.py:45
  86.8 5.3 %collective-permute-start.19 = (bf16[4,48,384]{2,1,0:T(8,128)(2,1)S(1)}, bf16[4,48,384]{2,1,0:T(8,128)(2,1)S(1)}, u32[]{:S(2)}, u32[]{:S(2)}) collective-permute-start(bf16[4,48,384]{2,1,0:T(8,128)(2,1)S(1)} %fusion.5), channel_id=1, source_target_pairs={{0,64},{1,193},{2,66},{3,195},{4,68},{5,197},{6,70},{7,199},{8,72}... | collective-permute-start | bytes 442376 | tf_op jit(solution)/shard_map/ppermute | solution.py:45
  93.7 8.6 %collective-permute-start.21 = (bf16[3,48,384]{2,1,0:T(8,128)(2,1)S(1)}, bf16[3,48,384]{2,1,0:T(8,128)(2,1)S(1)}, u32[]{:S(2)}, u32[]{:S(2)}) collective-permute-start(bf16[3,48,384]{2,1,0:T(8,128)(2,1)S(1)} %pad_maximum_fusion.7), channel_id=1, source_target_pairs={{0,48},{1,41},{2,50},{3,43},{4,52},{5,45},{6,54},{7,47},{8,56},{9,... | collective-permute-start | bytes 331784 | tf_op jit(solution)/shard_map/ppermute | solution.py:45
  94.2 8.2 %collective-permute-start.22 = (bf16[3,48,384]{2,1,0:T(8,128)(2,1)S(1)}, bf16[3,48,384]{2,1,0:T(8,128)(2,1)S(1)}, u32[]{:S(2)}, u32[]{:S(2)}) collective-permute-start(bf16[3,48,384]{2,1,0:T(8,128)(2,1)S(1)} %pad_maximum_fusion.8), channel_id=1, source_target_pairs={{0,32},{1,25},{2,34},{3,27},{4,36},{5,29},{6,38},{7,31},{8,40},{9,... | collective-permute-start | bytes 331784 | tf_op jit(solution)/shard_map/ppermute | solution.py:45
  97.2 10.4 %collective-permute-start.23 = (bf16[3,48,384]{2,1,0:T(8,128)(2,1)S(1)}, bf16[3,48,384]{2,1,0:T(8,128)(2,1)S(1)}, u32[]{:S(2)}, u32[]{:S(2)}) collective-permute-start(bf16[3,48,384]{2,1,0:T(8,128)(2,1)S(1)} %pad_maximum_fusion.9), channel_id=1, source_target_pairs={{0,16},{1,9},{2,18},{3,11},{4,20},{5,13},{6,22},{7,15},{8,24},{9,1... | collective-permute-start | bytes 331784 | tf_op jit(solution)/shard_map/ppermute | solution.py:45
  100.4 7.2 %collective-permute-start.20 = (bf16[3,48,384]{2,1,0:T(8,128)(2,1)S(1)}, bf16[3,48,384]{2,1,0:T(8,128)(2,1)S(1)}, u32[]{:S(2)}, u32[]{:S(2)}) collective-permute-start(bf16[3,48,384]{2,1,0:T(8,128)(2,1)S(1)} %pad_maximum_fusion.6), channel_id=1, source_target_pairs={{0,0},{1,57},{2,2},{3,59},{4,4},{5,61},{6,6},{7,63},{8,8},{9,1},{1... | collective-permute-start | bytes 331784 | tf_op jit(solution)/shard_map/ppermute | solution.py:45
  107.7 6.6 %collective-permute-start.24 = (bf16[4,3,24,384]{3,2,1,0:T(8,128)(2,1)S(1)}, bf16[4,3,24,384]{3,2,1,0:T(8,128)(2,1)S(1)}, u32[]{:S(2)}, u32[]{:S(2)}) collective-permute-start(bf16[4,3,24,384]{3,2,1,0:T(8,128)(2,1)S(1)} %get-tuple-element.57), channel_id=1, source_target_pairs={{0,1},{1,0},{2,3},{3,2},{4,5},{5,4},{6,7},{7,6},{8,9},{9,8},{10,11... | collective-permute-start | bytes 663560 | tf_op jit(solution)/shard_map/ppermute | solution.py:45
  (3 other events, 28.3 us)

commit v3 on v2

--- a/solution.py
+++ b/solution.py
@@ -21,6 +21,8 @@
 SCALE = 1.0 / math.sqrt(HD)
 LOG2E = 1.4426950408889634
 QCHUNK = 256
+LANE_BLOCKS = QROWS // HD
+LEVEL_ROWS = 24
 KROWS = 768
 KCHUNK = 512
 
@@ -120,8 +122,13 @@
     return send(array, lambda y, z, x, c: (y, z, x ^ (3 - 2 * c), c))
 
 
-def pieces(own, first, rest):
-    return (own, first, rest.at[0], rest.at[1])
+def pieces(pair, rest):
+    return (pair.at[0], pair.at[1], rest.at[0], rest.at[1])
+
+
+def lanes(ref, first, n):
+    blocks = QCHUNK // HD
+    return jnp.concatenate([ref[pl.ds(first + blocks * n + i, 1), :] for i in range(blocks)], axis=1)
 
 
 def clip_rows(count):
@@ -254,12 +261,12 @@
     q_group, q_live, q_first = read_queries(table)
     k_group, k_live, k_first, blocks = read_keys(table, o)
     if o == 0:
-        qbuf, qgrp, kbuf, kgrp, stats = refs[6:11]
-        load_queries(pieces(*refs[0:3]), qbuf, qgrp, q_group, q_live, q_first)
+        qbuf, qgrp, kbuf, kgrp, stats = refs[4:9]
+        load_queries(pieces(*refs[0:2]), qbuf, qgrp, q_group, q_live, q_first)
     else:
         qbuf, qgrp, before = refs[0:3]
-        kbuf, kgrp, stats = refs[6:9]
-    load_keys(pieces(*refs[3:6]), kbuf, kgrp, k_group, k_live, k_first)
+        kbuf, kgrp, stats = refs[5:8]
+    load_keys(pieces(*refs[2 + o : 4 + o]), kbuf, kgrp, k_group, k_live, k_first)
     stats[...] = jnp.zeros_like(stats)
     def chunk(n, _):
         rows = pl.ds(pl.multiple_of(n * QCHUNK, QCHUNK), QCHUNK)
@@ -291,12 +298,14 @@
             start = (start,) * HEADS
         else:
             start = tuple(
-                tuple(before[3 * k + h : 3 * k + h + 1, rows] for k in range(3)) for h in range(HEADS)
+                tuple(lanes(before, (3 * k + h) * LANE_BLOCKS, n) for k in range(3)) for h in range(HEADS)
             )
         final = visit(pick(blocks, n), step, start)
         for h in range(HEADS):
             for k in range(3):
-                stats[3 * k + h : 3 * k + h + 1, rows] = final[h][k]
+                for i in range(QCHUNK // HD):
+                    place = pl.ds((3 * k + h) * LANE_BLOCKS + n * (QCHUNK // HD) + i, 1)
+                    stats[place, :] = final[h][k][:, i * HD : (i + 1) * HD]
         return 0
 
     lax.fori_loop(0, QROWS // QCHUNK, chunk, 0)
@@ -304,15 +313,16 @@
 
 def combine(parts, levels):
     sts = [st[...] for st in parts]
-    top = functools.reduce(jnp.maximum, [st[0:3, :] for st in sts])
-    factors = [jnp.exp2(st[0:3, :] - top) for st in sts]
-    total = sum(f * st[3:6, :] for f, st in zip(factors, sts))
-    weighted = sum(f * st[6:9, :] for f, st in zip(factors, sts))
+    size = HEADS * LANE_BLOCKS
+    top = functools.reduce(jnp.maximum, [st[0:size] for st in sts])
+    factors = [jnp.exp2(st[0:size] - top) for st in sts]
+    total = sum(f * st[size : 2 * size] for f, st in zip(factors, sts))
+    weighted = sum(f * st[2 * size : 3 * size] for f, st in zip(factors, sts))
     some = total > 0.0
     safe = jnp.where(some, total, 1.0)
-    levels[0:3, :] = jnp.where(some, top + jnp.log2(safe), 0.0)
-    levels[3:6, :] = weighted / safe
-    levels[6:8, :] = jnp.zeros_like(levels[6:8, :])
+    levels[...] = jnp.zeros_like(levels)
+    levels[0:size, :] = jnp.where(some, top + jnp.log2(safe), 0.0)
+    levels[LEVEL_ROWS : LEVEL_ROWS + size, :] = weighted / safe
 
 
 def grad_kernel(o, table, qbuf, qgrp, kbuf, kgrp, *refs):
@@ -343,8 +353,8 @@
             for h in range(HEADS):
                 scores, dprobs = products[h]
                 scores = jnp.where(ok, scores * (SCALE * LOG2E), NEG)
-                probs = jnp.exp2(scores - levels[h : h + 1, rows])
-                dscores = probs * (dprobs - levels[3 + h : 4 + h, rows])
+                probs = jnp.exp2(scores - lanes(levels, h * LANE_BLOCKS, n))
+                dscores = probs * (dprobs - lanes(levels, LEVEL_ROWS + h * LANE_BLOCKS, n))
                 weights.append((probs.astype(jnp.bfloat16), dscores.astype(jnp.bfloat16)))
             for h in range(HEADS):
                 cols = slice(h * HD, (h + 1) * HD)
@@ -427,26 +437,28 @@
 
     kv_first, qd_first, table = lax.optimization_barrier((first_x(own_kv), first_y(own_qd), table))
     tables = (table,)
-    kv_rest = second_x(jnp.stack([own_kv, kv_first]))
-    qd_rest = second_y(jnp.stack([own_qd, qd_first]))
+    kv_pair = jnp.stack([own_kv, kv_first])
+    qd_pair = jnp.stack([own_qd, qd_first])
+    kv_rest = second_x(kv_pair)
+    qd_rest = second_y(qd_pair)
 
     kbuf_type = jax.ShapeDtypeStruct((2, KROWS, COLS), bf16)
     kgrp_type = jax.ShapeDtypeStruct((KROWS, HD), i32)
-    stats_type = jax.ShapeDtypeStruct((16, QROWS), f32)
+    stats_type = jax.ShapeDtypeStruct((56, HD), f32)
     qbuf, qgrp, kbuf, kgrp, part = run(
         functools.partial(stats_kernel, 0),
         "stats_own",
         (jax.ShapeDtypeStruct((2, QROWS, COLS), bf16), jax.ShapeDtypeStruct((8, QROWS), i32))
         + (kbuf_type, kgrp_type, stats_type),
         tables,
-        (own_qd, qd_first, qd_rest, own_kv, kv_first, kv_rest),
+        (qd_pair, qd_rest, kv_pair, kv_rest),
     )
     kbuf_other, kgrp_other, stats = run(
         functools.partial(stats_kernel, 1),
         "stats_other",
         (kbuf_type, kgrp_type, stats_type),
         tables,
-        (qbuf, qgrp, part, swap_core(own_kv), swap_core(kv_first), swap_core(kv_rest)),
+        (qbuf, qgrp, part, swap_core(kv_pair), swap_core(kv_rest)),
     )
 
     all_stats = [stats] + [send(stats, lambda y, z, x, c: (y + n, z, x, c)) for n in (1, 2, 3)]
@@ -463,7 +475,7 @@
         (
             dkv_type,
             jax.ShapeDtypeStruct((HEADS, HD, QROWS), f32),
-            jax.ShapeDtypeStruct((8, QROWS), f32),
+            jax.ShapeDtypeStruct((2 * LEVEL_ROWS, HD), f32),
         ),
         tables,
         (qbuf, qgrp, kbuf_other, kgrp_other, *all_stats),

time: 117 us -> 115 us (0.983); the launches traced: 115 us -> 116 us
    ppermute x25 -> x24, starting transfers between devices: 41.5 us -> 40.9 us  [send(): return lax.ppermute(array, ('tm', 'head'), pairs(move))]
    ppermute x25 -> x24, waiting for transfers between devices: 49 us -> 49.5 us  [send(): return lax.ppermute(array, ('tm', 'head'), pairs(move))]
  transfers between devices with their start and end apart: 25 -> 24, of which waited for: 15 -> 16; matrix products, arithmetic and copies ran while one was open for 0% -> 0% of each run, Pallas kernels for 11% -> 10%
where the time goes in v3:
time: 115 us; the launch traced here: 116 us
  waiting for transfers between devices  49.5 us (43%)
  starting transfers between devices  40.9 us (36%)
  Pallas kernels  21.7 us (19%)
  other arithmetic  2.3 us (2%)
    ppermute x24, waiting for transfers between devices, send(): return lax.ppermute(array, ('tm', 'head'), pairs(move))  49.5 us
    ppermute x24, starting transfers between devices, send(): return lax.ppermute(array, ('tm', 'head'), pairs(move))  40.9 us
    pallas_call x4, Pallas kernels, run(): pl.pallas_call(kernel, out_shape=out_shape, in_specs=[SMEM] * len(tables)...  16.7 us
  transfers between devices with their start and end apart: 24, of which 16 were waited for; matrix products, arithmetic and copies ran while one was open for 0% of the time, Pallas kernels for 10%

profile of v3, /device:TPU:1, one launch (start us, length us, event | category | flops | bytes accessed | tf_op | source)
XLA Modules:
  0.0 115.8 jit_solution(5180482338584034233)
XLA Ops:
  0.6 2.0 %pack.1 = (bf16[4,4,24,384]{3,2,1,0:T(8,128)(2,1)}, bf16[4,4,24,384]{3,2,1,0:T(8,128)(2,1)}) custom-call(bf16[24,3072]{1,0:T(8,128)(2,1)} %query.1, bf16[24,3072]{1,0:T(8,128)(2,1)} %grad.1, bf16[24,3072]{1,0:T(8,128)(2,1)} %keys.1, bf16[24,3072]{1,0:T(8,128)(2,1)} %values.1), custom_call_target="tpu_custom_call" | custom-call | tf_op jit(solution)/shard_map/pack/pallas_call | solution.py:412
  2.7 3.3 %collective-permute-start = (bf16[4,4,24,384]{3,2,1,0:T(8,128)(2,1)}, bf16[4,4,24,384]{3,2,1,0:T(8,128)(2,1)S(1)}, u32[]{:S(2)}, u32[]{:S(2)}) collective-permute-start(bf16[4,4,24,384]{3,2,1,0:T(8,128)(2,1)} %get-tuple-element.29), channel_id=1, source_target_pairs={{0,1},{1,0},{2,3},{3,2},{4,5},{5,4},{6,7},{7,6},{8,9},{9,8},{10,11... | collective-permute-start | bytes 884744 | tf_op jit(solution)/shard_map/ppermute | solution.py:47
  10.7 3.9 %collective-permute-start.4 = (bf16[4,48,384]{2,1,0:T(8,128)(2,1)S(1)}, bf16[4,48,384]{2,1,0:T(8,128)(2,1)S(1)}, u32[]{:S(2)}, u32[]{:S(2)}) collective-permute-start(bf16[4,48,384]{2,1,0:T(8,128)(2,1)S(1)} %get-tuple-element.54), channel_id=1, source_target_pairs={{0,48},{1,57},{2,50},{3,59},{4,52},{5,61},{6,54},{7,63},{8,56},{9,... | collective-permute-start | bytes 442376 | tf_op jit(solution)/shard_map/ppermute | solution.py:47
  14.6 2.3 %collective-permute-start.3 = (bf16[4,48,384]{2,1,0:T(8,128)(2,1)S(1)}, bf16[4,48,384]{2,1,0:T(8,128)(2,1)S(1)}, u32[]{:S(2)}, u32[]{:S(2)}) collective-permute-start(bf16[4,48,384]{2,1,0:T(8,128)(2,1)S(1)} %get-tuple-element.55), channel_id=1, source_target_pairs={{0,32},{1,41},{2,34},{3,43},{4,36},{5,45},{6,38},{7,47},{8,40},{9,... | collective-permute-start | bytes 442376 | tf_op jit(solution)/shard_map/ppermute | solution.py:47
  17.9 5.1 %collective-permute-done.4 = bf16[4,48,384]{2,1,0:T(8,128)(2,1)S(1)} collective-permute-done((bf16[4,48,384]{2,1,0:T(8,128)(2,1)S(1)}, bf16[4,48,384]{2,1,0:T(8,128)(2,1)S(1)}, u32[]{:S(2)}, u32[]{:S(2)}) %collective-permute-start.4) | collective-permute-done | bytes 147488 | tf_op jit(solution)/shard_map/ppermute | solution.py:47
  23.0 4.7 %collective-permute-done.3 = bf16[4,48,384]{2,1,0:T(8,128)(2,1)S(1)} collective-permute-done((bf16[4,48,384]{2,1,0:T(8,128)(2,1)S(1)}, bf16[4,48,384]{2,1,0:T(8,128)(2,1)S(1)}, u32[]{:S(2)}, u32[]{:S(2)}) %collective-permute-start.3) | collective-permute-done | bytes 147488 | tf_op jit(solution)/shard_map/ppermute | solution.py:47
  27.7 2.3 %collective-permute-done.2 = bf16[4,48,384]{2,1,0:T(8,128)(2,1)S(1)} collective-permute-done((bf16[4,48,384]{2,1,0:T(8,128)(2,1)S(1)}, bf16[4,48,384]{2,1,0:T(8,128)(2,1)S(1)}, u32[]{:S(2)}, u32[]{:S(2)}) %collective-permute-start.2) | collective-permute-done | bytes 147488 | tf_op jit(solution)/shard_map/ppermute | solution.py:47
  30.1 2.9 %collective-permute-start.6 = (bf16[4,2,48,384]{3,2,1,0:T(8,128)(2,1)S(1)}, bf16[4,2,48,384]{3,2,1,0:T(8,128)(2,1)S(1)}, u32[]{:S(2)}, u32[]{:S(2)}) collective-permute-start(bf16[4,2,48,384]{3,2,1,0:T(8,128)(2,1)S(1)} %get-tuple-element.66), channel_id=1, source_target_pairs={{0,64},{1,193},{2,66},{3,195},{4,68},{5,197},{6,70},{7,199},{8,72}... | collective-permute-start | bytes 884744 | tf_op jit(solution)/shard_map/ppermute | solution.py:47
  33.1 2.6 %collective-permute-start.5 = (bf16[4,2,48,384]{3,2,1,0:T(8,128)(2,1)S(1)}, bf16[4,2,48,384]{3,2,1,0:T(8,128)(2,1)S(1)}, u32[]{:S(2)}, u32[]{:S(2)}) collective-permute-start(bf16[4,2,48,384]{3,2,1,0:T(8,128)(2,1)S(1)} %get-tuple-element.64), channel_id=1, source_target_pairs={{0,2},{1,7},{2,0},{3,5},{4,6},{5,3},{6,4},{7,1},{8,10},{9,15},{10,... | collective-permute-start | bytes 884744 | tf_op jit(solution)/shard_map/ppermute | solution.py:47
  35.6 2.1 %table.1 = s32[128]{0:T(128)S(1)} custom-call(s32[32]{0:T(128)S(1)} %copy-done, s32[32]{0:T(128)S(1)} %copy-done.1), custom_call_target="tpu_custom_call" | custom-call | flops 2000000000 | bytes 1000000 | tf_op jit(solution)/shard_map/table/pallas_call | solution.py:425
  37.8 2.1 %collective-permute-done.5 = bf16[4,2,48,384]{3,2,1,0:T(8,128)(2,1)S(1)} collective-permute-done((bf16[4,2,48,384]{3,2,1,0:T(8,128)(2,1)S(1)}, bf16[4,2,48,384]{3,2,1,0:T(8,128)(2,1)S(1)}, u32[]{:S(2)}, u32[]{:S(2)}) %collective-permute-start.5) | collective-permute-done | bytes 294944 | tf_op jit(solution)/shard_map/ppermute | solution.py:47
  41.9 7.2 %collective-permute-done.8.refs_3_ = bf16[2,4,2,48,384]{4,3,2,1,0:T(8,128)(2,1)S(1)} collective-permute-done((bf16[2,4,2,48,384]{4,3,2,1,0:T(8,128)(2,1)S(1)}, bf16[2,4,2,48,384]{4,3,2,1,0:T(8,128)(2,1)S(1)}, u32[]{:S(2)}, u32[]{:S(2)}) %collective-permute-start.8) | collective-permute-done | bytes 589856 | tf_op jit(solution)/shard_map/ppermute | solution.py:47
  49.3 4.2 %stats_own.1 = (bf16[2,768,384]{2,1,0:T(8,128)(2,1)S(1)}, s32[8,768]{1,0:T(8,128)S(1)}, bf16[2,768,384]{2,1,0:T(8,128)(2,1)S(1)}, s32[768,128]{1,0:T(8,128)S(1)}, f32[56,128]{1,0:T(8,128)S(1)}) custom-call(s32[128]{0:T(128)S(1)} %table.1, bf16[2,4,2,48,384]{4,3,2,1,0:T(8,128)(2,1)S(1)} %pad_maximum_fusion.refs_0_, ...), custom_call_target="tpu_custom_call" | custom-call | flops 3000000000 | bytes 6000000 | tf_op jit(solution)/shard_map/stats_own/pallas_call | solution.py:396
  53.5 3.0 %stats_other.1 = (bf16[2,768,384]{2,1,0:T(8,128)(2,1)S(1)}, s32[768,128]{1,0:T(8,128)S(1)}, f32[56,128]{1,0:T(8,128)S(1)}) custom-call(s32[128]{0:T(128)S(1)} %table.1, bf16[2,768,384]{2,1,0:T(8,128)(2,1)S(1)} %get-tuple-element.36.refs_0_.qbuf, s32[8,768]{1,0:T(8,128)S(1)} %get-tuple-element.37.refs_1_.qgrp, f32[56,128]{1,0:T(8,128)S(1)} %get-tuple-element.40.refs_2_, ...), custom_call_target="tpu_custom_call" | custom-call | flops 3000000000 | bytes 6000000 | tf_op jit(solution)/shard_map/stats_other/pallas_call | solution.py:396
  59.6 2.6 %collective-permute-done.12.refs_2_ = f32[56,128]{1,0:T(8,128)S(1)} collective-permute-done((f32[56,128]{1,0:T(8,128)S(1)}, f32[56,128]{1,0:T(8,128)S(1)}, u32[]{:S(2)}, u32[]{:S(2)}) %collective-permute-start.12) | collective-permute-done | bytes 28704 | tf_op jit(solution)/shard_map/ppermute | solution.py:47
  62.3 4.0 %grads_other.1 = (bf16[4,4,2,48,384]{4,3,2,1,0:T(8,128)(2,1)S(1)}, f32[3,128,768]{2,1,0:T(8,128)S(1)}, f32[48,128]{1,0:T(8,128)S(1)}) custom-call(s32[128]{0:T(128)S(1)} %table.1, bf16[2,768,384]{2,1,0:T(8,128)(2,1)S(1)} %get-tuple-element.36.refs_0_.qbuf, s32[8,768]{1,0:T(8,128)S(1)} %get-tuple-element.37.refs_1_.qgrp, ...), custom_call_target="tpu_custom_call" | custom-call | flops 3000000000 | bytes 6000000 | tf_op jit(solution)/shard_map/grads_other/pallas_call | solution.py:396
  66.3 5.8 %collective-permute-start.14 = (bf16[4,4,2,48,384]{4,3,2,1,0:T(8,128)(2,1)S(1)}, bf16[4,4,2,48,384]{4,3,2,1,0:T(8,128)(2,1)S(1)}, u32[]{:S(2)}, u32[]{:S(2)}) collective-permute-start(bf16[4,4,2,48,384]{4,3,2,1,0:T(8,128)(2,1)S(1)} %get-tuple-element.48), channel_id=1, source_target_pairs={{0,1},{1,0},{2,3},{3,2},{4,5},{5,4},{6,7},{7,6},{8,9},{9,8},{10,11... | collective-permute-start | bytes 3538952 | tf_op jit(solution)/shard_map/ppermute | solution.py:47
  72.0 5.5 %grads_own.1 = (bf16[4,4,2,48,384]{4,3,2,1,0:T(8,128)(2,1)S(1)}, bf16[4,4,48,384]{3,2,1,0:T(8,128)(2,1)S(1)}) custom-call(s32[128]{0:T(128)S(1)} %table.1, bf16[2,768,384]{2,1,0:T(8,128)(2,1)S(1)} %get-tuple-element.36.refs_0_.qbuf, s32[8,768]{1,0:T(8,128)S(1)} %get-tuple-element.37.refs_1_.qgrp, bf16[2,768,384]{2,1,0:T(8,128)(2,1)S(1)} %get-tuple-element.38.kbuf, ...), custom_call_target="tpu_custom_call" | custom-call | flops 3000000000 | bytes 6000000 | tf_op jit(solution)/shard_map/grads_own/pallas_call | solution.py:396
  78.7 5.9 %collective-permute-done.16 = bf16[2,4,48,384]{3,2,1,0:T(8,128)(2,1)S(1)} collective-permute-done((bf16[2,4,48,384]{3,2,1,0:T(8,128)(2,1)S(1)}, bf16[2,4,48,384]{3,2,1,0:T(8,128)(2,1)S(1)}, u32[]{:S(2)}, u32[]{:S(2)}) %collective-permute-start.16) | collective-permute-done | bytes 294944 | tf_op jit(solution)/shard_map/ppermute | solution.py:47
  84.6 2.5 %collective-permute-done.15 = bf16[2,4,2,48,384]{4,3,2,1,0:T(8,128)(2,1)S(1)} collective-permute-done((bf16[2,4,2,48,384]{4,3,2,1,0:T(8,128)(2,1)S(1)}, bf16[2,4,2,48,384]{4,3,2,1,0:T(8,128)(2,1)S(1)}, u32[]{:S(2)}, u32[]{:S(2)}) %collective-permute-start.15) | collective-permute-done | bytes 589856 | tf_op jit(solution)/shard_map/ppermute | solution.py:47
  87.5 5.2 %collective-permute-done.18 = bf16[4,48,384]{2,1,0:T(8,128)(2,1)S(1)} collective-permute-done((bf16[4,48,384]{2,1,0:T(8,128)(2,1)S(1)}, bf16[4,48,384]{2,1,0:T(8,128)(2,1)S(1)}, u32[]{:S(2)}, u32[]{:S(2)}) %collective-permute-start.18) | collective-permute-done | bytes 147488 | tf_op jit(solution)/shard_map/ppermute | solution.py:47
  97.8 3.2 %collective-permute-start.22 = (bf16[3,48,384]{2,1,0:T(8,128)(2,1)S(1)}, bf16[3,48,384]{2,1,0:T(8,128)(2,1)S(1)}, u32[]{:S(2)}, u32[]{:S(2)}) collective-permute-start(bf16[3,48,384]{2,1,0:T(8,128)(2,1)S(1)} %pad_maximum_fusion.9), channel_id=1, source_target_pairs={{0,16},{1,9},{2,18},{3,11},{4,20},{5,13},{6,22},{7,15},{8,24},{9,1... | collective-permute-start | bytes 331784 | tf_op jit(solution)/shard_map/ppermute | solution.py:47
  103.1 6.7 %collective-permute-done.22 = bf16[3,48,384]{2,1,0:T(8,128)(2,1)S(1)} collective-permute-done((bf16[3,48,384]{2,1,0:T(8,128)(2,1)S(1)}, bf16[3,48,384]{2,1,0:T(8,128)(2,1)S(1)}, u32[]{:S(2)}, u32[]{:S(2)}) %collective-permute-start.22) | collective-permute-done | bytes 110624 | tf_op jit(solution)/shard_map/ppermute | solution.py:47
  109.9 3.9 %collective-permute-start.23 = (bf16[4,3,24,384]{3,2,1,0:T(8,128)(2,1)S(1)}, bf16[4,3,24,384]{3,2,1,0:T(8,128)(2,1)S(1)}, u32[]{:S(2)}, u32[]{:S(2)}) collective-permute-start(bf16[4,3,24,384]{3,2,1,0:T(8,128)(2,1)S(1)} %get-tuple-element.57), channel_id=1, source_target_pairs={{0,1},{1,0},{2,3},{3,2},{4,5},{5,4},{6,7},{7,6},{8,9},{9,8},{10,11... | collective-permute-start | bytes 663560 | tf_op jit(solution)/shard_map/ppermute | solution.py:47
  (65 shorter events, 21.7 us)
Async XLA Ops:
  2.7 4.7 %collective-permute-start = (bf16[4,4,24,384]{3,2,1,0:T(8,128)(2,1)}, bf16[4,4,24,384]{3,2,1,0:T(8,128)(2,1)S(1)}, u32[]{:S(2)}, u32[]{:S(2)}) collective-permute-start(bf16[4,4,24,384]{3,2,1,0:T(8,128)(2,1)} %get-tuple-element.29), channel_id=1, source_target_pairs={{0,1},{1,0},{2,3},{3,2},{4,5},{5,4},{6,7},{7,6},{8,9},{9,8},{10,11... | collective-permute-start | bytes 884744 | tf_op jit(solution)/shard_map/ppermute | solution.py:47
  8.7 9.1 %collective-permute-start.1 = (bf16[4,48,384]{2,1,0:T(8,128)(2,1)S(1)}, bf16[4,48,384]{2,1,0:T(8,128)(2,1)S(1)}, u32[]{:S(2)}, u32[]{:S(2)}) collective-permute-start(bf16[4,48,384]{2,1,0:T(8,128)(2,1)S(1)} %get-tuple-element.53), channel_id=1, source_target_pairs={{0,0},{1,9},{2,2},{3,11},{4,4},{5,13},{6,6},{7,15},{8,8},{9,17},{1... | collective-permute-start | bytes 442376 | tf_op jit(solution)/shard_map/ppermute | solution.py:47
  10.7 12.3 %collective-permute-start.4 = (bf16[4,48,384]{2,1,0:T(8,128)(2,1)S(1)}, bf16[4,48,384]{2,1,0:T(8,128)(2,1)S(1)}, u32[]{:S(2)}, u32[]{:S(2)}) collective-permute-start(bf16[4,48,384]{2,1,0:T(8,128)(2,1)S(1)} %get-tuple-element.54), channel_id=1, source_target_pairs={{0,48},{1,57},{2,50},{3,59},{4,52},{5,61},{6,54},{7,63},{8,56},{9,... | collective-permute-start | bytes 442376 | tf_op jit(solution)/shard_map/ppermute | solution.py:47
  14.6 13.1 %collective-permute-start.3 = (bf16[4,48,384]{2,1,0:T(8,128)(2,1)S(1)}, bf16[4,48,384]{2,1,0:T(8,128)(2,1)S(1)}, u32[]{:S(2)}, u32[]{:S(2)}) collective-permute-start(bf16[4,48,384]{2,1,0:T(8,128)(2,1)S(1)} %get-tuple-element.55), channel_id=1, source_target_pairs={{0,32},{1,41},{2,34},{3,43},{4,36},{5,45},{6,38},{7,47},{8,40},{9,... | collective-permute-start | bytes 442376 | tf_op jit(solution)/shard_map/ppermute | solution.py:47
  16.9 13.1 %collective-permute-start.2 = (bf16[4,48,384]{2,1,0:T(8,128)(2,1)S(1)}, bf16[4,48,384]{2,1,0:T(8,128)(2,1)S(1)}, u32[]{:S(2)}, u32[]{:S(2)}) collective-permute-start(bf16[4,48,384]{2,1,0:T(8,128)(2,1)S(1)} %get-tuple-element.56), channel_id=1, source_target_pairs={{0,16},{1,25},{2,18},{3,27},{4,20},{5,29},{6,22},{7,31},{8,24},{9,... | collective-permute-start | bytes 442376 | tf_op jit(solution)/shard_map/ppermute | solution.py:47
  30.1 7.7 %collective-permute-start.6 = (bf16[4,2,48,384]{3,2,1,0:T(8,128)(2,1)S(1)}, bf16[4,2,48,384]{3,2,1,0:T(8,128)(2,1)S(1)}, u32[]{:S(2)}, u32[]{:S(2)}) collective-permute-start(bf16[4,2,48,384]{3,2,1,0:T(8,128)(2,1)S(1)} %get-tuple-element.66), channel_id=1, source_target_pairs={{0,64},{1,193},{2,66},{3,195},{4,68},{5,197},{6,70},{7,199},{8,72}... | collective-permute-start | bytes 884744 | tf_op jit(solution)/shard_map/ppermute | solution.py:47
  33.1 6.9 %collective-permute-start.5 = (bf16[4,2,48,384]{3,2,1,0:T(8,128)(2,1)S(1)}, bf16[4,2,48,384]{3,2,1,0:T(8,128)(2,1)S(1)}, u32[]{:S(2)}, u32[]{:S(2)}) collective-permute-start(bf16[4,2,48,384]{3,2,1,0:T(8,128)(2,1)S(1)} %get-tuple-element.64), channel_id=1, source_target_pairs={{0,2},{1,7},{2,0},{3,5},{4,6},{5,3},{6,4},{7,1},{8,10},{9,15},{10,... | collective-permute-start | bytes 884744 | tf_op jit(solution)/shard_map/ppermute | solution.py:47
  40.0 9.1 %collective-permute-start.8 = (bf16[2,4,2,48,384]{4,3,2,1,0:T(8,128)(2,1)S(1)}, bf16[2,4,2,48,384]{4,3,2,1,0:T(8,128)(2,1)S(1)}, u32[]{:S(2)}, u32[]{:S(2)}) collective-permute-start(bf16[2,4,2,48,384]{4,3,2,1,0:T(8,128)(2,1)S(1)} %pad_maximum_fusion.1.refs_2_), channel_id=1, source_target_pairs={{0,6},{1,3},{2,4},{3,1},{4,2},{5,7},{6,0},{7,5},{8,14},{9,11},{10,... | collective-permute-start | bytes 1769480 | tf_op jit(solution)/shard_map/ppermute | solution.py:47
  40.2 9.1 %collective-permute-start.7 = (bf16[2,4,2,48,384]{4,3,2,1,0:T(8,128)(2,1)S(1)}, bf16[2,4,2,48,384]{4,3,2,1,0:T(8,128)(2,1)S(1)}, u32[]{:S(2)}, u32[]{:S(2)}) collective-permute-start(bf16[2,4,2,48,384]{4,3,2,1,0:T(8,128)(2,1)S(1)} %pad_maximum_fusion.refs_0_), channel_id=1, source_target_pairs={{0,192},{1,65},{2,194},{3,67},{4,196},{5,69},{6,198},{7,71},{8,200... | collective-permute-start | bytes 1769480 | tf_op jit(solution)/shard_map/ppermute | solution.py:47
  40.3 13.2 %collective-permute-start.9 = (bf16[2,4,2,48,384]{4,3,2,1,0:T(8,128)(2,1)S(1)}, bf16[2,4,2,48,384]{4,3,2,1,0:T(8,128)(2,1)S(1)}, u32[]{:S(2)}, u32[]{:S(2)}) collective-permute-start(bf16[2,4,2,48,384]{4,3,2,1,0:T(8,128)(2,1)S(1)} %pad_maximum_fusion.1.refs_2_), channel_id=1, source_target_pairs={{0,1},{1,0},{2,3},{3,2},{4,5},{5,4},{6,7},{7,6},{8,9},{9,8},{10,11... | collective-permute-start | bytes 1769480 | tf_op jit(solution)/shard_map/ppermute | solution.py:47
  49.1 4.4 %collective-permute-start.10 = (bf16[2,4,2,48,384]{4,3,2,1,0:T(8,128)(2,1)S(1)}, bf16[2,4,2,48,384]{4,3,2,1,0:T(8,128)(2,1)S(1)}, u32[]{:S(2)}, u32[]{:S(2)}) collective-permute-start(bf16[2,4,2,48,384]{4,3,2,1,0:T(8,128)(2,1)S(1)} %collective-permute-done.8.refs_3_), channel_id=1, source_target_pairs={{0,1},{1,0},{2,3},{3,2},{4,5},{5,4},{6,7},{7,6},{8,9},{9,8},{10,11... | collective-permute-start | bytes 1769480 | tf_op jit(solution)/shard_map/ppermute | solution.py:47
  56.6 3.0 %collective-permute-start.13 = (f32[56,128]{1,0:T(8,128)S(1)}, f32[56,128]{1,0:T(8,128)S(1)}, u32[]{:S(2)}, u32[]{:S(2)}) collective-permute-start(f32[56,128]{1,0:T(8,128)S(1)} %get-tuple-element.43.refs_0_), channel_id=1, source_target_pairs={{0,192},{1,193},{2,194},{3,195},{4,196},{5,197},{6,198},{7,199},{8... | collective-permute-start | bytes 86024 | tf_op jit(solution)/shard_map/ppermute | solution.py:47
  57.9 4.3 %collective-permute-start.12 = (f32[56,128]{1,0:T(8,128)S(1)}, f32[56,128]{1,0:T(8,128)S(1)}, u32[]{:S(2)}, u32[]{:S(2)}) collective-permute-start(f32[56,128]{1,0:T(8,128)S(1)} %get-tuple-element.43.refs_0_), channel_id=1, source_target_pairs={{0,128},{1,129},{2,130},{3,131},{4,132},{5,133},{6,134},{7,135},{8... | collective-permute-start | bytes 86024 | tf_op jit(solution)/shard_map/ppermute | solution.py:47
  57.9 4.4 %collective-permute-start.11 = (f32[56,128]{1,0:T(8,128)S(1)}, f32[56,128]{1,0:T(8,128)S(1)}, u32[]{:S(2)}, u32[]{:S(2)}) collective-permute-start(f32[56,128]{1,0:T(8,128)S(1)} %get-tuple-element.43.refs_0_), channel_id=1, source_target_pairs={{0,64},{1,65},{2,66},{3,67},{4,68},{5,69},{6,70},{7,71},{8,72},{9,... | collective-permute-start | bytes 86024 | tf_op jit(solution)/shard_map/ppermute | solution.py:47
  66.3 11.3 %collective-permute-start.14 = (bf16[4,4,2,48,384]{4,3,2,1,0:T(8,128)(2,1)S(1)}, bf16[4,4,2,48,384]{4,3,2,1,0:T(8,128)(2,1)S(1)}, u32[]{:S(2)}, u32[]{:S(2)}) collective-permute-start(bf16[4,4,2,48,384]{4,3,2,1,0:T(8,128)(2,1)S(1)} %get-tuple-element.48), channel_id=1, source_target_pairs={{0,1},{1,0},{2,3},{3,2},{4,5},{5,4},{6,7},{7,6},{8,9},{9,8},{10,11... | collective-permute-start | bytes 3538952 | tf_op jit(solution)/shard_map/ppermute | solution.py:47
  77.9 9.1 %collective-permute-start.15 = (bf16[2,4,2,48,384]{4,3,2,1,0:T(8,128)(2,1)S(1)}, bf16[2,4,2,48,384]{4,3,2,1,0:T(8,128)(2,1)S(1)}, u32[]{:S(2)}, u32[]{:S(2)}) collective-permute-start(bf16[2,4,2,48,384]{4,3,2,1,0:T(8,128)(2,1)S(1)} %slice.220), channel_id=1, source_target_pairs={{0,6},{1,3},{2,4},{3,1},{4,2},{5,7},{6,0},{7,5},{8,14},{9,11},{10,... | collective-permute-start | bytes 1769480 | tf_op jit(solution)/shard_map/ppermute | solution.py:47
  78.6 6.0 %collective-permute-start.16 = (bf16[2,4,48,384]{3,2,1,0:T(8,128)(2,1)S(1)}, bf16[2,4,48,384]{3,2,1,0:T(8,128)(2,1)S(1)}, u32[]{:S(2)}, u32[]{:S(2)}) collective-permute-start(bf16[2,4,48,384]{3,2,1,0:T(8,128)(2,1)S(1)} %slice.125), channel_id=1, source_target_pairs={{0,192},{1,65},{2,194},{3,67},{4,196},{5,69},{6,198},{7,71},{8,200... | collective-permute-start | bytes 884744 | tf_op jit(solution)/shard_map/ppermute | solution.py:47
  87.3 6.9 %collective-permute-start.17 = (bf16[4,2,48,384]{3,2,1,0:T(8,128)(2,1)S(1)}, bf16[4,2,48,384]{3,2,1,0:T(8,128)(2,1)S(1)}, u32[]{:S(2)}, u32[]{:S(2)}) collective-permute-start(bf16[4,2,48,384]{3,2,1,0:T(8,128)(2,1)S(1)} %fusion.2), channel_id=1, source_target_pairs={{0,2},{1,7},{2,0},{3,5},{4,6},{5,3},{6,4},{7,1},{8,10},{9,15},{10,... | collective-permute-start | bytes 884744 | tf_op jit(solution)/shard_map/ppermute | solution.py:47
  87.4 5.3 %collective-permute-start.18 = (bf16[4,48,384]{2,1,0:T(8,128)(2,1)S(1)}, bf16[4,48,384]{2,1,0:T(8,128)(2,1)S(1)}, u32[]{:S(2)}, u32[]{:S(2)}) collective-permute-start(bf16[4,48,384]{2,1,0:T(8,128)(2,1)S(1)} %fusion.5), channel_id=1, source_target_pairs={{0,64},{1,193},{2,66},{3,195},{4,68},{5,197},{6,70},{7,199},{8,72}... | collective-permute-start | bytes 442376 | tf_op jit(solution)/shard_map/ppermute | solution.py:47
  94.4 8.6 %collective-permute-start.20 = (bf16[3,48,384]{2,1,0:T(8,128)(2,1)S(1)}, bf16[3,48,384]{2,1,0:T(8,128)(2,1)S(1)}, u32[]{:S(2)}, u32[]{:S(2)}) collective-permute-start(bf16[3,48,384]{2,1,0:T(8,128)(2,1)S(1)} %pad_maximum_fusion.7), channel_id=1, source_target_pairs={{0,48},{1,41},{2,50},{3,43},{4,52},{5,45},{6,54},{7,47},{8,56},{9,... | collective-permute-start | bytes 331784 | tf_op jit(solution)/shard_map/ppermute | solution.py:47
  96.1 7.0 %collective-permute-start.21 = (bf16[3,48,384]{2,1,0:T(8,128)(2,1)S(1)}, bf16[3,48,384]{2,1,0:T(8,128)(2,1)S(1)}, u32[]{:S(2)}, u32[]{:S(2)}) collective-permute-start(bf16[3,48,384]{2,1,0:T(8,128)(2,1)S(1)} %pad_maximum_fusion.8), channel_id=1, source_target_pairs={{0,32},{1,25},{2,34},{3,27},{4,36},{5,29},{6,38},{7,31},{8,40},{9,... | collective-permute-start | bytes 331784 | tf_op jit(solution)/shard_map/ppermute | solution.py:47
  97.8 12.0 %collective-permute-start.22 = (bf16[3,48,384]{2,1,0:T(8,128)(2,1)S(1)}, bf16[3,48,384]{2,1,0:T(8,128)(2,1)S(1)}, u32[]{:S(2)}, u32[]{:S(2)}) collective-permute-start(bf16[3,48,384]{2,1,0:T(8,128)(2,1)S(1)} %pad_maximum_fusion.9), channel_id=1, source_target_pairs={{0,16},{1,9},{2,18},{3,11},{4,20},{5,13},{6,22},{7,15},{8,24},{9,1... | collective-permute-start | bytes 331784 | tf_op jit(solution)/shard_map/ppermute | solution.py:47
  101.1 8.8 %collective-permute-start.19 = (bf16[3,48,384]{2,1,0:T(8,128)(2,1)S(1)}, bf16[3,48,384]{2,1,0:T(8,128)(2,1)S(1)}, u32[]{:S(2)}, u32[]{:S(2)}) collective-permute-start(bf16[3,48,384]{2,1,0:T(8,128)(2,1)S(1)} %pad_maximum_fusion.6), channel_id=1, source_target_pairs={{0,0},{1,57},{2,2},{3,59},{4,4},{5,61},{6,6},{7,63},{8,8},{9,1},{1... | collective-permute-start | bytes 331784 | tf_op jit(solution)/shard_map/ppermute | solution.py:47
  109.9 5.0 %collective-permute-start.23 = (bf16[4,3,24,384]{3,2,1,0:T(8,128)(2,1)S(1)}, bf16[4,3,24,384]{3,2,1,0:T(8,128)(2,1)S(1)}, u32[]{:S(2)}, u32[]{:S(2)}) collective-permute-start(bf16[4,3,24,384]{3,2,1,0:T(8,128)(2,1)S(1)} %get-tuple-element.57), channel_id=1, source_target_pairs={{0,1},{1,0},{2,3},{3,2},{4,5},{5,4},{6,7},{7,6},{8,9},{9,8},{10,11... | collective-permute-start | bytes 663560 | tf_op jit(solution)/shard_map/ppermute | solution.py:47
  (2 other events, 25.3 us)

commit v4 on v2

--- a/solution.py
+++ b/solution.py
@@ -207,12 +207,12 @@
 
 
 def visit(blocks, step, state):
-    half = KCHUNK // 2
-    whole = blocks // 2
-    state = lax.fori_loop(0, whole, lambda i, v: step(pl.ds(pl.multiple_of(i * KCHUNK, KCHUNK), KCHUNK), v), state)
-    return lax.fori_loop(
-        0, blocks - 2 * whole, lambda i, v: step(pl.ds(pl.multiple_of(whole * KCHUNK, KCHUNK), half), v), state
-    )
+    def body(rows):
+        return lambda i, v: step(pl.ds(0, rows), v)
+
+    for count in (1, 2, 3):
+        state = lax.fori_loop(0, jnp.where(blocks == count, 1, 0), body(count * KCHUNK // 2), state)
+    return state
 
 
 def aligned(first):

time: 117 us -> 114 us (0.974)
  starting transfers between devices: 41.5 us -> 40 us
    ppermute x25, starting transfers between devices: 41.5 us -> 40 us  [send(): return lax.ppermute(array, ('tm', 'head'), pairs(move))]
  transfers between devices with their start and end apart: 25 -> 25, of which waited for: 15 -> 16; matrix products, arithmetic and copies ran while one was open for 0% -> 0% of each run, Pallas kernels for 11% -> 9%
where the time goes in v4:
time: 114 us; the launch traced here: 113 us
  waiting for transfers between devices  48.7 us (43%)
  starting transfers between devices  40 us (35%)
  Pallas kernels  20.7 us (18%)
  other arithmetic  2.28 us (2%)
    ppermute x25, waiting for transfers between devices, send(): return lax.ppermute(array, ('tm', 'head'), pairs(move))  48.7 us
    ppermute x25, starting transfers between devices, send(): return lax.ppermute(array, ('tm', 'head'), pairs(move))  40 us
    pallas_call x4, Pallas kernels, run(): pl.pallas_call(kernel, out_shape=out_shape, in_specs=[SMEM] * len(tables)...  15.7 us
  transfers between devices with their start and end apart: 25, of which 16 were waited for; matrix products, arithmetic and copies ran while one was open for 0% of the time, Pallas kernels for 9%

profile of v4, /device:TPU:1, one launch (start us, length us, event | category | flops | bytes accessed | tf_op | source)
XLA Modules:
  0.0 113.0 jit_solution(3228713023949023805)
XLA Ops:
  2.7 3.3 %collective-permute-start = (bf16[4,4,24,384]{3,2,1,0:T(8,128)(2,1)}, bf16[4,4,24,384]{3,2,1,0:T(8,128)(2,1)S(1)}, u32[]{:S(2)}, u32[]{:S(2)}) collective-permute-start(bf16[4,4,24,384]{3,2,1,0:T(8,128)(2,1)} %get-tuple-element.29), channel_id=1, source_target_pairs={{0,1},{1,0},{2,3},{3,2},{4,5},{5,4},{6,7},{7,6},{8,9},{9,8},{10,11... | collective-permute-start | bytes 884744 | tf_op jit(solution)/shard_map/ppermute | solution.py:45
  10.6 3.9 %collective-permute-start.4 = (bf16[4,48,384]{2,1,0:T(8,128)(2,1)S(1)}, bf16[4,48,384]{2,1,0:T(8,128)(2,1)S(1)}, u32[]{:S(2)}, u32[]{:S(2)}) collective-permute-start(bf16[4,48,384]{2,1,0:T(8,128)(2,1)S(1)} %get-tuple-element.54), channel_id=1, source_target_pairs={{0,48},{1,57},{2,50},{3,59},{4,52},{5,61},{6,54},{7,63},{8,56},{9,... | collective-permute-start | bytes 442376 | tf_op jit(solution)/shard_map/ppermute | solution.py:45
  14.6 2.3 %collective-permute-start.3 = (bf16[4,48,384]{2,1,0:T(8,128)(2,1)S(1)}, bf16[4,48,384]{2,1,0:T(8,128)(2,1)S(1)}, u32[]{:S(2)}, u32[]{:S(2)}) collective-permute-start(bf16[4,48,384]{2,1,0:T(8,128)(2,1)S(1)} %get-tuple-element.55), channel_id=1, source_target_pairs={{0,32},{1,41},{2,34},{3,43},{4,36},{5,45},{6,38},{7,47},{8,40},{9,... | collective-permute-start | bytes 442376 | tf_op jit(solution)/shard_map/ppermute | solution.py:45
  17.9 5.1 %collective-permute-done.4 = bf16[4,48,384]{2,1,0:T(8,128)(2,1)S(1)} collective-permute-done((bf16[4,48,384]{2,1,0:T(8,128)(2,1)S(1)}, bf16[4,48,384]{2,1,0:T(8,128)(2,1)S(1)}, u32[]{:S(2)}, u32[]{:S(2)}) %collective-permute-start.4) | collective-permute-done | bytes 147488 | tf_op jit(solution)/shard_map/ppermute | solution.py:45
  23.0 4.7 %collective-permute-done.3 = bf16[4,48,384]{2,1,0:T(8,128)(2,1)S(1)} collective-permute-done((bf16[4,48,384]{2,1,0:T(8,128)(2,1)S(1)}, bf16[4,48,384]{2,1,0:T(8,128)(2,1)S(1)}, u32[]{:S(2)}, u32[]{:S(2)}) %collective-permute-start.3) | collective-permute-done | bytes 147488 | tf_op jit(solution)/shard_map/ppermute | solution.py:45
  27.7 2.3 %collective-permute-done.2 = bf16[4,48,384]{2,1,0:T(8,128)(2,1)S(1)} collective-permute-done((bf16[4,48,384]{2,1,0:T(8,128)(2,1)S(1)}, bf16[4,48,384]{2,1,0:T(8,128)(2,1)S(1)}, u32[]{:S(2)}, u32[]{:S(2)}) %collective-permute-start.2) | collective-permute-done | bytes 147488 | tf_op jit(solution)/shard_map/ppermute | solution.py:45
  30.1 2.9 %collective-permute-start.6 = (bf16[4,2,48,384]{3,2,1,0:T(8,128)(2,1)S(1)}, bf16[4,2,48,384]{3,2,1,0:T(8,128)(2,1)S(1)}, u32[]{:S(2)}, u32[]{:S(2)}) collective-permute-start(bf16[4,2,48,384]{3,2,1,0:T(8,128)(2,1)S(1)} %get-tuple-element.66.refs_0_), channel_id=1, source_target_pairs={{0,64},{1,193},{2,66},{3,195},{4,68},{5,197},{6,70},{7,199},{8,72}... | collective-permute-start | bytes 884744 | tf_op jit(solution)/shard_map/ppermute | solution.py:45
  33.0 2.6 %collective-permute-start.5 = (bf16[4,2,48,384]{3,2,1,0:T(8,128)(2,1)S(1)}, bf16[4,2,48,384]{3,2,1,0:T(8,128)(2,1)S(1)}, u32[]{:S(2)}, u32[]{:S(2)}) collective-permute-start(bf16[4,2,48,384]{3,2,1,0:T(8,128)(2,1)S(1)} %get-tuple-element.64.refs_3_), channel_id=1, source_target_pairs={{0,2},{1,7},{2,0},{3,5},{4,6},{5,3},{6,4},{7,1},{8,10},{9,15},{10,... | collective-permute-start | bytes 884744 | tf_op jit(solution)/shard_map/ppermute | solution.py:45
  35.6 2.1 %table.1 = s32[128]{0:T(128)S(1)} custom-call(s32[32]{0:T(128)S(1)} %copy-done, s32[32]{0:T(128)S(1)} %copy-done.1), custom_call_target="tpu_custom_call" | custom-call | flops 2000000000 | bytes 1000000 | tf_op jit(solution)/shard_map/table/pallas_call | solution.py:415
  37.8 2.1 %collective-permute-done.5.refs_4_ = bf16[4,2,48,384]{3,2,1,0:T(8,128)(2,1)S(1)} collective-permute-done((bf16[4,2,48,384]{3,2,1,0:T(8,128)(2,1)S(1)}, bf16[4,2,48,384]{3,2,1,0:T(8,128)(2,1)S(1)}, u32[]{:S(2)}, u32[]{:S(2)}) %collective-permute-start.5) | collective-permute-done | bytes 294944 | tf_op jit(solution)/shard_map/ppermute | solution.py:45
  40.3 8.8 %collective-permute-done.8.refs_5_ = bf16[2,4,2,48,384]{4,3,2,1,0:T(8,128)(2,1)S(1)} collective-permute-done((bf16[2,4,2,48,384]{4,3,2,1,0:T(8,128)(2,1)S(1)}, bf16[2,4,2,48,384]{4,3,2,1,0:T(8,128)(2,1)S(1)}, u32[]{:S(2)}, u32[]{:S(2)}) %collective-permute-start.8) | collective-permute-done | bytes 589856 | tf_op jit(solution)/shard_map/ppermute | solution.py:45
  49.6 3.7 %stats_own.1 = (bf16[2,768,384]{2,1,0:T(8,128)(2,1)S(1)}, s32[8,768]{1,0:T(8,128)S(1)}, bf16[2,768,384]{2,1,0:T(8,128)(2,1)S(1)}, s32[768,128]{1,0:T(8,128)S(1)}, f32[16,768]{1,0:T(8,128)S(1)}) custom-call(s32[128]{0:T(128)S(1)} %table.1, bf16[4,2,48,384]{3,2,1,0:T(8,128)(2,1)S(1)} %get-tuple-element.66.refs_0_, ...), custom_call_target="tpu_custom_call" | custom-call | flops 3000000000 | bytes 6000000 | tf_op jit(solution)/shard_map/stats_own/pallas_call | solution.py:386
  53.3 3.1 %stats_other.1 = (bf16[2,768,384]{2,1,0:T(8,128)(2,1)S(1)}, s32[768,128]{1,0:T(8,128)S(1)}, f32[16,768]{1,0:T(8,128)S(1)}) custom-call(s32[128]{0:T(128)S(1)} %table.1, bf16[2,768,384]{2,1,0:T(8,128)(2,1)S(1)} %get-tuple-element.36.refs_0_.qbuf, s32[8,768]{1,0:T(8,128)S(1)} %get-tuple-element.37.refs_1_.qgrp, f32[16,768]{1,0:T(8,128)S(1)} %get-tuple-element.40.refs_2_, ...), custom_call_target="tpu_custom_call" | custom-call | flops 3000000000 | bytes 6000000 | tf_op jit(solution)/shard_map/stats_other/pallas_call | solution.py:386
  59.4 2.6 %collective-permute-done.13.refs_2_ = f32[16,768]{1,0:T(8,128)S(1)} collective-permute-done((f32[16,768]{1,0:T(8,128)S(1)}, f32[16,768]{1,0:T(8,128)S(1)}, u32[]{:S(2)}, u32[]{:S(2)}) %collective-permute-start.13) | collective-permute-done | bytes 49184 | tf_op jit(solution)/shard_map/ppermute | solution.py:45
  62.6 4.0 %grads_other.1 = (bf16[4,4,2,48,384]{4,3,2,1,0:T(8,128)(2,1)S(1)}, f32[3,128,768]{2,1,0:T(8,128)S(1)}, f32[8,768]{1,0:T(8,128)S(1)}) custom-call(s32[128]{0:T(128)S(1)} %table.1, bf16[2,768,384]{2,1,0:T(8,128)(2,1)S(1)} %get-tuple-element.36.refs_0_.qbuf, s32[8,768]{1,0:T(8,128)S(1)} %get-tuple-element.37.refs_1_.qgrp, ...), custom_call_target="tpu_custom_call" | custom-call | flops 3000000000 | bytes 6000000 | tf_op jit(solution)/shard_map/grads_other/pallas_call | solution.py:386
  66.6 3.9 %collective-permute-start.15 = (bf16[4,4,2,48,384]{4,3,2,1,0:T(8,128)(2,1)S(1)}, bf16[4,4,2,48,384]{4,3,2,1,0:T(8,128)(2,1)S(1)}, u32[]{:S(2)}, u32[]{:S(2)}) collective-permute-start(bf16[4,4,2,48,384]{4,3,2,1,0:T(8,128)(2,1)S(1)} %get-tuple-element.48), channel_id=1, source_target_pairs={{0,1},{1,0},{2,3},{3,2},{4,5},{5,4},{6,7},{7,6},{8,9},{9,8},{10,11... | collective-permute-start | bytes 3538952 | tf_op jit(solution)/shard_map/ppermute | solution.py:45
  70.5 4.9 %grads_own.1 = (bf16[4,4,2,48,384]{4,3,2,1,0:T(8,128)(2,1)S(1)}, bf16[4,4,48,384]{3,2,1,0:T(8,128)(2,1)S(1)}) custom-call(s32[128]{0:T(128)S(1)} %table.1, bf16[2,768,384]{2,1,0:T(8,128)(2,1)S(1)} %get-tuple-element.36.refs_0_.qbuf, s32[8,768]{1,0:T(8,128)S(1)} %get-tuple-element.37.refs_1_.qgrp, bf16[2,768,384]{2,1,0:T(8,128)(2,1)S(1)} %get-tuple-element.38.kbuf, ...), custom_call_target="tpu_custom_call" | custom-call | flops 3000000000 | bytes 6000000 | tf_op jit(solution)/shard_map/grads_own/pallas_call | solution.py:386
  76.0 5.9 %collective-permute-done.17 = bf16[2,4,48,384]{3,2,1,0:T(8,128)(2,1)S(1)} collective-permute-done((bf16[2,4,48,384]{3,2,1,0:T(8,128)(2,1)S(1)}, bf16[2,4,48,384]{3,2,1,0:T(8,128)(2,1)S(1)}, u32[]{:S(2)}, u32[]{:S(2)}) %collective-permute-start.17) | collective-permute-done | bytes 294944 | tf_op jit(solution)/shard_map/ppermute | solution.py:45
  81.9 3.0 %collective-permute-done.16 = bf16[2,4,2,48,384]{4,3,2,1,0:T(8,128)(2,1)S(1)} collective-permute-done((bf16[2,4,2,48,384]{4,3,2,1,0:T(8,128)(2,1)S(1)}, bf16[2,4,2,48,384]{4,3,2,1,0:T(8,128)(2,1)S(1)}, u32[]{:S(2)}, u32[]{:S(2)}) %collective-permute-start.16) | collective-permute-done | bytes 589856 | tf_op jit(solution)/shard_map/ppermute | solution.py:45
  85.5 5.1 %collective-permute-done.19 = bf16[4,48,384]{2,1,0:T(8,128)(2,1)S(1)} collective-permute-done((bf16[4,48,384]{2,1,0:T(8,128)(2,1)S(1)}, bf16[4,48,384]{2,1,0:T(8,128)(2,1)S(1)}, u32[]{:S(2)}, u32[]{:S(2)}) %collective-permute-start.19) | collective-permute-done | bytes 147488 | tf_op jit(solution)/shard_map/ppermute | solution.py:45
  92.3 4.3 %collective-permute-start.21 = (bf16[3,48,384]{2,1,0:T(8,128)(2,1)S(1)}, bf16[3,48,384]{2,1,0:T(8,128)(2,1)S(1)}, u32[]{:S(2)}, u32[]{:S(2)}) collective-permute-start(bf16[3,48,384]{2,1,0:T(8,128)(2,1)S(1)} %pad_maximum_fusion.7), channel_id=1, source_target_pairs={{0,48},{1,41},{2,50},{3,43},{4,52},{5,45},{6,54},{7,47},{8,56},{9,... | collective-permute-start | bytes 331784 | tf_op jit(solution)/shard_map/ppermute | solution.py:45
  96.7 2.7 %collective-permute-start.23 = (bf16[3,48,384]{2,1,0:T(8,128)(2,1)S(1)}, bf16[3,48,384]{2,1,0:T(8,128)(2,1)S(1)}, u32[]{:S(2)}, u32[]{:S(2)}) collective-permute-start(bf16[3,48,384]{2,1,0:T(8,128)(2,1)S(1)} %pad_maximum_fusion.9), channel_id=1, source_target_pairs={{0,16},{1,9},{2,18},{3,11},{4,20},{5,13},{6,22},{7,15},{8,24},{9,1... | collective-permute-start | bytes 331784 | tf_op jit(solution)/shard_map/ppermute | solution.py:45
  101.4 3.6 %collective-permute-done.22 = bf16[3,48,384]{2,1,0:T(8,128)(2,1)S(1)} collective-permute-done((bf16[3,48,384]{2,1,0:T(8,128)(2,1)S(1)}, bf16[3,48,384]{2,1,0:T(8,128)(2,1)S(1)}, u32[]{:S(2)}, u32[]{:S(2)}) %collective-permute-start.22) | collective-permute-done | bytes 110624 | tf_op jit(solution)/shard_map/ppermute | solution.py:45
  105.5 5.6 %collective-permute-start.24 = (bf16[4,3,24,384]{3,2,1,0:T(8,128)(2,1)S(1)}, bf16[4,3,24,384]{3,2,1,0:T(8,128)(2,1)S(1)}, u32[]{:S(2)}, u32[]{:S(2)}) collective-permute-start(bf16[4,3,24,384]{3,2,1,0:T(8,128)(2,1)S(1)} %get-tuple-element.57), channel_id=1, source_target_pairs={{0,1},{1,0},{2,3},{3,2},{4,5},{5,4},{6,7},{7,6},{8,9},{9,8},{10,11... | collective-permute-start | bytes 663560 | tf_op jit(solution)/shard_map/ppermute | solution.py:45
  (67 shorter events, 19.4 us)
Async XLA Ops:
  2.7 4.7 %collective-permute-start = (bf16[4,4,24,384]{3,2,1,0:T(8,128)(2,1)}, bf16[4,4,24,384]{3,2,1,0:T(8,128)(2,1)S(1)}, u32[]{:S(2)}, u32[]{:S(2)}) collective-permute-start(bf16[4,4,24,384]{3,2,1,0:T(8,128)(2,1)} %get-tuple-element.29), channel_id=1, source_target_pairs={{0,1},{1,0},{2,3},{3,2},{4,5},{5,4},{6,7},{7,6},{8,9},{9,8},{10,11... | collective-permute-start | bytes 884744 | tf_op jit(solution)/shard_map/ppermute | solution.py:45
  8.7 9.1 %collective-permute-start.1 = (bf16[4,48,384]{2,1,0:T(8,128)(2,1)S(1)}, bf16[4,48,384]{2,1,0:T(8,128)(2,1)S(1)}, u32[]{:S(2)}, u32[]{:S(2)}) collective-permute-start(bf16[4,48,384]{2,1,0:T(8,128)(2,1)S(1)} %get-tuple-element.53), channel_id=1, source_target_pairs={{0,0},{1,9},{2,2},{3,11},{4,4},{5,13},{6,6},{7,15},{8,8},{9,17},{1... | collective-permute-start | bytes 442376 | tf_op jit(solution)/shard_map/ppermute | solution.py:45
  10.6 12.3 %collective-permute-start.4 = (bf16[4,48,384]{2,1,0:T(8,128)(2,1)S(1)}, bf16[4,48,384]{2,1,0:T(8,128)(2,1)S(1)}, u32[]{:S(2)}, u32[]{:S(2)}) collective-permute-start(bf16[4,48,384]{2,1,0:T(8,128)(2,1)S(1)} %get-tuple-element.54), channel_id=1, source_target_pairs={{0,48},{1,57},{2,50},{3,59},{4,52},{5,61},{6,54},{7,63},{8,56},{9,... | collective-permute-start | bytes 442376 | tf_op jit(solution)/shard_map/ppermute | solution.py:45
  14.6 13.1 %collective-permute-start.3 = (bf16[4,48,384]{2,1,0:T(8,128)(2,1)S(1)}, bf16[4,48,384]{2,1,0:T(8,128)(2,1)S(1)}, u32[]{:S(2)}, u32[]{:S(2)}) collective-permute-start(bf16[4,48,384]{2,1,0:T(8,128)(2,1)S(1)} %get-tuple-element.55), channel_id=1, source_target_pairs={{0,32},{1,41},{2,34},{3,43},{4,36},{5,45},{6,38},{7,47},{8,40},{9,... | collective-permute-start | bytes 442376 | tf_op jit(solution)/shard_map/ppermute | solution.py:45
  16.9 13.1 %collective-permute-start.2 = (bf16[4,48,384]{2,1,0:T(8,128)(2,1)S(1)}, bf16[4,48,384]{2,1,0:T(8,128)(2,1)S(1)}, u32[]{:S(2)}, u32[]{:S(2)}) collective-permute-start(bf16[4,48,384]{2,1,0:T(8,128)(2,1)S(1)} %get-tuple-element.56), channel_id=1, source_target_pairs={{0,16},{1,25},{2,18},{3,27},{4,20},{5,29},{6,22},{7,31},{8,24},{9,... | collective-permute-start | bytes 442376 | tf_op jit(solution)/shard_map/ppermute | solution.py:45
  30.1 7.7 %collective-permute-start.6 = (bf16[4,2,48,384]{3,2,1,0:T(8,128)(2,1)S(1)}, bf16[4,2,48,384]{3,2,1,0:T(8,128)(2,1)S(1)}, u32[]{:S(2)}, u32[]{:S(2)}) collective-permute-start(bf16[4,2,48,384]{3,2,1,0:T(8,128)(2,1)S(1)} %get-tuple-element.66.refs_0_), channel_id=1, source_target_pairs={{0,64},{1,193},{2,66},{3,195},{4,68},{5,197},{6,70},{7,199},{8,72}... | collective-permute-start | bytes 884744 | tf_op jit(solution)/shard_map/ppermute | solution.py:45
  33.0 6.9 %collective-permute-start.5 = (bf16[4,2,48,384]{3,2,1,0:T(8,128)(2,1)S(1)}, bf16[4,2,48,384]{3,2,1,0:T(8,128)(2,1)S(1)}, u32[]{:S(2)}, u32[]{:S(2)}) collective-permute-start(bf16[4,2,48,384]{3,2,1,0:T(8,128)(2,1)S(1)} %get-tuple-element.64.refs_3_), channel_id=1, source_target_pairs={{0,2},{1,7},{2,0},{3,5},{4,6},{5,3},{6,4},{7,1},{8,10},{9,15},{10,... | collective-permute-start | bytes 884744 | tf_op jit(solution)/shard_map/ppermute | solution.py:45
  40.0 9.1 %collective-permute-start.8 = (bf16[2,4,2,48,384]{4,3,2,1,0:T(8,128)(2,1)S(1)}, bf16[2,4,2,48,384]{4,3,2,1,0:T(8,128)(2,1)S(1)}, u32[]{:S(2)}, u32[]{:S(2)}) collective-permute-start(bf16[2,4,2,48,384]{4,3,2,1,0:T(8,128)(2,1)S(1)} %pad_maximum_fusion.1), channel_id=1, source_target_pairs={{0,6},{1,3},{2,4},{3,1},{4,2},{5,7},{6,0},{7,5},{8,14},{9,11},{10,... | collective-permute-start | bytes 1769480 | tf_op jit(solution)/shard_map/ppermute | solution.py:45
  40.2 9.5 %collective-permute-start.7 = (bf16[2,4,2,48,384]{4,3,2,1,0:T(8,128)(2,1)S(1)}, bf16[2,4,2,48,384]{4,3,2,1,0:T(8,128)(2,1)S(1)}, u32[]{:S(2)}, u32[]{:S(2)}) collective-permute-start(bf16[2,4,2,48,384]{4,3,2,1,0:T(8,128)(2,1)S(1)} %pad_maximum_fusion), channel_id=1, source_target_pairs={{0,192},{1,65},{2,194},{3,67},{4,196},{5,69},{6,198},{7,71},{8,200... | collective-permute-start | bytes 1769480 | tf_op jit(solution)/shard_map/ppermute | solution.py:45
  49.1 4.2 %collective-permute-start.11 = (bf16[2,4,2,48,384]{4,3,2,1,0:T(8,128)(2,1)S(1)}, bf16[2,4,2,48,384]{4,3,2,1,0:T(8,128)(2,1)S(1)}, u32[]{:S(2)}, u32[]{:S(2)}) collective-permute-start(bf16[2,4,2,48,384]{4,3,2,1,0:T(8,128)(2,1)S(1)} %collective-permute-done.8.refs_5_), channel_id=1, source_target_pairs={{0,1},{1,0},{2,3},{3,2},{4,5},{5,4},{6,7},{7,6},{8,9},{9,8},{10,11... | collective-permute-start | bytes 1769480 | tf_op jit(solution)/shard_map/ppermute | solution.py:45
  49.1 4.2 %collective-permute-start.9 = (bf16[4,2,48,384]{3,2,1,0:T(8,128)(2,1)S(1)}, bf16[4,2,48,384]{3,2,1,0:T(8,128)(2,1)S(1)}, u32[]{:S(2)}, u32[]{:S(2)}) collective-permute-start(bf16[4,2,48,384]{3,2,1,0:T(8,128)(2,1)S(1)} %get-tuple-element.64.refs_3_), channel_id=1, source_target_pairs={{0,1},{1,0},{2,3},{3,2},{4,5},{5,4},{6,7},{7,6},{8,9},{9,8},{10,11... | collective-permute-start | bytes 884744 | tf_op jit(solution)/shard_map/ppermute | solution.py:45
  49.6 3.7 %collective-permute-start.10 = (bf16[4,2,48,384]{3,2,1,0:T(8,128)(2,1)S(1)}, bf16[4,2,48,384]{3,2,1,0:T(8,128)(2,1)S(1)}, u32[]{:S(2)}, u32[]{:S(2)}) collective-permute-start(bf16[4,2,48,384]{3,2,1,0:T(8,128)(2,1)S(1)} %collective-permute-done.5.refs_4_), channel_id=1, source_target_pairs={{0,1},{1,0},{2,3},{3,2},{4,5},{5,4},{6,7},{7,6},{8,9},{9,8},{10,11... | collective-permute-start | bytes 884744 | tf_op jit(solution)/shard_map/ppermute | solution.py:45
  57.6 4.5 %collective-permute-start.13 = (f32[16,768]{1,0:T(8,128)S(1)}, f32[16,768]{1,0:T(8,128)S(1)}, u32[]{:S(2)}, u32[]{:S(2)}) collective-permute-start(f32[16,768]{1,0:T(8,128)S(1)} %get-tuple-element.43.refs_0_), channel_id=1, source_target_pairs={{0,128},{1,129},{2,130},{3,131},{4,132},{5,133},{6,134},{7,135},{8... | collective-permute-start | bytes 147464 | tf_op jit(solution)/shard_map/ppermute | solution.py:45
  58.1 4.5 %collective-permute-start.12 = (f32[16,768]{1,0:T(8,128)S(1)}, f32[16,768]{1,0:T(8,128)S(1)}, u32[]{:S(2)}, u32[]{:S(2)}) collective-permute-start(f32[16,768]{1,0:T(8,128)S(1)} %get-tuple-element.43.refs_0_), channel_id=1, source_target_pairs={{0,64},{1,65},{2,66},{3,67},{4,68},{5,69},{6,70},{7,71},{8,72},{9,... | collective-permute-start | bytes 147464 | tf_op jit(solution)/shard_map/ppermute | solution.py:45
  66.6 8.8 %collective-permute-start.15 = (bf16[4,4,2,48,384]{4,3,2,1,0:T(8,128)(2,1)S(1)}, bf16[4,4,2,48,384]{4,3,2,1,0:T(8,128)(2,1)S(1)}, u32[]{:S(2)}, u32[]{:S(2)}) collective-permute-start(bf16[4,4,2,48,384]{4,3,2,1,0:T(8,128)(2,1)S(1)} %get-tuple-element.48), channel_id=1, source_target_pairs={{0,1},{1,0},{2,3},{3,2},{4,5},{5,4},{6,7},{7,6},{8,9},{9,8},{10,11... | collective-permute-start | bytes 3538952 | tf_op jit(solution)/shard_map/ppermute | solution.py:45
  75.8 9.1 %collective-permute-start.16 = (bf16[2,4,2,48,384]{4,3,2,1,0:T(8,128)(2,1)S(1)}, bf16[2,4,2,48,384]{4,3,2,1,0:T(8,128)(2,1)S(1)}, u32[]{:S(2)}, u32[]{:S(2)}) collective-permute-start(bf16[2,4,2,48,384]{4,3,2,1,0:T(8,128)(2,1)S(1)} %slice.220), channel_id=1, source_target_pairs={{0,6},{1,3},{2,4},{3,1},{4,2},{5,7},{6,0},{7,5},{8,14},{9,11},{10,... | collective-permute-start | bytes 1769480 | tf_op jit(solution)/shard_map/ppermute | solution.py:45
  75.9 6.0 %collective-permute-start.17 = (bf16[2,4,48,384]{3,2,1,0:T(8,128)(2,1)S(1)}, bf16[2,4,48,384]{3,2,1,0:T(8,128)(2,1)S(1)}, u32[]{:S(2)}, u32[]{:S(2)}) collective-permute-start(bf16[2,4,48,384]{3,2,1,0:T(8,128)(2,1)S(1)} %slice.125), channel_id=1, source_target_pairs={{0,192},{1,65},{2,194},{3,67},{4,196},{5,69},{6,198},{7,71},{8,200... | collective-permute-start | bytes 884744 | tf_op jit(solution)/shard_map/ppermute | solution.py:45
  85.2 6.9 %collective-permute-start.18 = (bf16[4,2,48,384]{3,2,1,0:T(8,128)(2,1)S(1)}, bf16[4,2,48,384]{3,2,1,0:T(8,128)(2,1)S(1)}, u32[]{:S(2)}, u32[]{:S(2)}) collective-permute-start(bf16[4,2,48,384]{3,2,1,0:T(8,128)(2,1)S(1)} %fusion.2), channel_id=1, source_target_pairs={{0,2},{1,7},{2,0},{3,5},{4,6},{5,3},{6,4},{7,1},{8,10},{9,15},{10,... | collective-permute-start | bytes 884744 | tf_op jit(solution)/shard_map/ppermute | solution.py:45
  85.3 5.3 %collective-permute-start.19 = (bf16[4,48,384]{2,1,0:T(8,128)(2,1)S(1)}, bf16[4,48,384]{2,1,0:T(8,128)(2,1)S(1)}, u32[]{:S(2)}, u32[]{:S(2)}) collective-permute-start(bf16[4,48,384]{2,1,0:T(8,128)(2,1)S(1)} %fusion.5), channel_id=1, source_target_pairs={{0,64},{1,193},{2,66},{3,195},{4,68},{5,197},{6,70},{7,199},{8,72}... | collective-permute-start | bytes 442376 | tf_op jit(solution)/shard_map/ppermute | solution.py:45
  92.3 9.1 %collective-permute-start.21 = (bf16[3,48,384]{2,1,0:T(8,128)(2,1)S(1)}, bf16[3,48,384]{2,1,0:T(8,128)(2,1)S(1)}, u32[]{:S(2)}, u32[]{:S(2)}) collective-permute-start(bf16[3,48,384]{2,1,0:T(8,128)(2,1)S(1)} %pad_maximum_fusion.7), channel_id=1, source_target_pairs={{0,48},{1,41},{2,50},{3,43},{4,52},{5,45},{6,54},{7,47},{8,56},{9,... | collective-permute-start | bytes 331784 | tf_op jit(solution)/shard_map/ppermute | solution.py:45
  96.5 8.5 %collective-permute-start.22 = (bf16[3,48,384]{2,1,0:T(8,128)(2,1)S(1)}, bf16[3,48,384]{2,1,0:T(8,128)(2,1)S(1)}, u32[]{:S(2)}, u32[]{:S(2)}) collective-permute-start(bf16[3,48,384]{2,1,0:T(8,128)(2,1)S(1)} %pad_maximum_fusion.8), channel_id=1, source_target_pairs={{0,32},{1,25},{2,34},{3,27},{4,36},{5,29},{6,38},{7,31},{8,40},{9,... | collective-permute-start | bytes 331784 | tf_op jit(solution)/shard_map/ppermute | solution.py:45
  96.7 8.4 %collective-permute-start.23 = (bf16[3,48,384]{2,1,0:T(8,128)(2,1)S(1)}, bf16[3,48,384]{2,1,0:T(8,128)(2,1)S(1)}, u32[]{:S(2)}, u32[]{:S(2)}) collective-permute-start(bf16[3,48,384]{2,1,0:T(8,128)(2,1)S(1)} %pad_maximum_fusion.9), channel_id=1, source_target_pairs={{0,16},{1,9},{2,18},{3,11},{4,20},{5,13},{6,22},{7,15},{8,24},{9,1... | collective-permute-start | bytes 331784 | tf_op jit(solution)/shard_map/ppermute | solution.py:45
  99.4 6.0 %collective-permute-start.20 = (bf16[3,48,384]{2,1,0:T(8,128)(2,1)S(1)}, bf16[3,48,384]{2,1,0:T(8,128)(2,1)S(1)}, u32[]{:S(2)}, u32[]{:S(2)}) collective-permute-start(bf16[3,48,384]{2,1,0:T(8,128)(2,1)S(1)} %pad_maximum_fusion.6), channel_id=1, source_target_pairs={{0,0},{1,57},{2,2},{3,59},{4,4},{5,61},{6,6},{7,63},{8,8},{9,1},{1... | collective-permute-start | bytes 331784 | tf_op jit(solution)/shard_map/ppermute | solution.py:45
  105.5 6.7 %collective-permute-start.24 = (bf16[4,3,24,384]{3,2,1,0:T(8,128)(2,1)S(1)}, bf16[4,3,24,384]{3,2,1,0:T(8,128)(2,1)S(1)}, u32[]{:S(2)}, u32[]{:S(2)}) collective-permute-start(bf16[4,3,24,384]{3,2,1,0:T(8,128)(2,1)S(1)} %get-tuple-element.57), channel_id=1, source_target_pairs={{0,1},{1,0},{2,3},{3,2},{4,5},{5,4},{6,7},{7,6},{8,9},{9,8},{10,11... | collective-permute-start | bytes 663560 | tf_op jit(solution)/shard_map/ppermute | solution.py:45
  (3 other events, 28.3 us)
